TPU v7x, 512 devices: a whole 4x4x16 slice. The times are simulated.
512 devices in a mesh: tm: 16 (over z_lo, x), space: 32 (over z_hi, y, core).
Axes of the slice: x: 4, y: 4, z: 16 (z_hi: 4, z_lo: 4; z = z_hi * 4 + z_lo), core: 2. Of those that a mesh axis runs over, the one named last changes fastest.
Arguments:
- start_state: float32 [16, 3, 16, 512, 128], P('tm', None, None, 'space'), may hold values from -6 to 6
- land_mask: int32 [512, 128], P('space'), may hold values 0 or 1
- fold_map: int32 [128], replicated, may hold values from 0 to 127, as said below
- coupling: float32 [16, 16], replicated, may hold values from -1 to 1, as said below
- depths: float32 [16], replicated, may hold values from 0.2 to 0.5
Outputs:
- next_state: float32 [16, 3, 16, 512, 128], P('tm', None, None, 'space')
Inputs may be any that keep to these rules, and one draw needn't show every extreme that they name: fold_map[i] = (q - i) mod 128 for one q with q % 4 == 3. `coupling`: symmetric; every diagonal entry exceeds the sum of the magnitudes of the other entries of its row.
All inputs are finite; a program needn't handle non-finite values. No bound on the sum of `land_mask` on one device may be relied on, other than what follows from the above.
Results may differ from a plain program's by a relative error of at most 0.0002.
Values sent between devices are 32-bit elements; how exact they have to be, the bound alone decides.
No kernel may reach another device: no remote copies, remote signals or barrier semaphores. Data moves between devices by JAX's collectives and lax.ppermute only.
A program may use at most 64 MiB of HBM per device.

v0:
```python
import jax
import jax.numpy as jnp
from jax import lax
from jax.sharding import PartitionSpec as P

FINE_STEPS = 8
COARSE_STEPS = 2


FRICTION = 0.02


def with_halo(block, sides, width):
    for axis, dim in sides:
        count = lax.axis_size(axis)
        forward = [(i, i + 1) for i in range(count - 1)]
        backward = [(target, source) for source, target in forward]
        low = lax.ppermute(
            lax.slice_in_dim(block, block.shape[dim] - width, None, axis=dim), axis, forward
        )
        high = lax.ppermute(lax.slice_in_dim(block, 0, width, axis=dim), axis, backward)
        block = jnp.concatenate([low, block, high], axis=dim)
    return block


def passed_along(block, axis, distance):
    devices = range(lax.axis_size(axis))
    route = [(i - distance, i) for i in devices if i - distance in devices]
    return lax.ppermute(block, axis, route)


def coriolis_rows(offset, count, extent):
    positions = (jnp.arange(count, dtype=jnp.int32) + offset).astype(jnp.float32)
    latitude = (positions + 0.5) / extent
    latitude = jnp.where(latitude > 1.0, 2.0 - latitude, latitude)
    return 0.3 * (latitude - 0.5)


def advance(extended, mask_rows, coriolis, coupling, depths, step_size):
    thickness, eastward, northward = (extended[0], extended[1], extended[2])
    pressure = jnp.einsum("lm,mrc->lrc", coupling, thickness, precision=lax.Precision.HIGHEST)
    gradient_east = jnp.roll(pressure, -1, axis=-1) - jnp.roll(pressure, 1, axis=-1)
    gradient_north = pressure[:, 2:] - pressure[:, :-2]
    wet_rows = mask_rows[1:-1]
    coriolis_mid = coriolis[1:-1, None]
    eastward_old = eastward[:, 1:-1]
    northward_old = northward[:, 1:-1]
    eastward_new = wet_rows * (
        eastward_old
        + step_size * (coriolis_mid * northward_old - FRICTION * eastward_old)
        - 0.5 * gradient_east[:, 1:-1]
    )
    northward_new = wet_rows * (
        northward_old
        - step_size * (coriolis_mid * eastward_new + FRICTION * northward_old)
        - 0.5 * gradient_north
    )
    spreading = (
        (jnp.roll(eastward_new, -1, axis=-1) - jnp.roll(eastward_new, 1, axis=-1))[:, 1:-1]
        + northward_new[:, 2:]
        - northward_new[:, :-2]
    )
    thickness_new = mask_rows[2:-2] * (thickness[:, 2:-2] - 0.5 * depths[:, None, None] * spreading)
    return jnp.stack([thickness_new, eastward_new[:, 1:-1], northward_new[:, 1:-1]])


def fold_top(extended, interior, rim_width, fold_map, parity, on_top):
    length = interior.shape[-2]
    facing = interior[..., length - rim_width :, :][..., ::-1, :]
    folded = jnp.take(facing, fold_map, axis=-1) * parity
    cut_point = extended.shape[-2] - rim_width
    kept_rows = extended[..., :cut_point, :]
    return jnp.concatenate(
        [kept_rows, jnp.where(on_top, folded, extended[..., cut_point:, :])], axis=-2
    )


def restrict(values):
    layout = values.shape
    blocks = values.reshape(layout[:-2] + (layout[-2] // 4, 4, layout[-1] // 4, 4))
    return jnp.mean(blocks, axis=(-3, -1))


def prolong(values):
    return jnp.repeat(jnp.repeat(values, 4, axis=-2), 4, axis=-1)


def body(start_state, land_mask, fold_map, coupling, depths):
    initial = start_state[0]
    tile_rows = initial.shape[2]
    parity = jnp.array([1.0, -1.0, -1.0], jnp.float32).reshape(3, 1, 1, 1)
    position = lax.axis_index("space")
    on_top = position == lax.axis_size("space") - 1
    extent = float(tile_rows * lax.axis_size("space"))
    margin = 8 * COARSE_STEPS
    wet = land_mask.astype(jnp.float32)
    wet_extended = with_halo(wet, (("space", 0),), margin)
    wet_extended = fold_top(wet_extended, wet, margin, fold_map, 1.0, on_top)
    fine_coriolis = coriolis_rows(position * tile_rows - margin, tile_rows + 2 * margin, extent)
    inner_two = slice(margin - 2, margin + tile_rows + 2)
    fine_field = initial
    for substep in range(FINE_STEPS):
        extended = with_halo(fine_field, (("space", 2),), 2)
        extended = fold_top(extended, fine_field, 2, fold_map, parity, on_top)
        fine_field = advance(
            extended, wet_extended[inner_two], fine_coriolis[inner_two], coupling, depths, 1.0
        )
    coarse_tile = tile_rows // 4
    coarse_width = 2 * COARSE_STEPS
    coarse_fold = fold_map[0::4] // 4
    coarse_mask = restrict(wet_extended)
    coarse_coriolis = coriolis_rows(
        position * coarse_tile - coarse_width, coarse_tile + 2 * coarse_width, extent / 4.0
    )
    mask_length = coarse_mask.shape[0]

    def coarse_run(coarse_state):
        extended = with_halo(coarse_state, (("space", 2),), coarse_width)
        extended = fold_top(extended, coarse_state, coarse_width, coarse_fold, parity, on_top)
        for substep in range(COARSE_STEPS):
            extended = advance(
                extended,
                coarse_mask[2 * substep : mask_length - 2 * substep],
                coarse_coriolis[2 * substep : mask_length - 2 * substep],
                coupling,
                depths,
                4.0,
            )
        return extended

    coarse_start = restrict(initial)
    fine_coarse = restrict(fine_field)
    discrepancy = fine_coarse - coarse_run(coarse_start)
    slice_index = lax.axis_index("tm")

    def handoff_turn(counter, carried):
        incoming = passed_along(coarse_run(carried) + discrepancy, "tm", 1)
        return jnp.where(slice_index == 0, carried, incoming)

    current = lax.fori_loop(0, lax.axis_size("tm") - 1, handoff_turn, coarse_start)
    advanced = coarse_run(current) + discrepancy
    result = fine_field + prolong(advanced - fine_coarse)
    return result[None]


def solution(mesh):
    return jax.shard_map(
        body,
        mesh=mesh,
        in_specs=(P("tm", None, None, "space", None), P("space", None), P(), P(), P()),
        out_specs=P("tm", None, None, "space", None),
        check_vma=False,
    )
```

profile of v0, /device:TPU:416, one launch (start us, length us, event | category | flops | bytes accessed | tf_op | source)
XLA Modules:
  0.0 584.6 jit_solution(10807567174059218144)
XLA Ops:
  0.7 7.3 %collective-permute-start.6 = (f32[16,128]{1,0:T(8,128)S(1)}, f32[16,128]{1,0:T(8,128)}, u32[]{:S(2)}, u32[]{:S(2)}) collective-permute-start(f32[16,128]{1,0:T(8,128)S(1)} %convert_element_type.9), channel_id=1, source_target_pairs={{1,0},{2,1},{3,2},{4,3},{5,4},{6,5},{7,6},{8,7},{9,8},{10,9},{11,1... | collective-permute-start | bytes 24584 | tf_op jit(solution)/shard_map/ppermute | solution.py:21
  18.5 9.7 %collective-permute-start.22 = (f32[3,16,4,32]{3,1,2,0:T(8,128)S(1)}, f32[3,16,4,32]{3,1,2,0:T(8,128)S(1)}, u32[]{:S(2)}, u32[]{:S(2)}) collective-permute-start(f32[3,16,4,32]{3,1,2,0:T(8,128)S(1)} %get-tuple-element.512), channel_id=1, source_target_pairs={{1,0},{2,1},{3,2},{4,3},{5,4},{6,5},{7,6},{8,7},{9,8},{10,9},{11,1... | collective-permute-start | bytes 73736 | tf_op jit(solution)/shard_map/ppermute | solution.py:21
  38.5 9.6 %collective-permute-start.4 = (f32[3,16,2,128]{3,1,2,0:T(8,128)}, f32[3,16,2,128]{3,1,2,0:T(8,128)S(1)}, u32[]{:S(2)}, u32[]{:S(2)}) collective-permute-start(f32[3,16,2,128]{3,1,2,0:T(8,128)} %get-tuple-element.268), channel_id=1, source_target_pairs={{1,0},{2,1},{3,2},{4,3},{5,4},{6,5},{7,6},{8,7},{9,8},{10,9},{11,1... | collective-permute-start | bytes 147464 | tf_op jit(solution)/shard_map/ppermute | solution.py:21
  53.5 8.4 %collective-permute-start.8 = (f32[3,16,2,128]{3,1,2,0:T(8,128)S(1)}, f32[3,16,2,128]{3,1,2,0:T(8,128)S(1)}, u32[]{:S(2)}, u32[]{:S(2)}) collective-permute-start(f32[3,16,2,128]{3,1,2,0:T(8,128)S(1)} %get-tuple-element.266), channel_id=1, source_target_pairs={{1,0},{2,1},{3,2},{4,3},{5,4},{6,5},{7,6},{8,7},{9,8},{10,9},{11,1... | collective-permute-start | bytes 147464 | tf_op jit(solution)/shard_map/ppermute | solution.py:21
  65.7 9.3 %collective-permute-done.7 = f32[3,16,2,128]{3,1,2,0:T(8,128)S(1)} collective-permute-done((f32[3,16,2,128]{3,1,2,0:T(8,128)S(1)}, f32[3,16,2,128]{3,1,2,0:T(8,128)S(1)}, u32[]{:S(2)}, u32[]{:S(2)}) %collective-permute-start.7) | collective-permute-done | bytes 49184 | tf_op jit(solution)/shard_map/ppermute | solution.py:18
  82.3 7.6 %collective-permute-done.9 = f32[3,16,2,128]{3,1,2,0:T(8,128)S(1)} collective-permute-done((f32[3,16,2,128]{3,1,2,0:T(8,128)S(1)}, f32[3,16,2,128]{3,1,2,0:T(8,128)S(1)}, u32[]{:S(2)}, u32[]{:S(2)}) %collective-permute-start.9) | collective-permute-done | bytes 49184 | tf_op jit(solution)/shard_map/ppermute | solution.py:18
  97.1 7.4 %collective-permute-done.11 = f32[3,16,2,128]{3,1,2,0:T(8,128)S(1)} collective-permute-done((f32[3,16,2,128]{3,1,2,0:T(8,128)S(1)}, f32[3,16,2,128]{3,1,2,0:T(8,128)S(1)}, u32[]{:S(2)}, u32[]{:S(2)}) %collective-permute-start.11) | collective-permute-done | bytes 49184 | tf_op jit(solution)/shard_map/ppermute | solution.py:18
  112.0 7.2 %collective-permute-done.13 = f32[3,16,2,128]{3,1,2,0:T(8,128)S(1)} collective-permute-done((f32[3,16,2,128]{3,1,2,0:T(8,128)S(1)}, f32[3,16,2,128]{3,1,2,0:T(8,128)S(1)}, u32[]{:S(2)}, u32[]{:S(2)}) %collective-permute-start.13) | collective-permute-done | bytes 49184 | tf_op jit(solution)/shard_map/ppermute | solution.py:18
  126.4 7.5 %collective-permute-done.15 = f32[3,16,2,128]{3,1,2,0:T(8,128)S(1)} collective-permute-done((f32[3,16,2,128]{3,1,2,0:T(8,128)S(1)}, f32[3,16,2,128]{3,1,2,0:T(8,128)S(1)}, u32[]{:S(2)}, u32[]{:S(2)}) %collective-permute-start.15) | collective-permute-done | bytes 49184 | tf_op jit(solution)/shard_map/ppermute | solution.py:18
  141.1 7.4 %collective-permute-done.17 = f32[3,16,2,128]{3,1,2,0:T(8,128)S(1)} collective-permute-done((f32[3,16,2,128]{3,1,2,0:T(8,128)S(1)}, f32[3,16,2,128]{3,1,2,0:T(8,128)S(1)}, u32[]{:S(2)}, u32[]{:S(2)}) %collective-permute-start.17) | collective-permute-done | bytes 49184 | tf_op jit(solution)/shard_map/ppermute | solution.py:18
  156.3 7.4 %collective-permute-done.19 = f32[3,16,2,128]{3,1,2,0:T(8,128)S(1)} collective-permute-done((f32[3,16,2,128]{3,1,2,0:T(8,128)S(1)}, f32[3,16,2,128]{3,1,2,0:T(8,128)S(1)}, u32[]{:S(2)}, u32[]{:S(2)}) %collective-permute-start.19) | collective-permute-done | bytes 49184 | tf_op jit(solution)/shard_map/ppermute | solution.py:18
  168.7 392.4 %while.13 = (s32[]{:T(128)}, f32[3,16,4,32]{3,1,2,0:T(8,128)S(1)}, pred[]{:T(512)}, f32[12,32]{1,0:T(8,128)S(1)}, pred[]{:T(512)}, /*index=5*/s32[32]{0:T(128)},...) while((s32[]{:T(128)}, f32[3,16,4,32]{3,1,2,0:T(8,128)S(1)}, ...), condition=%wide.region_4.7_spmd.clone, body=%wide.region_3.6_spmd.clone.sunk | while | flops 2260274 | bytes 1958779 | solution.py:140
  214.4 6.7 %collective-permute-done.2 = f32[3,16,4,32]{3,1,2,0:T(8,128)S(1)} collective-permute-done((f32[3,16,4,32]{3,1,2,0:T(8,128)S(1)}, f32[3,16,4,32]{3,1,2,0:T(8,128)S(1)}, u32[]{:S(2)}, u32[]{:S(2)}) %collective-permute-start.2) | collective-permute-done | bytes 24608 | tf_op jit(solution)/shard_map/while/body/eval_jaxpr/ppermute | solution.py:29
  240.5 6.7 %collective-permute-done.2 = f32[3,16,4,32]{3,1,2,0:T(8,128)S(1)} collective-permute-done((f32[3,16,4,32]{3,1,2,0:T(8,128)S(1)}, f32[3,16,4,32]{3,1,2,0:T(8,128)S(1)}, u32[]{:S(2)}, u32[]{:S(2)}) %collective-permute-start.2) | collective-permute-done | bytes 24608 | tf_op jit(solution)/shard_map/while/body/eval_jaxpr/ppermute | solution.py:29
  266.6 6.7 %collective-permute-done.2 = f32[3,16,4,32]{3,1,2,0:T(8,128)S(1)} collective-permute-done((f32[3,16,4,32]{3,1,2,0:T(8,128)S(1)}, f32[3,16,4,32]{3,1,2,0:T(8,128)S(1)}, u32[]{:S(2)}, u32[]{:S(2)}) %collective-permute-start.2) | collective-permute-done | bytes 24608 | tf_op jit(solution)/shard_map/while/body/eval_jaxpr/ppermute | solution.py:29
  292.8 6.7 %collective-permute-done.2 = f32[3,16,4,32]{3,1,2,0:T(8,128)S(1)} collective-permute-done((f32[3,16,4,32]{3,1,2,0:T(8,128)S(1)}, f32[3,16,4,32]{3,1,2,0:T(8,128)S(1)}, u32[]{:S(2)}, u32[]{:S(2)}) %collective-permute-start.2) | collective-permute-done | bytes 24608 | tf_op jit(solution)/shard_map/while/body/eval_jaxpr/ppermute | solution.py:29
  318.9 6.7 %collective-permute-done.2 = f32[3,16,4,32]{3,1,2,0:T(8,128)S(1)} collective-permute-done((f32[3,16,4,32]{3,1,2,0:T(8,128)S(1)}, f32[3,16,4,32]{3,1,2,0:T(8,128)S(1)}, u32[]{:S(2)}, u32[]{:S(2)}) %collective-permute-start.2) | collective-permute-done | bytes 24608 | tf_op jit(solution)/shard_map/while/body/eval_jaxpr/ppermute | solution.py:29
  345.1 6.7 %collective-permute-done.2 = f32[3,16,4,32]{3,1,2,0:T(8,128)S(1)} collective-permute-done((f32[3,16,4,32]{3,1,2,0:T(8,128)S(1)}, f32[3,16,4,32]{3,1,2,0:T(8,128)S(1)}, u32[]{:S(2)}, u32[]{:S(2)}) %collective-permute-start.2) | collective-permute-done | bytes 24608 | tf_op jit(solution)/shard_map/while/body/eval_jaxpr/ppermute | solution.py:29
  371.3 6.7 %collective-permute-done.2 = f32[3,16,4,32]{3,1,2,0:T(8,128)S(1)} collective-permute-done((f32[3,16,4,32]{3,1,2,0:T(8,128)S(1)}, f32[3,16,4,32]{3,1,2,0:T(8,128)S(1)}, u32[]{:S(2)}, u32[]{:S(2)}) %collective-permute-start.2) | collective-permute-done | bytes 24608 | tf_op jit(solution)/shard_map/while/body/eval_jaxpr/ppermute | solution.py:29
  397.4 6.7 %collective-permute-done.2 = f32[3,16,4,32]{3,1,2,0:T(8,128)S(1)} collective-permute-done((f32[3,16,4,32]{3,1,2,0:T(8,128)S(1)}, f32[3,16,4,32]{3,1,2,0:T(8,128)S(1)}, u32[]{:S(2)}, u32[]{:S(2)}) %collective-permute-start.2) | collective-permute-done | bytes 24608 | tf_op jit(solution)/shard_map/while/body/eval_jaxpr/ppermute | solution.py:29
  423.6 6.7 %collective-permute-done.2 = f32[3,16,4,32]{3,1,2,0:T(8,128)S(1)} collective-permute-done((f32[3,16,4,32]{3,1,2,0:T(8,128)S(1)}, f32[3,16,4,32]{3,1,2,0:T(8,128)S(1)}, u32[]{:S(2)}, u32[]{:S(2)}) %collective-permute-start.2) | collective-permute-done | bytes 24608 | tf_op jit(solution)/shard_map/while/body/eval_jaxpr/ppermute | solution.py:29
  449.7 6.7 %collective-permute-done.2 = f32[3,16,4,32]{3,1,2,0:T(8,128)S(1)} collective-permute-done((f32[3,16,4,32]{3,1,2,0:T(8,128)S(1)}, f32[3,16,4,32]{3,1,2,0:T(8,128)S(1)}, u32[]{:S(2)}, u32[]{:S(2)}) %collective-permute-start.2) | collective-permute-done | bytes 24608 | tf_op jit(solution)/shard_map/while/body/eval_jaxpr/ppermute | solution.py:29
  475.9 6.7 %collective-permute-done.2 = f32[3,16,4,32]{3,1,2,0:T(8,128)S(1)} collective-permute-done((f32[3,16,4,32]{3,1,2,0:T(8,128)S(1)}, f32[3,16,4,32]{3,1,2,0:T(8,128)S(1)}, u32[]{:S(2)}, u32[]{:S(2)}) %collective-permute-start.2) | collective-permute-done | bytes 24608 | tf_op jit(solution)/shard_map/while/body/eval_jaxpr/ppermute | solution.py:29
  567.3 9.6 %collective-permute-done.23 = f32[3,16,4,32]{3,1,2,0:T(8,128)S(1)} collective-permute-done((f32[3,16,4,32]{3,1,2,0:T(8,128)S(1)}, f32[3,16,4,32]{3,1,2,0:T(8,128)S(1)}, u32[]{:S(2)}, u32[]{:S(2)}) %collective-permute-start.23) | collective-permute-done | bytes 24608 | tf_op jit(solution)/shard_map/ppermute | solution.py:18
  (875 shorter events, 408.2 us)
Async XLA Ops:
  0.7 37.0 %collective-permute-start.6 = (f32[16,128]{1,0:T(8,128)S(1)}, f32[16,128]{1,0:T(8,128)}, u32[]{:S(2)}, u32[]{:S(2)}) collective-permute-start(f32[16,128]{1,0:T(8,128)S(1)} %convert_element_type.9), channel_id=1, source_target_pairs={{1,0},{2,1},{3,2},{4,3},{5,4},{6,5},{7,6},{8,7},{9,8},{10,9},{11,1... | collective-permute-start | bytes 24584 | tf_op jit(solution)/shard_map/ppermute | solution.py:21
  8.0 40.1 %collective-permute-start.5 = (f32[16,128]{1,0:T(8,128)S(1)}, f32[16,128]{1,0:T(8,128)}, u32[]{:S(2)}, u32[]{:S(2)}) collective-permute-start(f32[16,128]{1,0:T(8,128)S(1)} %convert_element_type.9), channel_id=1, source_target_pairs={{0,1},{1,2},{2,3},{3,4},{4,5},{5,6},{6,7},{7,8},{8,9},{9,10},{10,1... | collective-permute-start | bytes 24584 | tf_op jit(solution)/shard_map/ppermute | solution.py:18
  11.7 39.8 %collective-permute-start.3 = (f32[3,16,2,128]{3,1,2,0:T(8,128)}, f32[3,16,2,128]{3,1,2,0:T(8,128)}, u32[]{:S(2)}, u32[]{:S(2)}) collective-permute-start(f32[3,16,2,128]{3,1,2,0:T(8,128)} %get-tuple-element.267), channel_id=1, source_target_pairs={{0,1},{1,2},{2,3},{3,4},{4,5},{5,6},{6,7},{7,8},{8,9},{9,10},{10,1... | collective-permute-start | bytes 147464 | tf_op jit(solution)/shard_map/ppermute | solution.py:18
  18.5 31.4 %collective-permute-start.22 = (f32[3,16,4,32]{3,1,2,0:T(8,128)S(1)}, f32[3,16,4,32]{3,1,2,0:T(8,128)S(1)}, u32[]{:S(2)}, u32[]{:S(2)}) collective-permute-start(f32[3,16,4,32]{3,1,2,0:T(8,128)S(1)} %get-tuple-element.512), channel_id=1, source_target_pairs={{1,0},{2,1},{3,2},{4,3},{5,4},{6,5},{7,6},{8,7},{9,8},{10,9},{11,1... | collective-permute-start | bytes 73736 | tf_op jit(solution)/shard_map/ppermute | solution.py:21
  35.8 14.7 %collective-permute-start.21 = (f32[3,16,4,32]{3,1,2,0:T(8,128)S(1)}, f32[3,16,4,32]{3,1,2,0:T(8,128)S(1)}, u32[]{:S(2)}, u32[]{:S(2)}) collective-permute-start(f32[3,16,4,32]{3,1,2,0:T(8,128)S(1)} %get-tuple-element.512), channel_id=1, source_target_pairs={{0,1},{1,2},{2,3},{3,4},{4,5},{5,6},{6,7},{7,8},{8,9},{9,10},{10,1... | collective-permute-start | bytes 73736 | tf_op jit(solution)/shard_map/ppermute | solution.py:18
  38.5 13.0 %collective-permute-start.4 = (f32[3,16,2,128]{3,1,2,0:T(8,128)}, f32[3,16,2,128]{3,1,2,0:T(8,128)S(1)}, u32[]{:S(2)}, u32[]{:S(2)}) collective-permute-start(f32[3,16,2,128]{3,1,2,0:T(8,128)} %get-tuple-element.268), channel_id=1, source_target_pairs={{1,0},{2,1},{3,2},{4,3},{5,4},{6,5},{7,6},{8,7},{9,8},{10,9},{11,1... | collective-permute-start | bytes 147464 | tf_op jit(solution)/shard_map/ppermute | solution.py:21
  53.5 12.1 %collective-permute-start.8 = (f32[3,16,2,128]{3,1,2,0:T(8,128)S(1)}, f32[3,16,2,128]{3,1,2,0:T(8,128)S(1)}, u32[]{:S(2)}, u32[]{:S(2)}) collective-permute-start(f32[3,16,2,128]{3,1,2,0:T(8,128)S(1)} %get-tuple-element.266), channel_id=1, source_target_pairs={{1,0},{2,1},{3,2},{4,3},{5,4},{6,5},{7,6},{8,7},{9,8},{10,9},{11,1... | collective-permute-start | bytes 147464 | tf_op jit(solution)/shard_map/ppermute | solution.py:21
  62.1 12.9 %collective-permute-start.7 = (f32[3,16,2,128]{3,1,2,0:T(8,128)S(1)}, f32[3,16,2,128]{3,1,2,0:T(8,128)S(1)}, u32[]{:S(2)}, u32[]{:S(2)}) collective-permute-start(f32[3,16,2,128]{3,1,2,0:T(8,128)S(1)} %get-tuple-element.265), channel_id=1, source_target_pairs={{0,1},{1,2},{2,3},{3,4},{4,5},{5,6},{6,7},{7,8},{8,9},{9,10},{10,1... | collective-permute-start | bytes 147464 | tf_op jit(solution)/shard_map/ppermute | solution.py:18
  170.6 13.8 %collective-permute-start.1 = (f32[3,16,4,32]{3,1,2,0:T(8,128)S(1)}, f32[3,16,4,32]{3,1,2,0:T(8,128)S(1)}, u32[]{:S(2)}, u32[]{:S(2)}) collective-permute-start(f32[3,16,4,32]{3,1,2,0:T(8,128)S(1)} %get-tuple-element.524), channel_id=1, source_target_pairs={{0,1},{1,2},{2,3},{3,4},{4,5},{5,6},{6,7},{7,8},{8,9},{9,10},{10,1... | collective-permute-start | bytes 73736 | tf_op jit(solution)/shard_map/while/body/eval_jaxpr/ppermute | solution.py:18
  196.8 14.0 %collective-permute-start.1 = (f32[3,16,4,32]{3,1,2,0:T(8,128)S(1)}, f32[3,16,4,32]{3,1,2,0:T(8,128)S(1)}, u32[]{:S(2)}, u32[]{:S(2)}) collective-permute-start(f32[3,16,4,32]{3,1,2,0:T(8,128)S(1)} %get-tuple-element.524), channel_id=1, source_target_pairs={{0,1},{1,2},{2,3},{3,4},{4,5},{5,6},{6,7},{7,8},{8,9},{9,10},{10,1... | collective-permute-start | bytes 73736 | tf_op jit(solution)/shard_map/while/body/eval_jaxpr/ppermute | solution.py:18
  223.0 13.8 %collective-permute-start.1 = (f32[3,16,4,32]{3,1,2,0:T(8,128)S(1)}, f32[3,16,4,32]{3,1,2,0:T(8,128)S(1)}, u32[]{:S(2)}, u32[]{:S(2)}) collective-permute-start(f32[3,16,4,32]{3,1,2,0:T(8,128)S(1)} %get-tuple-element.524), channel_id=1, source_target_pairs={{0,1},{1,2},{2,3},{3,4},{4,5},{5,6},{6,7},{7,8},{8,9},{9,10},{10,1... | collective-permute-start | bytes 73736 | tf_op jit(solution)/shard_map/while/body/eval_jaxpr/ppermute | solution.py:18
  249.2 13.8 %collective-permute-start.1 = (f32[3,16,4,32]{3,1,2,0:T(8,128)S(1)}, f32[3,16,4,32]{3,1,2,0:T(8,128)S(1)}, u32[]{:S(2)}, u32[]{:S(2)}) collective-permute-start(f32[3,16,4,32]{3,1,2,0:T(8,128)S(1)} %get-tuple-element.524), channel_id=1, source_target_pairs={{0,1},{1,2},{2,3},{3,4},{4,5},{5,6},{6,7},{7,8},{8,9},{9,10},{10,1... | collective-permute-start | bytes 73736 | tf_op jit(solution)/shard_map/while/body/eval_jaxpr/ppermute | solution.py:18
  275.4 13.8 %collective-permute-start.1 = (f32[3,16,4,32]{3,1,2,0:T(8,128)S(1)}, f32[3,16,4,32]{3,1,2,0:T(8,128)S(1)}, u32[]{:S(2)}, u32[]{:S(2)}) collective-permute-start(f32[3,16,4,32]{3,1,2,0:T(8,128)S(1)} %get-tuple-element.524), channel_id=1, source_target_pairs={{0,1},{1,2},{2,3},{3,4},{4,5},{5,6},{6,7},{7,8},{8,9},{9,10},{10,1... | collective-permute-start | bytes 73736 | tf_op jit(solution)/shard_map/while/body/eval_jaxpr/ppermute | solution.py:18
  301.5 13.8 %collective-permute-start.1 = (f32[3,16,4,32]{3,1,2,0:T(8,128)S(1)}, f32[3,16,4,32]{3,1,2,0:T(8,128)S(1)}, u32[]{:S(2)}, u32[]{:S(2)}) collective-permute-start(f32[3,16,4,32]{3,1,2,0:T(8,128)S(1)} %get-tuple-element.524), channel_id=1, source_target_pairs={{0,1},{1,2},{2,3},{3,4},{4,5},{5,6},{6,7},{7,8},{8,9},{9,10},{10,1... | collective-permute-start | bytes 73736 | tf_op jit(solution)/shard_map/while/body/eval_jaxpr/ppermute | solution.py:18
  327.7 13.8 %collective-permute-start.1 = (f32[3,16,4,32]{3,1,2,0:T(8,128)S(1)}, f32[3,16,4,32]{3,1,2,0:T(8,128)S(1)}, u32[]{:S(2)}, u32[]{:S(2)}) collective-permute-start(f32[3,16,4,32]{3,1,2,0:T(8,128)S(1)} %get-tuple-element.524), channel_id=1, source_target_pairs={{0,1},{1,2},{2,3},{3,4},{4,5},{5,6},{6,7},{7,8},{8,9},{9,10},{10,1... | collective-permute-start | bytes 73736 | tf_op jit(solution)/shard_map/while/body/eval_jaxpr/ppermute | solution.py:18
  353.8 13.8 %collective-permute-start.1 = (f32[3,16,4,32]{3,1,2,0:T(8,128)S(1)}, f32[3,16,4,32]{3,1,2,0:T(8,128)S(1)}, u32[]{:S(2)}, u32[]{:S(2)}) collective-permute-start(f32[3,16,4,32]{3,1,2,0:T(8,128)S(1)} %get-tuple-element.524), channel_id=1, source_target_pairs={{0,1},{1,2},{2,3},{3,4},{4,5},{5,6},{6,7},{7,8},{8,9},{9,10},{10,1... | collective-permute-start | bytes 73736 | tf_op jit(solution)/shard_map/while/body/eval_jaxpr/ppermute | solution.py:18
  380.0 13.8 %collective-permute-start.1 = (f32[3,16,4,32]{3,1,2,0:T(8,128)S(1)}, f32[3,16,4,32]{3,1,2,0:T(8,128)S(1)}, u32[]{:S(2)}, u32[]{:S(2)}) collective-permute-start(f32[3,16,4,32]{3,1,2,0:T(8,128)S(1)} %get-tuple-element.524), channel_id=1, source_target_pairs={{0,1},{1,2},{2,3},{3,4},{4,5},{5,6},{6,7},{7,8},{8,9},{9,10},{10,1... | collective-permute-start | bytes 73736 | tf_op jit(solution)/shard_map/while/body/eval_jaxpr/ppermute | solution.py:18
  406.2 13.8 %collective-permute-start.1 = (f32[3,16,4,32]{3,1,2,0:T(8,128)S(1)}, f32[3,16,4,32]{3,1,2,0:T(8,128)S(1)}, u32[]{:S(2)}, u32[]{:S(2)}) collective-permute-start(f32[3,16,4,32]{3,1,2,0:T(8,128)S(1)} %get-tuple-element.524), channel_id=1, source_target_pairs={{0,1},{1,2},{2,3},{3,4},{4,5},{5,6},{6,7},{7,8},{8,9},{9,10},{10,1... | collective-permute-start | bytes 73736 | tf_op jit(solution)/shard_map/while/body/eval_jaxpr/ppermute | solution.py:18
  432.3 13.8 %collective-permute-start.1 = (f32[3,16,4,32]{3,1,2,0:T(8,128)S(1)}, f32[3,16,4,32]{3,1,2,0:T(8,128)S(1)}, u32[]{:S(2)}, u32[]{:S(2)}) collective-permute-start(f32[3,16,4,32]{3,1,2,0:T(8,128)S(1)} %get-tuple-element.524), channel_id=1, source_target_pairs={{0,1},{1,2},{2,3},{3,4},{4,5},{5,6},{6,7},{7,8},{8,9},{9,10},{10,1... | collective-permute-start | bytes 73736 | tf_op jit(solution)/shard_map/while/body/eval_jaxpr/ppermute | solution.py:18
  458.5 13.8 %collective-permute-start.1 = (f32[3,16,4,32]{3,1,2,0:T(8,128)S(1)}, f32[3,16,4,32]{3,1,2,0:T(8,128)S(1)}, u32[]{:S(2)}, u32[]{:S(2)}) collective-permute-start(f32[3,16,4,32]{3,1,2,0:T(8,128)S(1)} %get-tuple-element.524), channel_id=1, source_target_pairs={{0,1},{1,2},{2,3},{3,4},{4,5},{5,6},{6,7},{7,8},{8,9},{9,10},{10,1... | collective-permute-start | bytes 73736 | tf_op jit(solution)/shard_map/while/body/eval_jaxpr/ppermute | solution.py:18
  484.6 13.8 %collective-permute-start.1 = (f32[3,16,4,32]{3,1,2,0:T(8,128)S(1)}, f32[3,16,4,32]{3,1,2,0:T(8,128)S(1)}, u32[]{:S(2)}, u32[]{:S(2)}) collective-permute-start(f32[3,16,4,32]{3,1,2,0:T(8,128)S(1)} %get-tuple-element.524), channel_id=1, source_target_pairs={{0,1},{1,2},{2,3},{3,4},{4,5},{5,6},{6,7},{7,8},{8,9},{9,10},{10,1... | collective-permute-start | bytes 73736 | tf_op jit(solution)/shard_map/while/body/eval_jaxpr/ppermute | solution.py:18
  510.8 13.8 %collective-permute-start.1 = (f32[3,16,4,32]{3,1,2,0:T(8,128)S(1)}, f32[3,16,4,32]{3,1,2,0:T(8,128)S(1)}, u32[]{:S(2)}, u32[]{:S(2)}) collective-permute-start(f32[3,16,4,32]{3,1,2,0:T(8,128)S(1)} %get-tuple-element.524), channel_id=1, source_target_pairs={{0,1},{1,2},{2,3},{3,4},{4,5},{5,6},{6,7},{7,8},{8,9},{9,10},{10,1... | collective-permute-start | bytes 73736 | tf_op jit(solution)/shard_map/while/body/eval_jaxpr/ppermute | solution.py:18
  537.0 13.8 %collective-permute-start.1 = (f32[3,16,4,32]{3,1,2,0:T(8,128)S(1)}, f32[3,16,4,32]{3,1,2,0:T(8,128)S(1)}, u32[]{:S(2)}, u32[]{:S(2)}) collective-permute-start(f32[3,16,4,32]{3,1,2,0:T(8,128)S(1)} %get-tuple-element.524), channel_id=1, source_target_pairs={{0,1},{1,2},{2,3},{3,4},{4,5},{5,6},{6,7},{7,8},{8,9},{9,10},{10,1... | collective-permute-start | bytes 73736 | tf_op jit(solution)/shard_map/while/body/eval_jaxpr/ppermute | solution.py:18
  563.2 13.8 %collective-permute-start.23 = (f32[3,16,4,32]{3,1,2,0:T(8,128)S(1)}, f32[3,16,4,32]{3,1,2,0:T(8,128)S(1)}, u32[]{:S(2)}, u32[]{:S(2)}) collective-permute-start(f32[3,16,4,32]{3,1,2,0:T(8,128)S(1)} %get-tuple-element.134), channel_id=1, source_target_pairs={{0,1},{1,2},{2,3},{3,4},{4,5},{5,6},{6,7},{7,8},{8,9},{9,10},{10,1... | collective-permute-start | bytes 73736 | tf_op jit(solution)/shard_map/ppermute | solution.py:18
  (70 other events, 1846.9 us)
where the time goes:
time: 588 us; the launch traced here: 585 us
  waiting for transfers between devices  255 us (43%)
  starting transfers between devices  169 us (29%)
  local copies, waits for them, and re-layouts  84.4 us (14%)
  other arithmetic  63.1 us (11%)
  matrix products  9.4 us (2%)
    ppermute x26, waiting for transfers between devices, with_halo(): lax.ppermute(lax.slice_in_dim(block, block.shape[dim] - width, None, axis...  156 us
    ppermute x15, waiting for transfers between devices, passed_along(): return lax.ppermute(block, axis, route)  98.9 us
    ppermute x26, starting transfers between devices, with_halo(): lax.ppermute(lax.slice_in_dim(block, 0, width, axis=dim), axis, backward)  78.4 us
    ppermute x26, starting transfers between devices, with_halo(): lax.ppermute(lax.slice_in_dim(block, block.shape[dim] - width, None, axis...  59.8 us
    ppermute x15, starting transfers between devices, passed_along(): return lax.ppermute(block, axis, route)  30.3 us
    gather x52, local copies, waits for them, and re-layouts, fold_top(): folded = jnp.take(facing, fold_map, axis=-1) * parity  25 us
    slice x33, local copies, waits for them, and re-layouts, advance(): coriolis_mid = coriolis[1:-1, None]  22.5 us
    select_n x26, other arithmetic, fold_top(): jnp.where(on_top, folded, extended[..., cut_point:, :])  12.7 us
  transfers between devices with their start and end apart: 67, of which 40 were waited for; matrix products, arithmetic and copies ran while one was open for 19% of the time, Pallas kernels for 0%

commit v1 on v0

v1 whole, which is shorter than its diff:
```python
import functools

import jax
import jax.numpy as jnp
from jax import lax
from jax.experimental import pallas as pl
from jax.experimental.pallas import tpu as pltpu
from jax.sharding import Mesh
from jax.sharding import PartitionSpec as P

LAYERS = 16
ZONAL = 128
FINE_STEPS = 8
BAND = 16
BANDS = 32
EXTENT = BAND * BANDS
HALO = 2 * FINE_STEPS
SPAN = BAND + 2 * HALO
PAD = 4
FRICTION = 0.02
HIGHEST = lax.Precision.HIGHEST
F32 = jnp.float32
BF16 = jnp.bfloat16

SPACE = ("zh", "y", "c")
TIME = ("zl", "x")
PLANE = ("x", "y", "c")

SWEEPS = 6
SHIFT = 1.0


def iota(shape, axis):
    return lax.broadcasted_iota(jnp.int32, shape, axis)


def block_mean_matrix():
    row = iota((4 * ZONAL, ZONAL), 0)
    col = iota((4 * ZONAL, ZONAL), 1)
    target = (row // ZONAL) * 32 + (row % ZONAL) // 4
    return jnp.where(col == target, 1.0 / 16.0, 0.0).astype(F32)


def restrict_kernel(own, out, sums):
    for f in range(3):
        for cr in range(4):
            total = None
            for r in range(4):
                row = own[pl.ds(f * 256 + 4 * cr + r, LAYERS, stride=BAND), :]
                total = row if total is None else total + row
            sums[f * LAYERS : (f + 1) * LAYERS, cr * ZONAL : (cr + 1) * ZONAL] = total
    out[...] = jnp.dot(sums[...], block_mean_matrix(), precision=HIGHEST, preferred_element_type=F32)


def swap_rows(x, k):
    halves = [x[:8], x[8:]]
    if k & 8:
        halves = halves[::-1]
    done = []
    for y in halves:
        sub = iota(y.shape, 0)
        if k & 4:
            y = pltpu.roll(y, 4, 0)
        if k & 2:
            y = jnp.where((sub & 2) == 0, pltpu.roll(y, 6, 0), pltpu.roll(y, 2, 0))
        if k & 1:
            y = jnp.where((sub & 1) == 0, pltpu.roll(y, 7, 0), pltpu.roll(y, 1, 0))
        done.append(y)
    return jnp.concatenate(done, axis=0)


def modes_kernel(coupling, depths, vectors, values):
    row = iota((LAYERS, ZONAL), 0)
    lane = iota((LAYERS, ZONAL), 1)
    eye = row == lane
    root = jnp.sqrt(depths[...])
    root = jnp.concatenate([root, jnp.zeros((1, ZONAL - LAYERS), F32)], axis=1)
    root_lanes = jnp.broadcast_to(root, (LAYERS, ZONAL))
    root_rows = jnp.sum(jnp.where(eye, root_lanes, 0.0), axis=1, keepdims=True)
    matrix = jnp.concatenate([coupling[...], jnp.zeros((LAYERS, ZONAL - LAYERS), F32)], axis=1)
    matrix = matrix * root_lanes * root_rows
    start = matrix + jnp.where(eye, SHIFT, 0.0) + jnp.where(lane == row + LAYERS, 1.0, 0.0)
    active = lane < LAYERS

    def sweep(_, x):
        size = jnp.sum(jnp.where(active, x * x, 0.0), axis=1, keepdims=True)
        size = jnp.broadcast_to(size, x.shape)
        for k in range(1, LAYERS):
            other = swap_rows(x, k)
            other_size = swap_rows(size, k)
            inner = jnp.sum(jnp.where(active, x * other, 0.0), axis=1, keepdims=True)
            inner = jnp.broadcast_to(inner, x.shape)
            gap = other_size - size
            first = (row & (1 << (k.bit_length() - 1))) == 0
            sign = jnp.where(gap > 0.0, 1.0, jnp.where(gap < 0.0, -1.0, jnp.where(first, 1.0, -1.0)))
            below = jnp.abs(gap) + jnp.sqrt(gap * gap + 4.0 * inner * inner)
            tangent = jnp.where(below > 0.0, 2.0 * inner * sign / jnp.maximum(below, 1e-30), 0.0)
            cosine = lax.rsqrt(1.0 + tangent * tangent)
            x = cosine * (x - tangent * other)
            size = size - tangent * inner
        return x

    x = lax.fori_loop(0, SWEEPS, sweep, start)
    turned = pltpu.roll(x, ZONAL - LAYERS, 1)
    vectors[...] = jnp.where(active, turned, 0.0)
    value = jnp.sum(jnp.where(active, x * turned, 0.0), axis=1, keepdims=True) - SHIFT
    values[...] = jnp.broadcast_to(value, (LAYERS, ZONAL))


def fine_kernel(
    place, own, low, high, mask_own, mask_low, mask_high, fold, coupling, depths, vectors, following,
    fine, chunk, hs, us, vs, ps, ms, fs, sums,
):
    position = place[0]
    on_top = position == BANDS - 1
    fields = (hs, us, vs)

    def put(field, row, value):
        fields[field][row] = value.reshape(2, 8, ZONAL)

    def mask_put(row, value):
        ms[row] = jnp.broadcast_to(value, (8, ZONAL))

    for f in range(3):
        for r in range(BAND):
            here = pl.ds(f * 256 + r, LAYERS, stride=BAND)
            put(f, PAD + r, low[here, :])
            put(f, PAD + HALO + r, own[here, :])
    for r in range(BAND):
        mask_put(PAD + r, mask_low[r : r + 1, :].astype(F32))
        mask_put(PAD + HALO + r, mask_own[r : r + 1, :].astype(F32))

    @pl.when(jnp.logical_not(on_top))
    def _():
        for f in range(3):
            for r in range(BAND):
                put(f, PAD + HALO + BAND + r, high[pl.ds(f * 256 + r, LAYERS, stride=BAND), :])
        for r in range(BAND):
            mask_put(PAD + HALO + BAND + r, mask_high[r : r + 1, :].astype(F32))

    @pl.when(on_top)
    def _():
        index = jnp.broadcast_to(fold[...], (LAYERS, ZONAL))
        for f in range(3):
            for r in range(BAND):
                facing = own[pl.ds(f * 256 + BAND - 1 - r, LAYERS, stride=BAND), :]
                facing = jnp.take_along_axis(facing, index, axis=1)
                put(f, PAD + HALO + BAND + r, facing if f == 0 else -facing)
        for r in range(BAND):
            facing = jnp.broadcast_to(mask_own[BAND - 1 - r : BAND - r, :].astype(F32), (8, ZONAL))
            ms[PAD + HALO + BAND + r] = jnp.take_along_axis(facing, index[:8], axis=1)

    rows = iota((SPAN + 2 * PAD, 8, ZONAL), 0) + (position * BAND - HALO - PAD)
    latitude = (rows.astype(F32) + 0.5) / float(EXTENT)
    latitude = jnp.where(latitude > 1.0, 2.0 - latitude, latitude)
    fs[...] = 0.3 * (latitude - 0.5)

    half = 0.5 * coupling[...]
    half_top = half.astype(BF16)
    half_rest = (half - half_top.astype(F32)).astype(BF16)
    weights = jnp.concatenate([half_top, half_top, half_rest], axis=1)
    lanes = jnp.broadcast_to(depths[...], (LAYERS, LAYERS))
    eye = iota((LAYERS, LAYERS), 0) == iota((LAYERS, LAYERS), 1)
    thick = 0.5 * jnp.sum(jnp.where(eye, lanes, 0.0), axis=1, keepdims=True)
    thick = jnp.broadcast_to(thick, (LAYERS, ZONAL)).reshape(1, 2, 8, ZONAL)
    keep = 1.0 - FRICTION

    def east(x):
        flat = x.reshape(-1, ZONAL)
        return (pltpu.roll(flat, ZONAL - 1, 1) - pltpu.roll(flat, 1, 1)).reshape(x.shape)

    for step in range(FINE_STEPS):
        first, last = PAD + 2 * step, PAD + SPAN - 2 * step
        for j in range(first, last, 4):
            group = [hs[j + i].reshape(LAYERS, ZONAL) for i in range(4)]
            wide = jnp.concatenate(group, axis=1)
            top = wide.astype(BF16)
            rest = (wide - top.astype(F32)).astype(BF16)
            stacked = jnp.concatenate([top, rest, top], axis=0)
            result = jnp.dot(weights, stacked, preferred_element_type=F32)
            for i in range(4):
                ps[j + i] = result[:, i * ZONAL : (i + 1) * ZONAL].reshape(2, 8, ZONAL)
        for j in range(first + 1, last - 1, 2):
            m = ms[j : j + 2][:, None]
            f = fs[j : j + 2][:, None]
            p = ps[j : j + 2]
            u = us[j : j + 2]
            v = vs[j : j + 2]
            u = m * (keep * u + f * v - east(p))
            v = m * (keep * v - f * u - (ps[j + 1 : j + 3] - ps[j - 1 : j + 1]))
            us[j : j + 2] = u
            vs[j : j + 2] = v
        for j in range(first + 2, last - 2, 2):
            m = ms[j : j + 2][:, None]
            spread = east(us[j : j + 2]) + (vs[j + 1 : j + 3] - vs[j - 1 : j + 1])
            hs[j : j + 2] = m * (hs[j : j + 2] - thick * spread)

    begin = PAD + HALO
    for f in range(3):
        for cr in range(4):
            total = None
            for r in range(4):
                row = fields[f][begin + 4 * cr + r].reshape(LAYERS, ZONAL)
                fine[f * BAND + 4 * cr + r] = row
                total = row if total is None else total + row
            sums[f * LAYERS : (f + 1) * LAYERS, cr * ZONAL : (cr + 1) * ZONAL] = total
    for cr in range(4):
        total = None
        for r in range(4):
            row = ms[begin + 4 * cr + r]
            total = row if total is None else total + row
        sums[3 * LAYERS :, cr * ZONAL : (cr + 1) * ZONAL] = total
    mean = jnp.dot(sums[...], block_mean_matrix(), precision=HIGHEST, preferred_element_type=F32)
    jump = mean[: 3 * LAYERS] - following[...]
    root = jnp.sqrt(depths[...])
    for f in range(3):
        basis = vectors[:, :LAYERS] / root if f == 0 else vectors[:, :LAYERS] * root
        in_modes = jnp.dot(
            basis, jump[f * LAYERS : (f + 1) * LAYERS], precision=HIGHEST, preferred_element_type=F32
        )
        chunk[pl.ds(f, LAYERS, stride=8), :] = in_modes
        chunk[pl.ds(4 + f, LAYERS, stride=8), :] = in_modes
    chunk[pl.ds(3, BANDS, stride=4), :] = jnp.broadcast_to(mean[3 * LAYERS : 3 * LAYERS + 1], (BANDS, ZONAL))


def coarse_tools(value, mask, fold):
    row = iota((32, ZONAL), 0)
    lane = iota((32, ZONAL), 1)
    seg = lane // 32
    col = lane % 32
    after = seg * 32 + (col + 1) % 32
    before = seg * 32 + (col + 31) % 32
    position = (seg * 32 + row).astype(F32)
    coriolis = (4.0 * 0.3) * ((position + 0.5) / float(EXTENT // 4) - 0.5)
    keep = 1.0 - 4.0 * FRICTION
    sub = iota((8, ZONAL), 0)
    seg8 = seg[:8]
    k = fold[0, 0] // 4
    fold_index = 96 + (k - iota((8, ZONAL), 1) + 128) % 32

    def gather(x, index):
        return jnp.take_along_axis(x, index, axis=1)

    def east(x):
        return gather(x, after) - gather(x, before)

    def north(x, sign):
        up = pltpu.roll(x, 31, 0)
        down = pltpu.roll(x, 1, 0)
        mirror = sign * gather(x[24:], fold_index)
        edge = jnp.where(seg8 == 3, mirror, pltpu.roll(up[24:], 96, 1))
        up = jnp.concatenate([up[:24], jnp.where(sub == 7, edge, up[24:])], axis=0)
        edge = jnp.where(seg8 == 0, 0.0, pltpu.roll(down[:8], 32, 1))
        down = jnp.concatenate([jnp.where(sub == 0, edge, down[:8]), down[8:]], axis=0)
        return up - down

    def propagate(h, u, v):
        for _ in range(2):
            p = (0.5 * value) * h
            u = mask * (keep * u + coriolis * v - east(p))
            v = mask * (keep * v - coriolis * u - north(p, 1.0))
            h = mask * (h - 0.5 * (east(u) + north(v, -1.0)))
        return h, u, v

    return propagate


def pair_kernel(place, gathered, values, fold, jumps, mask_out, total):
    lane = iota((8, ZONAL), 1)
    seg = lane // 32
    mode = place[1]
    for x in range(2):
        for f in range(4 if x == 0 else 3):
            rows = [None] * 4
            for zh in range(4):
                piece = gathered[pl.ds(zh * 64 + x * 32 + f, 8, stride=4), :]
                for cr in range(4):
                    shift = (32 * (zh - cr)) % ZONAL
                    moved = pltpu.roll(piece, shift, 1) if shift else piece
                    rows[cr] = moved if zh == 0 else jnp.where(seg == zh, moved, rows[cr])
            for cr in range(4):
                if f == 3:
                    mask_out[pl.ds(cr, 8, stride=4), :] = rows[cr]
                else:
                    jumps[pl.ds((x * 3 + f) * 32 + cr, 8, stride=4), :] = rows[cr]
    propagate = coarse_tools(values[pl.ds(mode, 1), :], mask_out[...], fold)
    state = propagate(*(jumps[f * 32 : (f + 1) * 32, :] for f in range(3)))
    for f in range(3):
        result = state[f] + jumps[(3 + f) * 32 : (4 + f) * 32, :]
        for copy in range(8):
            total[(copy * 3 + f) * 32 : (copy * 3 + f + 1) * 32, :] = result


def chain_kernel(place, totals, jumps, mask, values, fold, chunk, held):
    mode = place[1]
    pair = place[2]
    quarter = place[3]
    core = place[4]
    propagate = coarse_tools(values[pl.ds(mode, 1), :], mask[...], fold)

    def turn(index, state):
        state = propagate(*propagate(*state))
        return tuple(
            state[f] + totals[pl.ds(pl.multiple_of((index * 3 + f) * 32, 32), 32), :] for f in range(3)
        )

    zero = jnp.zeros((32, ZONAL), F32)
    state = lax.fori_loop(0, pair, turn, (zero, zero, zero))
    seg = iota((8, ZONAL), 1) // 32
    chunk[...] = jnp.zeros_like(chunk)
    for x in range(2):
        state = propagate(*state)
        for f in range(3):
            held[f * 32 : (f + 1) * 32, :] = state[f]
        for f in range(3):
            packed = None
            for cr in range(4):
                piece = held[pl.ds(f * 32 + cr, 8, stride=4), :]
                piece = pltpu.roll(piece, lax.rem(32 * (cr - quarter) + ZONAL, ZONAL), 1)
                packed = piece if cr == 0 else jnp.where(seg == cr, piece, packed)
            chunk[pl.ds((2 * core + x) * 32 + f, 8, stride=4), :] = packed
        if x == 0:
            state = tuple(state[f] + jumps[f * 32 : (f + 1) * 32, :] for f in range(3))


def correct_kernel(place, fine, gathered, vectors, depths, out):
    half = place[5]
    lanes = jnp.broadcast_to(depths[...], (LAYERS, LAYERS))
    eye = iota((LAYERS, LAYERS), 0) == iota((LAYERS, LAYERS), 1)
    root = jnp.sqrt(jnp.sum(jnp.where(eye, lanes, 0.0), axis=1, keepdims=True))
    lane = iota((LAYERS, ZONAL), 1)
    for f in range(3):
        in_modes = gathered[pl.ds(half * 4 + f, LAYERS, stride=8), :]
        change = lax.dot_general(
            vectors[:, :LAYERS], in_modes, (((0,), (0,)), ((), ())),
            precision=HIGHEST, preferred_element_type=F32,
        )
        change = change * root if f == 0 else change / root
        for cr in range(4):
            spread = jnp.take_along_axis(change, cr * 32 + lane // 4, axis=1)
            for r in range(4):
                row = 4 * cr + r
                out[pl.ds(f * 256 + row, LAYERS, stride=BAND), :] = fine[f * BAND + row] + spread


def call(kernel, out_shapes, scratch=(), scalars=False, flops=1 << 20, vmem=24 << 20):
    def run(*arrays):
        vmem_spec = pl.BlockSpec(memory_space=pltpu.VMEM)
        specs = [vmem_spec] * len(arrays)
        if scalars:
            specs[0] = pl.BlockSpec(memory_space=pltpu.SMEM)
        return pl.pallas_call(
            kernel,
            out_shape=[jax.ShapeDtypeStruct(s, F32) for s in out_shapes],
            in_specs=specs,
            out_specs=[vmem_spec] * len(out_shapes),
            scratch_shapes=list(scratch),
            compiler_params=pltpu.CompilerParams(vmem_limit_bytes=vmem),
            cost_estimate=pl.CostEstimate(flops=flops, bytes_accessed=1 << 20, transcendentals=0),
        )(*arrays)

    return run


def swap(block, axes):
    return lax.all_to_all(block, axes, 0, 0, tiled=True)


def body(start_state, land_mask, fold_map, coupling, depths):
    own = start_state.reshape(3 * LAYERS * BAND, ZONAL)
    fold = fold_map.reshape(1, ZONAL)
    depth_row = depths.reshape(1, LAYERS)
    zl, x, zh, y, c = (lax.axis_index(a) for a in ("zl", "x", "zh", "y", "c"))
    position = zh * 8 + y * 2 + c
    place = jnp.stack([position, x * 4 + y, zl * 2 + c, zh, c, x // 2]).astype(jnp.int32)

    up = [(i, i + 1) for i in range(BANDS - 1)]
    down = [(b, a) for a, b in up]
    low = lax.ppermute(own, SPACE, up)
    high = lax.ppermute(own, SPACE, down)
    mask_low = lax.ppermute(land_mask, SPACE, up)
    mask_high = lax.ppermute(land_mask, SPACE, down)

    (restricted,) = call(
        restrict_kernel, [(48, ZONAL)], [pltpu.VMEM((48, 4 * ZONAL), F32)]
    )(own)
    following = lax.ppermute(restricted, TIME, [(n + 1, n) for n in range(15)])
    vectors, values = call(modes_kernel, [(LAYERS, ZONAL), (LAYERS, ZONAL)], flops=10 << 20)(
        coupling, depth_row
    )

    rows = SPAN + 2 * PAD
    state = pltpu.VMEM((rows, 2, 8, ZONAL), F32)
    table = pltpu.VMEM((rows, 8, ZONAL), F32)
    fine, chunk = call(
        fine_kernel,
        [(3 * BAND, LAYERS, ZONAL), (4 * BANDS, ZONAL)],
        [state, state, state, state, table, table, pltpu.VMEM((56, 4 * ZONAL), F32)],
        scalars=True,
    )(
        place, own, low, high, land_mask, mask_low, mask_high, fold, coupling, depth_row, vectors, following
    )

    spread = swap(chunk, PLANE)
    mine = lax.dynamic_slice_in_dim(spread, c * 64, 64, 0)
    grid = swap(jnp.concatenate([mine] * 4, axis=0), ("zh",))
    jumps, mask, total = call(
        pair_kernel, [(192, ZONAL), (32, ZONAL), (8 * 96, ZONAL)], scalars=True
    )(place, grid, values, fold)
    totals = swap(total, ("zl", "c"))
    (chunk,) = call(
        chain_kernel, [(4 * BANDS, ZONAL)], [pltpu.VMEM((96, ZONAL), F32)], scalars=True
    )(place, totals, jumps, mask, values, fold)
    change = swap(chunk, PLANE)
    (result,) = call(correct_kernel, [(3 * LAYERS * BAND, ZONAL)], scalars=True)(
        place, fine, change, vectors, depth_row
    )
    return result.reshape(1, 3, LAYERS, BAND, ZONAL)


def solution(mesh):
    parts = Mesh(mesh.devices.reshape(4, 4, 4, 4, 2), ("zl", "x", "zh", "y", "c"))
    return jax.shard_map(
        body,
        mesh=parts,
        in_specs=(P(TIME, None, None, SPACE, None), P(SPACE, None), P(), P(), P()),
        out_specs=P(TIME, None, None, SPACE, None),
        check_vma=False,
    )
```

time: 588 us -> 115 us (0.20)
  the two profiles are of different devices: /device:TPU:416 before, /device:TPU:1 now
where the time goes in v1:
time: 115 us; the launch traced here: 114 us
  blocking collectives  58.2 us (51%)
  starting transfers between devices  25.9 us (23%)
  Pallas kernels  20.1 us (17%)
  waiting for transfers between devices  7.38 us (6%)
  local copies, waits for them, and re-layouts  2.4 us (2%)
    all_to_all x3, blocking collectives, swap(): return lax.all_to_all(block, axes, 0, 0, tiled=True)  58.2 us
    pallas_call x6, Pallas kernels, run(): pl.pallas_call(kernel, out_shape=[jax.ShapeDtypeStruct(s, F32) for s in o...  20.1 us
    all_to_all x1, starting transfers between devices, swap(): return lax.all_to_all(block, axes, 0, 0, tiled=True)  9.63 us
    ppermute x1, starting transfers between devices, body(): high = lax.ppermute(own, SPACE, down)  8.77 us
    all_to_all x1, waiting for transfers between devices, swap(): return lax.all_to_all(block, axes, 0, 0, tiled=True)  7.36 us
    ppermute x1, starting transfers between devices, body(): mask_high = lax.ppermute(land_mask, SPACE, down)  2.4 us
    unnamed x12, local copies, waits for them, and re-layouts  2.31 us
  transfers between devices with their start and end apart: 6, of which 1 were waited for; matrix products, arithmetic and copies ran while one was open for 0% of the time, Pallas kernels for 9%

profile of v1, /device:TPU:1, one launch (start us, length us, event | category | flops | bytes accessed | tf_op | source)
XLA Modules:
  0.0 114.3 jit_solution(5036632051855409016)
XLA Ops:
  0.0 8.8 %collective-permute-start.1 = (f32[768,128]{1,0:T(8,128)}, f32[768,128]{1,0:T(8,128)S(1)}, u32[]{:S(2)}, u32[]{:S(2)}) collective-permute-start(f32[768,128]{1,0:T(8,128)} %bitcast.19), channel_id=1, source_target_pairs={{1,0},{2,1},{3,2},{4,3},{5,4},{6,5},{7,6},{8,7},{9,8},{10,9},{11,1... | collective-permute-start | bytes 1179656 | tf_op jit(solution)/shard_map/ppermute | solution.py:380
  8.8 1.9 %collective-permute-start = (f32[768,128]{1,0:T(8,128)}, f32[768,128]{1,0:T(8,128)S(1)}, u32[]{:S(2)}, u32[]{:S(2)}) collective-permute-start(f32[768,128]{1,0:T(8,128)} %bitcast.20), channel_id=1, source_target_pairs={{0,1},{1,2},{2,3},{3,4},{4,5},{5,6},{6,7},{7,8},{8,9},{9,10},{10,1... | collective-permute-start | bytes 1179656 | tf_op jit(solution)/shard_map/ppermute | solution.py:379
  10.7 1.0 copy-done
  11.7 0.4 shard_map.56
  12.1 1.3 %collective-permute-start.4 = (f32[48,128]{1,0:T(8,128)S(1)}, f32[48,128]{1,0:T(8,128)S(1)}, u32[]{:S(2)}, u32[]{:S(2)}) collective-permute-start(f32[48,128]{1,0:T(8,128)S(1)} %shard_map.56), channel_id=1, source_target_pairs={{32,0},{64,32},{96,64},{128,96},{160,128},{192,160},{224,192},{256... | collective-permute-start | bytes 73736 | tf_op jit(solution)/shard_map/ppermute | solution.py:387
  13.4 1.9 %collective-permute-start.2 = (s32[16,128]{1,0:T(8,128)S(1)}, s32[16,128]{1,0:T(8,128)S(1)}, u32[]{:S(2)}, u32[]{:S(2)}) collective-permute-start(s32[16,128]{1,0:T(8,128)S(1)} %copy-done.2), channel_id=1, source_target_pairs={{0,1},{1,2},{2,3},{3,4},{4,5},{5,6},{6,7},{7,8},{8,9},{9,10},{10,1... | collective-permute-start | bytes 24584 | tf_op jit(solution)/shard_map/ppermute | solution.py:381
  15.4 2.4 %collective-permute-start.3 = (s32[16,128]{1,0:T(8,128)S(1)}, s32[16,128]{1,0:T(8,128)S(1)}, u32[]{:S(2)}, u32[]{:S(2)}) collective-permute-start(s32[16,128]{1,0:T(8,128)S(1)} %copy-done.2), channel_id=1, source_target_pairs={{1,0},{2,1},{3,2},{4,3},{5,4},{6,5},{7,6},{8,7},{9,8},{10,9},{11,1... | collective-permute-start | bytes 24584 | tf_op jit(solution)/shard_map/ppermute | solution.py:382
  17.8 0.0 copy-start.3
  17.8 0.1 stack.27.place
  17.9 0.6 copy-done.3
  18.5 0.1 copy-done.5
  18.5 10.0 %shard_map.55 = (f32[16,128]{1,0:T(8,128)S(1)}, f32[16,128]{1,0:T(8,128)S(1)}) custom-call(f32[16,16]{1,0:T(8,128)S(1)} %copy-done.3, f32[1,16]{1,0:T(1,128)S(1)} %bitcast.30), custom_call_target="tpu_custom_call" | custom-call | flops 10485760 | bytes 1048576 | tf_op jit(solution)/shard_map/pallas_call | solution.py:352
  28.5 0.0 collective-permute-done.4.following
  28.6 0.0 copy-start.4
  28.6 0.6 copy-done.4
  29.2 5.1 %shard_map.57 = (f32[48,16,128]{2,1,0:T(8,128)S(1)}, f32[128,128]{1,0:T(8,128)}) custom-call(s32[6]{0:T(128)S(1)} %stack.27.place, f32[768,128]{1,0:T(8,128)S(1)} %bitcast.22, f32[768,128]{1,0:T(8,128)S(1)} %collective-permute-done.low, f32[768,128]{1,0:T(8,128)S(1)} %collective-permute-done.1.high, s32[16,128]{1,0:T(8,128)S(1)} %copy-done.2, ...), custom_call_target="tpu_custom_call" | custom-call | flops 1048576 | bytes 1048576 | tf_op jit(solution)/shard_map/pallas_call | solution.py:352
  34.3 9.6 %all-to-all-start = ((f32[32,4,128]{2,1,0:T(4,128)}), f32[32,4,128]{2,1,0:T(4,128)S(1)}, u32[]{:S(2)}, u32[]{:S(2)}) async-start(f32[32,4,128]{2,1,0:T(4,128)} %bitcast.9), calls=%async_computation | async-start | bytes 131072 | tf_op jit(solution)/shard_map/all_to_all | solution.py:366
  44.0 7.4 %all-to-all-done = f32[32,4,128]{2,1,0:T(4,128)S(1)} async-done(((f32[32,4,128]{2,1,0:T(4,128)}), f32[32,4,128]{2,1,0:T(4,128)S(1)}, u32[]{:S(2)}, u32[]{:S(2)}) %all-to-all-start) | async-done | bytes 65568 | tf_op jit(solution)/shard_map/all_to_all | solution.py:366
  51.4 27.1 %all_to_all.45 = f32[4,64,128]{2,1,0:T(8,128)S(1)} all-to-all(f32[4,64,128]{2,1,0:T(8,128)S(1)} %bitcast.33), channel_id=1, replica_groups=mesh['zl'=4,'x'=4,'zh'=4,'y'=4,'c'=2] {'zh'}, dimensions={0} | all-to-all | bytes 262144 | tf_op jit(solution)/shard_map/all_to_all | solution.py:366
  78.5 1.0 shard_map.58
  79.5 20.5 %all_to_all.46 = f32[8,96,128]{2,1,0:T(8,128)S(1)} all-to-all(f32[8,96,128]{2,1,0:T(8,128)S(1)} %bitcast.24), channel_id=1, replica_groups=mesh['zl'=4,'x'=4,'zh'=4,'y'=4,'c'=2] {'zl','c'}, dimensions={0} | all-to-all | bytes 786432 | tf_op jit(solution)/shard_map/all_to_all | solution.py:366
  100.0 2.0 %shard_map.59 = f32[128,128]{1,0:T(8,128)S(1)} custom-call(s32[6]{0:T(128)S(1)} %stack.27.place, f32[768,128]{1,0:T(8,128)S(1)} %bitcast.18, f32[192,128]{1,0:T(8,128)S(1)} %get-tuple-element.17.jumps, f32[32,128]{1,0:T(8,128)S(1)} %get-tuple-element.18.mask, f32[16,128]{1,0:T(8,128)S(1)} %get-tuple-element.15.values, s32[1,128]{1,0:T(1,128)S(1)} %bitcast.29), custom_call_target="tpu_custom_call" | custom-call | flops 1048576 | bytes 1048576 | tf_op jit(solution)/shard_map/pallas_call | solution.py:352
  102.0 10.6 %all_to_all.47 = f32[32,4,128]{2,1,0:T(4,128)S(1)} all-to-all(f32[32,4,128]{2,1,0:T(4,128)S(1)} %bitcast.25), channel_id=1, replica_groups=mesh['zl'=4,'x'=4,'zh'=4,'y'=4,'c'=2] {'x','y','c'}, dimensions={0} | all-to-all | bytes 131072 | tf_op jit(solution)/shard_map/all_to_all | solution.py:366
  112.6 1.7 %shard_map.60 = f32[768,128]{1,0:T(8,128)} custom-call(s32[6]{0:T(128)S(1)} %stack.27.place, f32[48,16,128]{2,1,0:T(8,128)S(1)} %get-tuple-element.13.fine, f32[128,128]{1,0:T(8,128)S(1)} %bitcast.26, f32[16,128]{1,0:T(8,128)S(1)} %get-tuple-element.12.vectors, f32[1,16]{1,0:T(1,128)S(1)} %bitcast.32), custom_call_target="tpu_custom_call" | custom-call | flops 1048576 | bytes 1048576 | tf_op jit(solution)/shard_map/pallas_call | solution.py:352
  (12 shorter events, 0.0 us)
Async XLA Ops:
  0.0 28.5 %collective-permute-start.1 = (f32[768,128]{1,0:T(8,128)}, f32[768,128]{1,0:T(8,128)S(1)}, u32[]{:S(2)}, u32[]{:S(2)}) collective-permute-start(f32[768,128]{1,0:T(8,128)} %bitcast.19), channel_id=1, source_target_pairs={{1,0},{2,1},{3,2},{4,3},{5,4},{6,5},{7,6},{8,7},{9,8},{10,9},{11,1... | collective-permute-start | bytes 1179656 | tf_op jit(solution)/shard_map/ppermute | solution.py:380
  8.8 19.8 %collective-permute-start = (f32[768,128]{1,0:T(8,128)}, f32[768,128]{1,0:T(8,128)S(1)}, u32[]{:S(2)}, u32[]{:S(2)}) collective-permute-start(f32[768,128]{1,0:T(8,128)} %bitcast.20), channel_id=1, source_target_pairs={{0,1},{1,2},{2,3},{3,4},{4,5},{5,6},{6,7},{7,8},{8,9},{9,10},{10,1... | collective-permute-start | bytes 1179656 | tf_op jit(solution)/shard_map/ppermute | solution.py:379
  10.7 1.0 copy-start
  11.7 1.7 %copy-start.2 = (s32[16,128]{1,0:T(8,128)S(1)}, s32[16,128]{1,0:T(8,128)}, u32[]{:S(2)}) copy-start(s32[16,128]{1,0:T(8,128)} %mask_own.1) | copy-start | bytes 24580
  11.7 16.9 %copy-start.1 = (f32[1,3,16,16,128]{4,3,2,1,0:T(8,128)S(1)}, f32[1,3,16,16,128]{4,3,2,1,0:T(8,128)}, u32[]{:S(2)}) copy-start(f32[1,3,16,16,128]{4,3,2,1,0:T(8,128)} %param.5) | copy-start | bytes 1179652
  12.1 16.4 %collective-permute-start.4 = (f32[48,128]{1,0:T(8,128)S(1)}, f32[48,128]{1,0:T(8,128)S(1)}, u32[]{:S(2)}, u32[]{:S(2)}) collective-permute-start(f32[48,128]{1,0:T(8,128)S(1)} %shard_map.56), channel_id=1, source_target_pairs={{32,0},{64,32},{96,64},{128,96},{160,128},{192,160},{224,192},{256... | collective-permute-start | bytes 73736 | tf_op jit(solution)/shard_map/ppermute | solution.py:387
  13.4 15.1 %collective-permute-start.2 = (s32[16,128]{1,0:T(8,128)S(1)}, s32[16,128]{1,0:T(8,128)S(1)}, u32[]{:S(2)}, u32[]{:S(2)}) collective-permute-start(s32[16,128]{1,0:T(8,128)S(1)} %copy-done.2), channel_id=1, source_target_pairs={{0,1},{1,2},{2,3},{3,4},{4,5},{5,6},{6,7},{7,8},{8,9},{9,10},{10,1... | collective-permute-start | bytes 24584 | tf_op jit(solution)/shard_map/ppermute | solution.py:381
  15.4 13.2 %collective-permute-start.3 = (s32[16,128]{1,0:T(8,128)S(1)}, s32[16,128]{1,0:T(8,128)S(1)}, u32[]{:S(2)}, u32[]{:S(2)}) collective-permute-start(s32[16,128]{1,0:T(8,128)S(1)} %copy-done.2), channel_id=1, source_target_pairs={{1,0},{2,1},{3,2},{4,3},{5,4},{6,5},{7,6},{8,7},{9,8},{10,9},{11,1... | collective-permute-start | bytes 24584 | tf_op jit(solution)/shard_map/ppermute | solution.py:382
  17.8 0.7 copy-start.3
  17.9 0.7 copy-start.5
  28.6 0.7 copy-start.4
  34.3 17.0 %all-to-all-start = ((f32[32,4,128]{2,1,0:T(4,128)}), f32[32,4,128]{2,1,0:T(4,128)S(1)}, u32[]{:S(2)}, u32[]{:S(2)}) async-start(f32[32,4,128]{2,1,0:T(4,128)} %bitcast.9), calls=%async_computation | async-start | bytes 131072 | tf_op jit(solution)/shard_map/all_to_all | solution.py:366

commit v2 on v0

v2 whole, which is shorter than its diff:
```python
import functools

import jax
import jax.numpy as jnp
from jax import lax
from jax.experimental import pallas as pl
from jax.experimental.pallas import tpu as pltpu
from jax.sharding import Mesh
from jax.sharding import PartitionSpec as P

LAYERS = 16
ZONAL = 128
FINE_STEPS = 8
BAND = 16
BANDS = 32
EXTENT = BAND * BANDS
HALO = 2 * FINE_STEPS
SPAN = BAND + 2 * HALO
FRICTION = 0.02
CUT = 2 * LAYERS * BAND
MASK = 3 * LAYERS * BAND
HIGHEST = lax.Precision.HIGHEST
F32 = jnp.float32
BF16 = jnp.bfloat16

SPACE = ("zh", "y", "c")
TIME = ("zl", "x")
PLANE = ("x", "y", "c")

SHIFT = 1.0


def iota(shape, axis):
    return lax.broadcasted_iota(jnp.int32, shape, axis)


def two_parts(x):
    top = x.astype(BF16)
    return top, (x - top.astype(F32)).astype(BF16)


def dot3(a, b):
    (a_top, a_rest), (b_top, b_rest) = two_parts(a), two_parts(b)
    left = jnp.concatenate([a_top, a_top, a_rest], axis=1)
    right = jnp.concatenate([b_top, b_rest, b_top], axis=0)
    return jnp.dot(left, right, preferred_element_type=F32)


def block_mean(rows):
    part = iota(rows[0].shape, 1) % 4

    def pairs(x, y, step):
        first = (part & step) == 0
        return jnp.where(first, x + pltpu.roll(x, ZONAL - step, 1), y + pltpu.roll(y, step, 1))

    return pairs(pairs(rows[0], rows[1], 1), pairs(rows[2], rows[3], 1), 2) * (1.0 / 16.0)


def pack_kernel(state, mask, packed, first, rest, restricted, rows, sems):
    copies = [
        pltpu.make_async_copy(state, packed.at[pl.ds(0, MASK)], sems.at[0]),
        pltpu.make_async_copy(mask, rows, sems.at[1]),
    ]
    for copy in copies:
        copy.start()
    for copy in copies:
        copy.wait()
    packed[MASK:, :] = rows[...].astype(F32)
    first[...] = packed[:CUT, :]
    rest[...] = packed[CUT:, :]
    for f in range(3):
        rows = []
        for cr in range(4):
            here = [packed[pl.ds(f * 256 + 4 * cr + r, LAYERS, stride=BAND), :] for r in range(4)]
            rows.append(here[0] + here[1] + here[2] + here[3])
        restricted[f * LAYERS : (f + 1) * LAYERS, :] = block_mean(rows)


def modes_kernel(coupling, depths, vectors, values):
    row = iota((LAYERS, ZONAL), 0)
    lane = iota((LAYERS, ZONAL), 1)
    eye = row == lane
    root = jnp.sqrt(depths[...])
    root = jnp.concatenate([root, jnp.zeros((1, ZONAL - LAYERS), F32)], axis=1)
    root_lanes = jnp.broadcast_to(root, (LAYERS, ZONAL))
    root_rows = jnp.sum(jnp.where(eye, root_lanes, 0.0), axis=1, keepdims=True)
    matrix = jnp.concatenate([coupling[...], jnp.zeros((LAYERS, ZONAL - LAYERS), F32)], axis=1)
    matrix = matrix * root_lanes * root_rows
    start = matrix + jnp.where(eye, SHIFT, 0.0) + jnp.where(lane == row + LAYERS, 1.0, 0.0)
    active = iota((8, ZONAL), 1) < LAYERS
    sub = iota((8, ZONAL), 0)

    def sums(x):
        return jnp.broadcast_to(jnp.sum(jnp.where(active, x, 0.0), axis=1, keepdims=True), x.shape)

    def turn(width, x):
        if width == 8:
            return pltpu.roll(x, 1, 0)
        return jnp.where((sub & (width - 1)) == 0, pltpu.roll(x, 9 - width, 0), pltpu.roll(x, 1, 0))

    def regroup(half, x, y):
        low = (sub & half) == 0
        return jnp.where(low, x, pltpu.roll(y, half, 0)), jnp.where(low, pltpu.roll(x, 8 - half, 0), y)

    def sweep(carry):
        count, _, x, y = carry
        xx, yy = sums(x * x), sums(y * y)
        worst = jnp.zeros((8, ZONAL), F32)
        for width in (8, 4, 2, 1):
            for _ in range(width):
                xy = sums(x * y)
                gap = yy - xx
                side = jnp.maximum(jnp.abs(gap), 1e-12)
                scale = lax.rsqrt(side * side + 4.0 * xy * xy)
                square = 0.5 + 0.5 * side * scale
                cosine_over = lax.rsqrt(square)
                signed = jnp.where(gap >= 0.0, xy, -xy) * scale
                cosine = square * cosine_over
                sine = signed * cosine_over
                tangent_xy = signed * xy / square
                worst = jnp.maximum(worst, jnp.abs(xy))
                x, y = cosine * x - sine * y, sine * x + cosine * y
                xx, yy = xx - tangent_xy, yy + tangent_xy
                if width > 1:
                    y, yy = turn(width, y), turn(width, yy)
            if width > 1:
                x, y = regroup(width // 2, x, y)
                xx, yy = regroup(width // 2, xx, yy)
        return count + 1, jnp.max(worst), x, y

    def unfinished(carry):
        return jnp.logical_and(carry[0] < 12, carry[1] > 2e-4)

    _, _, x, y = lax.while_loop(unfinished, sweep, (0, jnp.float32(1.0), start[:8], start[8:]))
    x = jnp.concatenate([x, y], axis=0)
    active = lane < LAYERS
    turned = pltpu.roll(x, ZONAL - LAYERS, 1)
    vectors[...] = jnp.where(active, turned, 0.0)
    value = jnp.sum(jnp.where(active, x * turned, 0.0), axis=1, keepdims=True) - SHIFT
    values[...] = jnp.broadcast_to(value, (LAYERS, ZONAL))


def east(x):
    flat = x.reshape(-1, ZONAL)
    return (pltpu.roll(flat, ZONAL - 1, 1) - pltpu.roll(flat, 1, 1)).reshape(x.shape)


def fine_tools(fields, ps, ms, fs, coupling, depths):
    hs, us, vs = fields
    half_top, half_rest = two_parts(0.5 * coupling[...])
    weights = jnp.concatenate([half_top, half_top, half_rest], axis=1)
    lanes = jnp.broadcast_to(depths[...], (LAYERS, LAYERS))
    eye = iota((LAYERS, LAYERS), 0) == iota((LAYERS, LAYERS), 1)
    thick = 0.5 * jnp.sum(jnp.where(eye, lanes, 0.0), axis=1, keepdims=True)
    thick = jnp.broadcast_to(thick, (LAYERS, ZONAL)).reshape(1, 2, 8, ZONAL)
    keep = 1.0 - FRICTION

    def pressure(low, high):
        wide = jnp.concatenate([hs[j].reshape(LAYERS, ZONAL) for j in range(low, high)], axis=1)
        top, rest = two_parts(wide)
        stacked = jnp.concatenate([top, rest, top], axis=0)
        result = jnp.dot(weights, stacked, preferred_element_type=F32)
        for j in range(low, high):
            ps[j] = result[:, (j - low) * ZONAL : (j - low + 1) * ZONAL].reshape(2, 8, ZONAL)

    def velocity(low, high):
        m = ms[low:high][:, None]
        f = fs[low:high][:, None]
        u = us[low:high]
        v = vs[low:high]
        u = m * (keep * u + f * v - east(ps[low:high]))
        v = m * (keep * v - f * u - (ps[low + 1 : high + 1] - ps[low - 1 : high - 1]))
        us[low:high] = u
        vs[low:high] = v

    def thickness(low, high):
        m = ms[low:high][:, None]
        spread = east(us[low:high]) + (vs[low + 1 : high + 1] - vs[low - 1 : high - 1])
        hs[low:high] = m * (hs[low:high] - thick * spread)

    def steps(bounds):
        for low, ends in bounds:
            for at in range(low, ends[0], 4):
                pressure(at, min(at + 4, ends[0]))
            for at in range(low + 1, ends[1], 4):
                velocity(at, min(at + 4, ends[1]))
            for at in range(low + 2, ends[2], 4):
                thickness(at, min(at + 4, ends[2]))

    return steps


def core_index():
    return lax.axis_index("c")


def band_index():
    return lax.axis_index("zh") * 8 + lax.axis_index("y") * 2 + lax.axis_index("c")


def mode_index():
    return lax.axis_index("x") * 4 + lax.axis_index("y")


def put_band(fields, ms, begin, blocks, cut, core, sign):
    for odd in (False, True):

        @pl.when(core == int(odd))
        def _():
            for r in range(BAND):
                row = begin + (BAND - 1 - r if odd else r)
                for f in range(3):
                    at = f * 256 + r - (cut if f == 2 else 0)
                    value = blocks[f // 2][pl.ds(at, LAYERS, stride=BAND), :].reshape(2, 8, ZONAL)
                    fields[f][row] = sign * value if f == 2 else value
                at = MASK - cut + r
                ms[row] = jnp.broadcast_to(blocks[1][at : at + 1, :], (8, ZONAL))


def coriolis_table(fs, position, core, sign):
    offset = iota(fs.shape, 0) - HALO
    rows = position * BAND + jnp.where(core == 1, BAND - 1 - offset, offset)
    latitude = (rows.astype(F32) + 0.5) / float(EXTENT)
    latitude = jnp.where(latitude > 1.0, 2.0 - latitude, latitude)
    fs[...] = sign * (0.3 * (latitude - 0.5))


KEPT = 20


def inner_kernel(
    own, mate_first, mate_rest, fold, coupling, depths, h_out, u_out, v_out, fold_out, hs, us, vs, ps, ms, fs
):
    core = core_index()
    sign = (1 - 2 * core).astype(F32)
    fields = (hs, us, vs)
    put_band(fields, ms, HALO, (own, own), 0, core, sign)
    put_band(fields, ms, HALO + BAND, (mate_first, mate_rest), CUT, core, sign)
    coriolis_table(fs, band_index(), core, sign)
    steps = fine_tools(fields, ps, ms, fs, coupling, depths)
    ends = [SPAN - 2 * t for t in range(FINE_STEPS)]
    steps([(HALO + 2 * t, (ends[t], ends[t] - 1, ends[t] - 2)) for t in range(FINE_STEPS)])
    fold_out[...] = fold[...].astype(F32)
    for out, field in zip((h_out, u_out, v_out), fields):
        out[...] = field[HALO : HALO + KEPT]


def outer_kernel(
    own, other, h_in, u_in, v_in, fold, coupling, depths, vectors, following,
    fine, chunk, hs, us, vs, ps, ms, fs,
):
    position = band_index()
    core = core_index()
    sign = (1 - 2 * core).astype(F32)
    on_top = position == BANDS - 1
    fields = (hs, us, vs)
    for field, kept in zip(fields, (h_in, u_in, v_in)):
        field[HALO : HALO + KEPT] = kept[...]
    for r in range(BAND):
        row = HALO + r + core * (BAND - 1 - 2 * r)
        ms[row] = jnp.broadcast_to(own[MASK + r : MASK + r + 1, :], (8, ZONAL))

    @pl.when(jnp.logical_not(on_top))
    def _():
        put_band(fields, ms, 0, (other, other), 0, core, sign)

    @pl.when(on_top)
    def _():
        index = jnp.broadcast_to(fold[...].astype(jnp.int32), (LAYERS, ZONAL))
        for r in range(BAND):
            for f in range(3):
                image = own[pl.ds(f * 256 + r, LAYERS, stride=BAND), :]
                image = jnp.take_along_axis(image, index, axis=1).reshape(2, 8, ZONAL)
                fields[f][r] = -image if f == 1 else image
            image = jnp.broadcast_to(own[MASK + r : MASK + r + 1, :], (8, ZONAL))
            ms[r] = jnp.take_along_axis(image, index[:8], axis=1)

    coriolis_table(fs, position, core, sign)
    steps = fine_tools(fields, ps, ms, fs, coupling, depths)
    steps([(2 * t, (2 * t + 18, 2 * t + 17, 2 * t + 18)) for t in range(FINE_STEPS)])

    def row_of(r):
        return HALO + r + core * (BAND - 1 - 2 * r)

    root = jnp.sqrt(depths[...])
    jumps = []
    for f in range(3):
        rows = []
        for cr in range(4):
            here = [fields[f][row_of(4 * cr + r)].reshape(LAYERS, ZONAL) for r in range(4)]
            if f == 2:
                here = [sign * row for row in here]
            for r in range(4):
                fine[f * BAND + 4 * cr + r] = here[r]
            rows.append(here[0] + here[1] + here[2] + here[3])
        jumps.append(block_mean(rows) - following[f * LAYERS : (f + 1) * LAYERS, :])
    of_thickness = dot3(vectors[:, :LAYERS] / root, jumps[0])
    of_velocity = dot3(vectors[:, :LAYERS] * root, jnp.concatenate(jumps[1:], axis=1))
    for f, in_modes in enumerate((of_thickness, of_velocity[:, :ZONAL], of_velocity[:, ZONAL:])):
        chunk[pl.ds(f, LAYERS, stride=8), :] = in_modes
        chunk[pl.ds(4 + f, LAYERS, stride=8), :] = in_modes
    rows = []
    for cr in range(4):
        here = [ms[row_of(4 * cr + r)] for r in range(4)]
        rows.append(here[0] + here[1] + here[2] + here[3])
    chunk[pl.ds(3, BANDS, stride=4), :] = jnp.broadcast_to(block_mean(rows)[:1], (BANDS, ZONAL))


def coarse_tools(value, masks, fold):
    sub = iota((8, ZONAL), 0)
    lane = iota((8, ZONAL), 1)
    seg = lane % 4
    coriolis = []
    for cr in range(4):
        position = ((seg * 8 + sub) * 4 + cr).astype(F32)
        coriolis.append((4.0 * 0.3) * ((position + 0.5) / float(EXTENT // 4) - 0.5))
    keep = 1.0 - 4.0 * FRICTION
    k = fold[0, 0] // 4
    fold_index = 4 * ((k - lane // 4 + 32) % 32) + 3
    last, top = sub == 7, jnp.logical_and(sub == 7, seg == 3)
    first, bottom = sub == 0, jnp.logical_and(sub == 0, seg == 0)

    def east(x):
        return pltpu.roll(x, ZONAL - 4, 1) - pltpu.roll(x, 4, 1)

    def north(x, sign):
        up = pltpu.roll(x[0], 7, 0)
        up = jnp.where(last, pltpu.roll(up, ZONAL - 1, 1), up)
        up = jnp.where(top, sign * jnp.take_along_axis(x[3], fold_index, axis=1), up)
        down = pltpu.roll(x[3], 1, 0)
        down = jnp.where(first, pltpu.roll(down, 1, 1), down)
        down = jnp.where(bottom, 0.0, down)
        return [x[1] - down, x[2] - x[0], x[3] - x[1], up - x[2]]

    def propagate(state):
        h, u, v = state
        for _ in range(2):
            p = [(0.5 * value) * x for x in h]
            north_p = north(p, 1.0)
            u = [masks[i] * (keep * u[i] + coriolis[i] * v[i] - east(p[i])) for i in range(4)]
            v = [masks[i] * (keep * v[i] - coriolis[i] * u[i] - north_p[i]) for i in range(4)]
            north_v = north(v, -1.0)
            h = [masks[i] * (h[i] - 0.5 * (east(u[i]) + north_v[i])) for i in range(4)]
        return [h, u, v]

    return propagate


def load_state(ref, begin=0):
    return [[ref[begin + f * 32 + cr * 8 : begin + f * 32 + cr * 8 + 8, :] for cr in range(4)] for f in range(3)]


def store_state(ref, state, begin=0):
    for f in range(3):
        for cr in range(4):
            ref[begin + f * 32 + cr * 8 : begin + f * 32 + cr * 8 + 8, :] = state[f][cr]


def add_state(a, b):
    return [[x + y for x, y in zip(p, q)] for p, q in zip(a, b)]


def load_masks(ref):
    return [ref[cr * 8 : cr * 8 + 8, :] for cr in range(4)]


def pair_kernel(gathered, values, fold, jumps, mask_out, total):
    lane = iota((8, ZONAL), 1)
    seg = lane % 4
    for x in range(2):
        for f in range(4 if x == 0 else 3):
            rows = [None] * 4
            for zh in range(4):
                piece = gathered[pl.ds(zh * 64 + x * 32 + f, 8, stride=4), :]
                for cr in range(4):
                    shift = (zh - cr) % ZONAL
                    moved = pltpu.roll(piece, shift, 1) if shift else piece
                    rows[cr] = moved if zh == 0 else jnp.where(seg == zh, moved, rows[cr])
            for cr in range(4):
                if f == 3:
                    mask_out[cr * 8 : cr * 8 + 8, :] = rows[cr]
                else:
                    begin = x * 96 + f * 32 + cr * 8
                    jumps[begin : begin + 8, :] = rows[cr]
    propagate = coarse_tools(values[pl.ds(mode_index(), 1), :], load_masks(mask_out), fold)
    store_state(total, add_state(propagate(load_state(jumps)), load_state(jumps, 96)))


def group_kernel(total, mate, mask, values, fold, both):
    propagate = coarse_tools(values[pl.ds(mode_index(), 1), :], load_masks(mask), fold)
    odd = core_index() == 1
    mine, theirs = load_state(total), load_state(mate)
    earlier = [[jnp.where(odd, t, m) for m, t in zip(a, b)] for a, b in zip(mine, theirs)]
    later = [[jnp.where(odd, m, t) for m, t in zip(a, b)] for a, b in zip(mine, theirs)]
    store_state(both, add_state(propagate(propagate(earlier)), later))


def chain_kernel(one, two, three, mate, jumps, mask, values, fold, chunk):
    quarter = lax.axis_index("zh")
    core = core_index()
    propagate = coarse_tools(values[pl.ds(mode_index(), 1), :], load_masks(mask), fold)

    def twice(state):
        return propagate(propagate(state))

    state = load_state(three)
    for ref in (two, one):
        state = lax.fori_loop(0, 2, lambda _, s: twice(s), state)
        state = add_state(state, load_state(ref))
    state = lax.fori_loop(0, core, lambda _, s: add_state(twice(s), load_state(mate)), state)
    seg = iota((8, ZONAL), 1) % 4
    chunk[...] = jnp.zeros_like(chunk)
    for x in range(2):
        state = propagate(state)
        for f in range(3):
            packed = None
            for cr in range(4):
                piece = pltpu.roll(state[f][cr], lax.rem(cr - quarter + ZONAL, ZONAL), 1)
                packed = piece if cr == 0 else jnp.where(seg == cr, piece, packed)
            chunk[pl.ds((2 * core + x) * 32 + f, 8, stride=4), :] = packed
        if x == 0:
            state = add_state(state, load_state(jumps))


def correct_kernel(fine, gathered, vectors, depths, out, result, sems):
    half = lax.axis_index("x") // 2
    lanes = jnp.broadcast_to(depths[...], (LAYERS, LAYERS))
    eye = iota((LAYERS, LAYERS), 0) == iota((LAYERS, LAYERS), 1)
    root = jnp.sqrt(jnp.sum(jnp.where(eye, lanes, 0.0), axis=1, keepdims=True))
    lane = iota((LAYERS, ZONAL), 1)
    copies = []
    for f in range(3):
        in_modes = gathered[pl.ds(half * 4 + f, LAYERS, stride=8), :]
        change = lax.dot_general(
            vectors[:, :LAYERS], in_modes, (((0,), (0,)), ((), ())),
            precision=HIGHEST, preferred_element_type=F32,
        )
        change = change * root if f == 0 else change / root
        for cr in range(4):
            spread = jnp.take_along_axis(change, lane // 4 * 4 + cr, axis=1)
            for r in range(4):
                row = 4 * cr + r
                result[pl.ds(f * 256 + row, LAYERS, stride=BAND), :] = fine[f * BAND + row] + spread
        here = pl.ds(f * 256, 256)
        copies.append(pltpu.make_async_copy(result.at[here], out.at[here], sems.at[f]))
        copies[-1].start()
    for copy in copies:
        copy.wait()


def call(kernel, out_shapes, scratch=(), spaces=None, out_space=pltpu.VMEM, flops=1 << 20, vmem=24 << 20):
    def run(*arrays):
        specs = [pl.BlockSpec(memory_space=s) for s in spaces or (pltpu.VMEM,) * len(arrays)]
        return pl.pallas_call(
            kernel,
            out_shape=[jax.ShapeDtypeStruct(s, F32) for s in out_shapes],
            in_specs=specs,
            out_specs=[pl.BlockSpec(memory_space=out_space)] * len(out_shapes),
            scratch_shapes=list(scratch),
            compiler_params=pltpu.CompilerParams(vmem_limit_bytes=vmem),
            cost_estimate=pl.CostEstimate(flops=flops, bytes_accessed=1 << 20, transcendentals=0),
        )(*arrays)

    return run


def swap(block, axes):
    return lax.all_to_all(block, axes, 0, 0, tiled=True)


def body(start_state, land_mask, fold_map, coupling, depths):
    own, first, rest, restricted = call(
        pack_kernel,
        [(MASK + BAND, ZONAL), (CUT, ZONAL), (MASK + BAND - CUT, ZONAL), (3 * LAYERS, ZONAL)],
        [pltpu.VMEM((BAND, ZONAL), jnp.int32), pltpu.SemaphoreType.DMA((2,))],
        spaces=(pl.ANY, pl.ANY),
    )(start_state.reshape(MASK, ZONAL), land_mask)
    fold = fold_map.reshape(1, ZONAL)
    depth_row = depths.reshape(1, LAYERS)
    across = [(i, i + 1) for i in range(1, BANDS - 1, 2)]
    across += [(b, a) for a, b in across]
    other = lax.ppermute(own, SPACE, across)
    following = lax.ppermute(restricted, TIME, [(n + 1, n) for n in range(15)])
    vectors, values = call(modes_kernel, [(LAYERS, ZONAL), (LAYERS, ZONAL)], flops=10 << 20)(
        coupling, depth_row
    )
    inside = [(i, i ^ 1) for i in range(BANDS)]
    mate = [lax.ppermute(part, SPACE, inside) for part in (first, rest)]

    state = pltpu.VMEM((SPAN, 2, 8, ZONAL), F32)
    table = pltpu.VMEM((SPAN, 8, ZONAL), F32)
    scratch = [state, state, state, state, table, table]
    *inner, fold_held = call(
        inner_kernel, [(KEPT, 2, 8, ZONAL)] * 3 + [(1, ZONAL)], scratch, flops=4 << 20
    )(own, *mate, fold, coupling, depth_row)
    fine, chunk = call(
        outer_kernel, [(3 * BAND, LAYERS, ZONAL), (4 * BANDS, ZONAL)], scratch
    )(
        own, other, *inner, fold_held, coupling, depth_row, vectors, following
    )

    spread = swap(chunk, PLANE)
    mine = lax.dynamic_slice_in_dim(spread, lax.axis_index("c") * 64, 64, 0)
    grid = swap(jnp.concatenate([mine] * 4, axis=0), ("zh",))
    jumps, mask, total = call(
        pair_kernel, [(192, ZONAL), (32, ZONAL), (96, ZONAL)]
    )(grid, values, fold)
    mate = lax.ppermute(total, ("c",), [(0, 1), (1, 0)])
    (both,) = call(group_kernel, [(96, ZONAL)])(total, mate, mask, values, fold)
    one, two, three = (
        lax.ppermute(both, ("zl",), [(i, i + d) for i in range(4 - d)]) for d in (1, 2, 3)
    )
    (chunk,) = call(chain_kernel, [(4 * BANDS, ZONAL)])(
        one, two, three, mate, jumps, mask, values, fold
    )
    change = swap(chunk, PLANE)
    (result,) = call(
        correct_kernel,
        [(MASK, ZONAL)],
        [pltpu.VMEM((MASK, ZONAL), F32), pltpu.SemaphoreType.DMA((3,))],
        out_space=pl.ANY,
    )(
        fine, change, vectors, depth_row
    )
    return result.reshape(1, 3, LAYERS, BAND, ZONAL)


def solution(mesh):
    parts = Mesh(mesh.devices.reshape(4, 4, 4, 4, 2), ("zl", "x", "zh", "y", "c"))
    return jax.shard_map(
        body,
        mesh=parts,
        in_specs=(P(TIME, None, None, SPACE, None), P(SPACE, None), P(), P(), P()),
        out_specs=P(TIME, None, None, SPACE, None),
        check_vma=False,
    )
```

time: 588 us -> 104 us (0.18)
  the two profiles are of different devices: /device:TPU:416 before, /device:TPU:1 now
where the time goes in v2:
time: 104 us
  blocking collectives  38.1 us (37%)
  starting transfers between devices  33 us (32%)
  Pallas kernels  20.4 us (20%)
  waiting for transfers between devices  9.55 us (9%)
  local copies, waits for them, and re-layouts  2.35 us (2%)
    all_to_all x2, blocking collectives, swap(): return lax.all_to_all(block, axes, 0, 0, tiled=True)  38.1 us
    pallas_call x8, Pallas kernels, run(): pl.pallas_call(kernel, out_shape=[jax.ShapeDtypeStruct(s, F32) for s in o...  20.4 us
    all_to_all x1, starting transfers between devices, swap(): return lax.all_to_all(block, axes, 0, 0, tiled=True)  12.2 us
    all_to_all x1, waiting for transfers between devices, swap(): return lax.all_to_all(block, axes, 0, 0, tiled=True)  7.36 us
    ppermute x2, starting transfers between devices, body(): mate = [lax.ppermute(part, SPACE, inside) for part in (first, rest)]  6.8 us
    ppermute x1, starting transfers between devices, body(): other = lax.ppermute(own, SPACE, across)  4.59 us
    ppermute x3, starting transfers between devices, body(): lax.ppermute(both, ('zl',), [(i, i + d) for i in range(4 - d)])  4.44 us
    ppermute x1, starting transfers between devices, body(): mate = lax.ppermute(total, ('c',), [(0, 1), (1, 0)])  3.73 us
  transfers between devices with their start and end apart: 9, of which 3 were waited for; matrix products, arithmetic and copies ran while one was open for 0% of the time, Pallas kernels for 10%

profile of v2, /device:TPU:1, one launch (start us, length us, event | category | flops | bytes accessed | tf_op | source)
XLA Modules:
  0.0 103.6 jit_solution(2147406663228567937)
XLA Ops:
  0.0 1.0 copy-done
  1.0 0.7 copy-done.3
  1.7 0.5 shard_map.55
  2.2 4.6 %collective-permute-start = (f32[784,128]{1,0:T(8,128)S(1)}, f32[784,128]{1,0:T(8,128)S(1)}, u32[]{:S(2)}, u32[]{:S(2)}) collective-permute-start(f32[784,128]{1,0:T(8,128)S(1)} %get-tuple-element.20.own), channel_id=1, source_target_pairs={{1,2},{3,4},{5,6},{7,8},{9,10},{11,12},{13,14},{15,16},{17,18},{19... | collective-permute-start | bytes 1204232 | tf_op jit(solution)/shard_map/ppermute | solution.py:482
  6.8 4.9 %collective-permute-start.1 = (f32[512,128]{1,0:T(8,128)S(1)}, f32[512,128]{1,0:T(8,128)S(1)}, u32[]{:S(2)}, u32[]{:S(2)}) collective-permute-start(f32[512,128]{1,0:T(8,128)S(1)} %get-tuple-element.21), channel_id=1, source_target_pairs={{0,1},{1,0},{2,3},{3,2},{4,5},{5,4},{6,7},{7,6},{8,9},{9,8},{10,11... | collective-permute-start | bytes 786440 | tf_op jit(solution)/shard_map/ppermute | solution.py:488
  11.7 1.9 %collective-permute-start.2 = (f32[272,128]{1,0:T(8,128)S(1)}, f32[272,128]{1,0:T(8,128)S(1)}, u32[]{:S(2)}, u32[]{:S(2)}) collective-permute-start(f32[272,128]{1,0:T(8,128)S(1)} %get-tuple-element.22), channel_id=1, source_target_pairs={{0,1},{1,0},{2,3},{3,2},{4,5},{5,4},{6,7},{7,6},{8,9},{9,8},{10,11... | collective-permute-start | bytes 417800 | tf_op jit(solution)/shard_map/ppermute | solution.py:488
  13.6 1.3 %collective-permute-start.3 = (f32[48,128]{1,0:T(8,128)S(1)}, f32[48,128]{1,0:T(8,128)S(1)}, u32[]{:S(2)}, u32[]{:S(2)}) collective-permute-start(f32[48,128]{1,0:T(8,128)S(1)} %get-tuple-element.28), channel_id=1, source_target_pairs={{32,0},{64,32},{96,64},{128,96},{160,128},{192,160},{224,192},{256... | collective-permute-start | bytes 73736 | tf_op jit(solution)/shard_map/ppermute | solution.py:483
  14.9 7.7 %shard_map.57 = (f32[16,128]{1,0:T(8,128)S(1)}, f32[16,128]{1,0:T(8,128)S(1)}) custom-call(f32[16,16]{1,0:T(8,128)S(1)} %copy-done.1, f32[1,16]{1,0:T(1,128)S(1)} %bitcast.18), custom_call_target="tpu_custom_call" | custom-call | flops 10485760 | bytes 1048576 | tf_op jit(solution)/shard_map/pallas_call | solution.py:454
  22.7 0.6 copy-done.2
  23.3 2.6 %shard_map.56 = (f32[20,2,8,128]{3,2,1,0:T(8,128)S(1)}, f32[20,2,8,128]{3,2,1,0:T(8,128)S(1)}, f32[20,2,8,128]{3,2,1,0:T(8,128)S(1)}, f32[1,128]{1,0:T(1,128)S(1)}) custom-call(f32[784,128]{1,0:T(8,128)S(1)} %get-tuple-element.20.own, f32[512,128]{1,0:T(8,128)S(1)} %collective-permute-done.1.mate_first, f32[272,128]{1,0:T(8,128)S(1)} %collective-permute-done.2.mate_rest, ...), custom_call_target="tpu_custom_call" | custom-call | flops 4194304 | bytes 1048576 | tf_op jit(solution)/shard_map/pallas_call | solution.py:454
  26.0 3.5 %shard_map.58 = (f32[48,16,128]{2,1,0:T(8,128)S(1)}, f32[128,128]{1,0:T(8,128)}) custom-call(f32[784,128]{1,0:T(8,128)S(1)} %get-tuple-element.20.own, f32[784,128]{1,0:T(8,128)S(1)} %collective-permute-done.other, f32[20,2,8,128]{3,2,1,0:T(8,128)S(1)} %get-tuple-element.23.h_in, f32[20,2,8,128]{3,2,1,0:T(8,128)S(1)} %get-tuple-element.24.u_in, ...), custom_call_target="tpu_custom_call" | custom-call | flops 1048576 | bytes 1048576 | tf_op jit(solution)/shard_map/pallas_call | solution.py:454
  29.5 12.2 %all-to-all-start = ((f32[32,4,128]{2,1,0:T(4,128)}), f32[32,4,128]{2,1,0:T(4,128)S(1)}, u32[]{:S(2)}, u32[]{:S(2)}) async-start(f32[32,4,128]{2,1,0:T(4,128)} %bitcast.3), calls=%async_computation | async-start | bytes 131072 | tf_op jit(solution)/shard_map/all_to_all | solution.py:468
  41.7 7.4 %all-to-all-done = f32[32,4,128]{2,1,0:T(4,128)S(1)} async-done(((f32[32,4,128]{2,1,0:T(4,128)}), f32[32,4,128]{2,1,0:T(4,128)S(1)}, u32[]{:S(2)}, u32[]{:S(2)}) %all-to-all-start) | async-done | bytes 65568 | tf_op jit(solution)/shard_map/all_to_all | solution.py:468
  49.1 27.0 %all_to_all.34 = f32[4,64,128]{2,1,0:T(8,128)S(1)} all-to-all(f32[4,64,128]{2,1,0:T(8,128)S(1)} %bitcast.22), channel_id=1, replica_groups=mesh['zl'=4,'x'=4,'zh'=4,'y'=4,'c'=2] {'zh'}, dimensions={0} | all-to-all | bytes 262144 | tf_op jit(solution)/shard_map/all_to_all | solution.py:468
  76.5 3.7 %collective-permute-start.4 = (f32[96,128]{1,0:T(8,128)S(1)}, f32[96,128]{1,0:T(8,128)S(1)}, u32[]{:S(2)}, u32[]{:S(2)}) collective-permute-start(f32[96,128]{1,0:T(8,128)S(1)} %get-tuple-element.32.total), channel_id=1, source_target_pairs={{0,1},{1,0},{2,3},{3,2},{4,5},{5,4},{6,7},{7,6},{8,9},{9,8},{10,11... | collective-permute-start | bytes 147464 | tf_op jit(solution)/shard_map/ppermute | solution.py:508
  80.2 0.9 collective-permute-done.4.mate
  81.1 0.7 shard_map.60
  81.7 1.3 %collective-permute-start.5 = (f32[96,128]{1,0:T(8,128)S(1)}, f32[96,128]{1,0:T(8,128)S(1)}, u32[]{:S(2)}, u32[]{:S(2)}) collective-permute-start(f32[96,128]{1,0:T(8,128)S(1)} %shard_map.60), channel_id=1, source_target_pairs={{0,128},{128,256},{256,384},{1,129},{129,257},{257,385},{2,130},{1... | collective-permute-start | bytes 147464 | tf_op jit(solution)/shard_map/ppermute | solution.py:511
  83.0 1.9 %collective-permute-start.6 = (f32[96,128]{1,0:T(8,128)S(1)}, f32[96,128]{1,0:T(8,128)S(1)}, u32[]{:S(2)}, u32[]{:S(2)}) collective-permute-start(f32[96,128]{1,0:T(8,128)S(1)} %shard_map.60), channel_id=1, source_target_pairs={{0,256},{128,384},{1,257},{129,385},{2,258},{130,386},{3,259},{131... | collective-permute-start | bytes 147464 | tf_op jit(solution)/shard_map/ppermute | solution.py:511
  84.9 1.3 %collective-permute-start.7 = (f32[96,128]{1,0:T(8,128)S(1)}, f32[96,128]{1,0:T(8,128)S(1)}, u32[]{:S(2)}, u32[]{:S(2)}) collective-permute-start(f32[96,128]{1,0:T(8,128)S(1)} %shard_map.60), channel_id=1, source_target_pairs={{0,384},{1,385},{2,386},{3,387},{4,388},{5,389},{6,390},{7,391},{8... | collective-permute-start | bytes 147464 | tf_op jit(solution)/shard_map/ppermute | solution.py:511
  86.2 1.3 %collective-permute-done.7.three = f32[96,128]{1,0:T(8,128)S(1)} collective-permute-done((f32[96,128]{1,0:T(8,128)S(1)}, f32[96,128]{1,0:T(8,128)S(1)}, u32[]{:S(2)}, u32[]{:S(2)}) %collective-permute-start.7) | collective-permute-done | bytes 49184 | tf_op jit(solution)/shard_map/ppermute | solution.py:511
  87.5 3.9 %shard_map.61 = f32[128,128]{1,0:T(8,128)S(1)} custom-call(f32[96,128]{1,0:T(8,128)S(1)} %collective-permute-done.5.one, f32[96,128]{1,0:T(8,128)S(1)} %collective-permute-done.6.two, f32[96,128]{1,0:T(8,128)S(1)} %collective-permute-done.7.three, f32[96,128]{1,0:T(8,128)S(1)} %collective-permute-done.4.mate, f32[192,128]{1,0:T(8,128)S(1)} %get-tuple-element.34.jumps, ...), custom_call_target="tpu_custom_call" | custom-call | flops 1048576 | bytes 1048576 | tf_op jit(solution)/shard_map/pallas_call | solution.py:454
  91.4 11.1 %all_to_all.35 = f32[32,4,128]{2,1,0:T(4,128)S(1)} all-to-all(f32[32,4,128]{2,1,0:T(4,128)S(1)} %bitcast.13), channel_id=1, replica_groups=mesh['zl'=4,'x'=4,'zh'=4,'y'=4,'c'=2] {'x','y','c'}, dimensions={0} | all-to-all | bytes 131072 | tf_op jit(solution)/shard_map/all_to_all | solution.py:468
  102.5 1.1 %shard_map.62 = f32[768,128]{1,0:T(8,128)} custom-call(f32[48,16,128]{2,1,0:T(8,128)S(1)} %get-tuple-element.29.fine, f32[128,128]{1,0:T(8,128)S(1)} %bitcast.12, f32[16,128]{1,0:T(8,128)S(1)} %get-tuple-element.27.vectors, f32[1,16]{1,0:T(1,128)S(1)} %bitcast.21), custom_call_target="tpu_custom_call" | custom-call | flops 1048576 | bytes 1048576 | tf_op jit(solution)/shard_map/pallas_call | solution.py:454
  (16 shorter events, 0.4 us)
Async XLA Ops:
  0.0 1.0 copy-start
  1.0 0.7 copy-start.3
  2.2 12.7 %copy-start.1 = (f32[16,16]{1,0:T(8,128)S(1)}, f32[16,16]{1,0:T(8,128)}, u32[]{:S(2)}) copy-start(f32[16,16]{1,0:T(8,128)} %coupling.5) | copy-start | bytes 3076
  2.2 23.8 %collective-permute-start = (f32[784,128]{1,0:T(8,128)S(1)}, f32[784,128]{1,0:T(8,128)S(1)}, u32[]{:S(2)}, u32[]{:S(2)}) collective-permute-start(f32[784,128]{1,0:T(8,128)S(1)} %get-tuple-element.20.own), channel_id=1, source_target_pairs={{1,2},{3,4},{5,6},{7,8},{9,10},{11,12},{13,14},{15,16},{17,18},{19... | collective-permute-start | bytes 1204232 | tf_op jit(solution)/shard_map/ppermute | solution.py:482
  6.8 15.9 %collective-permute-start.1 = (f32[512,128]{1,0:T(8,128)S(1)}, f32[512,128]{1,0:T(8,128)S(1)}, u32[]{:S(2)}, u32[]{:S(2)}) collective-permute-start(f32[512,128]{1,0:T(8,128)S(1)} %get-tuple-element.21), channel_id=1, source_target_pairs={{0,1},{1,0},{2,3},{3,2},{4,5},{5,4},{6,7},{7,6},{8,9},{9,8},{10,11... | collective-permute-start | bytes 786440 | tf_op jit(solution)/shard_map/ppermute | solution.py:488
  11.7 11.0 %collective-permute-start.2 = (f32[272,128]{1,0:T(8,128)S(1)}, f32[272,128]{1,0:T(8,128)S(1)}, u32[]{:S(2)}, u32[]{:S(2)}) collective-permute-start(f32[272,128]{1,0:T(8,128)S(1)} %get-tuple-element.22), channel_id=1, source_target_pairs={{0,1},{1,0},{2,3},{3,2},{4,5},{5,4},{6,7},{7,6},{8,9},{9,8},{10,11... | collective-permute-start | bytes 417800 | tf_op jit(solution)/shard_map/ppermute | solution.py:488
  13.6 1.3 %copy-start.4 = (f32[16]{0:T(128)S(1)}, f32[16]{0:T(128)}, u32[]{:S(2)}) copy-start(f32[16]{0:T(128)} %param.9) | copy-start | bytes 196
  13.6 12.3 %collective-permute-start.3 = (f32[48,128]{1,0:T(8,128)S(1)}, f32[48,128]{1,0:T(8,128)S(1)}, u32[]{:S(2)}, u32[]{:S(2)}) collective-permute-start(f32[48,128]{1,0:T(8,128)S(1)} %get-tuple-element.28), channel_id=1, source_target_pairs={{32,0},{64,32},{96,64},{128,96},{160,128},{192,160},{224,192},{256... | collective-permute-start | bytes 73736 | tf_op jit(solution)/shard_map/ppermute | solution.py:483
  22.7 0.7 copy-start.2
  29.5 19.5 %all-to-all-start = ((f32[32,4,128]{2,1,0:T(4,128)}), f32[32,4,128]{2,1,0:T(4,128)S(1)}, u32[]{:S(2)}, u32[]{:S(2)}) async-start(f32[32,4,128]{2,1,0:T(4,128)} %bitcast.3), calls=%async_computation | async-start | bytes 131072 | tf_op jit(solution)/shard_map/all_to_all | solution.py:468
  76.5 4.6 %collective-permute-start.4 = (f32[96,128]{1,0:T(8,128)S(1)}, f32[96,128]{1,0:T(8,128)S(1)}, u32[]{:S(2)}, u32[]{:S(2)}) collective-permute-start(f32[96,128]{1,0:T(8,128)S(1)} %get-tuple-element.32.total), channel_id=1, source_target_pairs={{0,1},{1,0},{2,3},{3,2},{4,5},{5,4},{6,7},{7,6},{8,9},{9,8},{10,11... | collective-permute-start | bytes 147464 | tf_op jit(solution)/shard_map/ppermute | solution.py:508
  81.7 4.5 %collective-permute-start.5 = (f32[96,128]{1,0:T(8,128)S(1)}, f32[96,128]{1,0:T(8,128)S(1)}, u32[]{:S(2)}, u32[]{:S(2)}) collective-permute-start(f32[96,128]{1,0:T(8,128)S(1)} %shard_map.60), channel_id=1, source_target_pairs={{0,128},{128,256},{256,384},{1,129},{129,257},{257,385},{2,130},{1... | collective-permute-start | bytes 147464 | tf_op jit(solution)/shard_map/ppermute | solution.py:511
  83.0 3.2 %collective-permute-start.6 = (f32[96,128]{1,0:T(8,128)S(1)}, f32[96,128]{1,0:T(8,128)S(1)}, u32[]{:S(2)}, u32[]{:S(2)}) collective-permute-start(f32[96,128]{1,0:T(8,128)S(1)} %shard_map.60), channel_id=1, source_target_pairs={{0,256},{128,384},{1,257},{129,385},{2,258},{130,386},{3,259},{131... | collective-permute-start | bytes 147464 | tf_op jit(solution)/shard_map/ppermute | solution.py:511
  84.9 2.6 %collective-permute-start.7 = (f32[96,128]{1,0:T(8,128)S(1)}, f32[96,128]{1,0:T(8,128)S(1)}, u32[]{:S(2)}, u32[]{:S(2)}) collective-permute-start(f32[96,128]{1,0:T(8,128)S(1)} %shard_map.60), channel_id=1, source_target_pairs={{0,384},{1,385},{2,386},{3,387},{4,388},{5,389},{6,390},{7,391},{8... | collective-permute-start | bytes 147464 | tf_op jit(solution)/shard_map/ppermute | solution.py:511

commit v3 on v2

--- a/solution.py
+++ b/solution.py
@@ -56,22 +56,42 @@
     return pairs(pairs(rows[0], rows[1], 1), pairs(rows[2], rows[3], 1), 2) * (1.0 / 16.0)
 
 
-def pack_kernel(state, mask, packed, first, rest, restricted, rows, sems):
+VELOCITY_AT = (0, LAYERS * BAND, LAYERS * (2 * BAND - 1))
+MASK_AT = LAYERS * (3 * BAND - 2)
+
+
+def pack_kernel(state, mask, sent, first, rest, restricted, rows, sems):
     copies = [
-        pltpu.make_async_copy(state, packed.at[pl.ds(0, MASK)], sems.at[0]),
-        pltpu.make_async_copy(mask, rows, sems.at[1]),
+        pltpu.make_async_copy(state.at[pl.ds(0, CUT)], first, sems.at[0]),
+        pltpu.make_async_copy(state.at[pl.ds(CUT, MASK - CUT)], rest.at[pl.ds(0, MASK - CUT)], sems.at[1]),
+        pltpu.make_async_copy(mask, rows, sems.at[2]),
     ]
     for copy in copies:
         copy.start()
     for copy in copies:
         copy.wait()
-    packed[MASK:, :] = rows[...].astype(F32)
-    first[...] = packed[:CUT, :]
-    rest[...] = packed[CUT:, :]
+    rest[MASK - CUT :, :] = rows[...].astype(F32)
+
+    def row_of(f, r):
+        if f < 2:
+            return first[pl.ds(f * 256 + r, LAYERS, stride=BAND), :]
+        return rest[pl.ds(r, LAYERS, stride=BAND), :]
+
+    for odd in (False, True):
+
+        @pl.when(core_index() == int(odd))
+        def _():
+            for k in range(BAND):
+                r = BAND - 1 - k if odd else k
+                for f in range(3 if k < BAND - 1 else 1):
+                    at = VELOCITY_AT[f] + LAYERS * k
+                    sent[at : at + LAYERS, :] = row_of(f, r)
+                sent[MASK_AT + k : MASK_AT + k + 1, :] = rest[MASK - CUT + r : MASK - CUT + r + 1, :]
+
     for f in range(3):
         rows = []
         for cr in range(4):
-            here = [packed[pl.ds(f * 256 + 4 * cr + r, LAYERS, stride=BAND), :] for r in range(4)]
+            here = [row_of(f, 4 * cr + r) for r in range(4)]
             rows.append(here[0] + here[1] + here[2] + here[3])
         restricted[f * LAYERS : (f + 1) * LAYERS, :] = block_mean(rows)
 
@@ -202,7 +222,7 @@
     return lax.axis_index("x") * 4 + lax.axis_index("y")
 
 
-def put_band(fields, ms, begin, blocks, cut, core, sign):
+def put_band(fields, ms, begin, blocks, core, sign):
     for odd in (False, True):
 
         @pl.when(core == int(odd))
@@ -210,10 +230,10 @@
             for r in range(BAND):
                 row = begin + (BAND - 1 - r if odd else r)
                 for f in range(3):
-                    at = f * 256 + r - (cut if f == 2 else 0)
+                    at = f * 256 + r - (CUT if f == 2 else 0)
                     value = blocks[f // 2][pl.ds(at, LAYERS, stride=BAND), :].reshape(2, 8, ZONAL)
                     fields[f][row] = sign * value if f == 2 else value
-                at = MASK - cut + r
+                at = MASK - CUT + r
                 ms[row] = jnp.broadcast_to(blocks[1][at : at + 1, :], (8, ZONAL))
 
 
@@ -229,13 +249,13 @@
 
 
 def inner_kernel(
-    own, mate_first, mate_rest, fold, coupling, depths, h_out, u_out, v_out, fold_out, hs, us, vs, ps, ms, fs
+    own_first, own_rest, mate_first, mate_rest, fold, coupling, depths, h_out, u_out, v_out, fold_out, hs, us, vs, ps, ms, fs
 ):
     core = core_index()
     sign = (1 - 2 * core).astype(F32)
     fields = (hs, us, vs)
-    put_band(fields, ms, HALO, (own, own), 0, core, sign)
-    put_band(fields, ms, HALO + BAND, (mate_first, mate_rest), CUT, core, sign)
+    put_band(fields, ms, HALO, (own_first, own_rest), core, sign)
+    put_band(fields, ms, HALO + BAND, (mate_first, mate_rest), core, sign)
     coriolis_table(fs, band_index(), core, sign)
     steps = fine_tools(fields, ps, ms, fs, coupling, depths)
     ends = [SPAN - 2 * t for t in range(FINE_STEPS)]
@@ -246,7 +266,7 @@
 
 
 def outer_kernel(
-    own, other, h_in, u_in, v_in, fold, coupling, depths, vectors, following,
+    own_first, own_rest, other, h_in, u_in, v_in, fold, coupling, depths, vectors, following,
     fine, chunk, hs, us, vs, ps, ms, fs,
 ):
     position = band_index()
@@ -258,21 +278,27 @@
         field[HALO : HALO + KEPT] = kept[...]
     for r in range(BAND):
         row = HALO + r + core * (BAND - 1 - 2 * r)
-        ms[row] = jnp.broadcast_to(own[MASK + r : MASK + r + 1, :], (8, ZONAL))
+        ms[row] = jnp.broadcast_to(own_rest[MASK - CUT + r : MASK - CUT + r + 1, :], (8, ZONAL))
 
     @pl.when(jnp.logical_not(on_top))
     def _():
-        put_band(fields, ms, 0, (other, other), 0, core, sign)
+        for k in range(BAND):
+            for f in range(3 if k < BAND - 1 else 1):
+                at = VELOCITY_AT[f] + LAYERS * k
+                value = other[at : at + LAYERS, :].reshape(2, 8, ZONAL)
+                fields[f][BAND - 1 - k] = sign * value if f == 2 else value
+            ms[BAND - 1 - k] = jnp.broadcast_to(other[MASK_AT + k : MASK_AT + k + 1, :], (8, ZONAL))
 
     @pl.when(on_top)
     def _():
         index = jnp.broadcast_to(fold[...].astype(jnp.int32), (LAYERS, ZONAL))
         for r in range(BAND):
             for f in range(3):
-                image = own[pl.ds(f * 256 + r, LAYERS, stride=BAND), :]
+                block, at = (own_first, f * 256 + r) if f < 2 else (own_rest, r)
+                image = block[pl.ds(at, LAYERS, stride=BAND), :]
                 image = jnp.take_along_axis(image, index, axis=1).reshape(2, 8, ZONAL)
                 fields[f][r] = -image if f == 1 else image
-            image = jnp.broadcast_to(own[MASK + r : MASK + r + 1, :], (8, ZONAL))
+            image = jnp.broadcast_to(own_rest[MASK - CUT + r : MASK - CUT + r + 1, :], (8, ZONAL))
             ms[r] = jnp.take_along_axis(image, index[:8], axis=1)
 
     coriolis_table(fs, position, core, sign)
@@ -364,24 +390,32 @@
     return [ref[cr * 8 : cr * 8 + 8, :] for cr in range(4)]
 
 
-def pair_kernel(gathered, values, fold, jumps, mask_out, total):
-    lane = iota((8, ZONAL), 1)
-    seg = lane % 4
-    for x in range(2):
-        for f in range(4 if x == 0 else 3):
-            rows = [None] * 4
-            for zh in range(4):
-                piece = gathered[pl.ds(zh * 64 + x * 32 + f, 8, stride=4), :]
-                for cr in range(4):
-                    shift = (zh - cr) % ZONAL
-                    moved = pltpu.roll(piece, shift, 1) if shift else piece
-                    rows[cr] = moved if zh == 0 else jnp.where(seg == zh, moved, rows[cr])
+PARTS = 7
+
+
+def collect_kernel(spread, out):
+    for part in range(PARTS):
+        at = core_index() * 64 + part + (1 if part > 3 else 0) * 28
+        out[part * 8 : part * 8 + 8, :] = spread[pl.ds(at, 8, stride=4), :]
+
+
+def pair_kernel(half, other_half, values, fold, jumps, mask_out, total):
+    seg = iota((8, ZONAL), 1) % 4
+    zh = lax.axis_index("zh")
+    quarters = [(half, 0, zh), (half, PARTS * 8, zh ^ 1), (other_half, 0, zh ^ 3), (other_half, PARTS * 8, zh ^ 2)]
+    for part in range(PARTS):
+        rows = [None] * 4
+        for ref, begin, quarter in quarters:
+            piece = ref[begin + part * 8 : begin + part * 8 + 8, :]
             for cr in range(4):
-                if f == 3:
-                    mask_out[cr * 8 : cr * 8 + 8, :] = rows[cr]
-                else:
-                    begin = x * 96 + f * 32 + cr * 8
-                    jumps[begin : begin + 8, :] = rows[cr]
+                moved = pltpu.roll(piece, lax.rem(quarter - cr + ZONAL, ZONAL), 1)
+                rows[cr] = moved if rows[cr] is None else jnp.where(seg == quarter, moved, rows[cr])
+        for cr in range(4):
+            if part == 3:
+                mask_out[cr * 8 : cr * 8 + 8, :] = rows[cr]
+            else:
+                begin = (part if part < 3 else part - 1) * 32 + cr * 8
+                jumps[begin : begin + 8, :] = rows[cr]
     propagate = coarse_tools(values[pl.ds(mode_index(), 1), :], load_masks(mask_out), fold)
     store_state(total, add_state(propagate(load_state(jumps)), load_state(jumps, 96)))
 
@@ -395,7 +429,13 @@
     store_state(both, add_state(propagate(propagate(earlier)), later))
 
 
-def chain_kernel(one, two, three, mate, jumps, mask, values, fold, chunk):
+def earlier_kernel(two, three, mask, values, fold, out):
+    propagate = coarse_tools(values[pl.ds(mode_index(), 1), :], load_masks(mask), fold)
+    state = lax.fori_loop(0, 2, lambda _, s: propagate(propagate(s)), load_state(three))
+    store_state(out, add_state(state, load_state(two)))
+
+
+def chain_kernel(one, earlier, mate, jumps, mask, values, fold, chunk):
     quarter = lax.axis_index("zh")
     core = core_index()
     propagate = coarse_tools(values[pl.ds(mode_index(), 1), :], load_masks(mask), fold)
@@ -403,10 +443,8 @@
     def twice(state):
         return propagate(propagate(state))
 
-    state = load_state(three)
-    for ref in (two, one):
-        state = lax.fori_loop(0, 2, lambda _, s: twice(s), state)
-        state = add_state(state, load_state(ref))
+    state = lax.fori_loop(0, 2, lambda _, s: twice(s), load_state(earlier))
+    state = add_state(state, load_state(one))
     state = lax.fori_loop(0, core, lambda _, s: add_state(twice(s), load_state(mate)), state)
     seg = iota((8, ZONAL), 1) % 4
     chunk[...] = jnp.zeros_like(chunk)
@@ -469,17 +507,17 @@
 
 
 def body(start_state, land_mask, fold_map, coupling, depths):
-    own, first, rest, restricted = call(
+    sent, first, rest, restricted = call(
         pack_kernel,
-        [(MASK + BAND, ZONAL), (CUT, ZONAL), (MASK + BAND - CUT, ZONAL), (3 * LAYERS, ZONAL)],
-        [pltpu.VMEM((BAND, ZONAL), jnp.int32), pltpu.SemaphoreType.DMA((2,))],
+        [(MASK_AT + BAND, ZONAL), (CUT, ZONAL), (MASK + BAND - CUT, ZONAL), (3 * LAYERS, ZONAL)],
+        [pltpu.VMEM((BAND, ZONAL), jnp.int32), pltpu.SemaphoreType.DMA((3,))],
         spaces=(pl.ANY, pl.ANY),
     )(start_state.reshape(MASK, ZONAL), land_mask)
     fold = fold_map.reshape(1, ZONAL)
     depth_row = depths.reshape(1, LAYERS)
     across = [(i, i + 1) for i in range(1, BANDS - 1, 2)]
     across += [(b, a) for a, b in across]
-    other = lax.ppermute(own, SPACE, across)
+    other = lax.ppermute(sent, SPACE, across)
     following = lax.ppermute(restricted, TIME, [(n + 1, n) for n in range(15)])
     vectors, values = call(modes_kernel, [(LAYERS, ZONAL), (LAYERS, ZONAL)], flops=10 << 20)(
         coupling, depth_row
@@ -492,26 +530,29 @@
     scratch = [state, state, state, state, table, table]
     *inner, fold_held = call(
         inner_kernel, [(KEPT, 2, 8, ZONAL)] * 3 + [(1, ZONAL)], scratch, flops=4 << 20
-    )(own, *mate, fold, coupling, depth_row)
+    )(first, rest, *mate, fold, coupling, depth_row)
     fine, chunk = call(
         outer_kernel, [(3 * BAND, LAYERS, ZONAL), (4 * BANDS, ZONAL)], scratch
     )(
-        own, other, *inner, fold_held, coupling, depth_row, vectors, following
+        first, rest, other, *inner, fold_held, coupling, depth_row, vectors, following
     )
 
     spread = swap(chunk, PLANE)
-    mine = lax.dynamic_slice_in_dim(spread, lax.axis_index("c") * 64, 64, 0)
-    grid = swap(jnp.concatenate([mine] * 4, axis=0), ("zh",))
+    (mine,) = call(collect_kernel, [(PARTS * 8, ZONAL)])(spread)
+    beside = lax.ppermute(mine, ("zh",), [(i, i ^ 1) for i in range(4)])
+    half = jnp.concatenate([mine, beside], axis=0)
+    other_half = lax.ppermute(half, ("zh",), [(i, i ^ 3) for i in range(4)])
     jumps, mask, total = call(
         pair_kernel, [(192, ZONAL), (32, ZONAL), (96, ZONAL)]
-    )(grid, values, fold)
+    )(half, other_half, values, fold)
     mate = lax.ppermute(total, ("c",), [(0, 1), (1, 0)])
     (both,) = call(group_kernel, [(96, ZONAL)])(total, mate, mask, values, fold)
-    one, two, three = (
-        lax.ppermute(both, ("zl",), [(i, i + d) for i in range(4 - d)]) for d in (1, 2, 3)
+    three, two, one = (
+        lax.ppermute(both, ("zl",), [(i, i + d) for i in range(4 - d)]) for d in (3, 2, 1)
     )
+    (earlier,) = call(earlier_kernel, [(96, ZONAL)])(two, three, mask, values, fold)
     (chunk,) = call(chain_kernel, [(4 * BANDS, ZONAL)])(
-        one, two, three, mate, jumps, mask, values, fold
+        one, earlier, mate, jumps, mask, values, fold
     )
     change = swap(chunk, PLANE)
     (result,) = call(

time: 104 us -> 101 us (0.971)
  starting transfers between devices: 33 us -> 42.7 us
  blocking collectives: 38.1 us -> 29.7 us
  waiting for transfers between devices: 9.55 us -> 5.32 us
    ppermute x1 -> x3, starting transfers between devices: 4.59 us -> 21 us  [the longest x1 8.81 us: body(): beside = lax.ppermute(mine, ('zh',), [(i, i ^ 1) for i in range(4)])]
    all_to_all x1 -> x0, starting transfers between devices: 12.2 us -> none  [swap(): return lax.all_to_all(block, axes, 0, 0, tiled=True)]
    all_to_all x2, blocking collectives: 38.1 us -> 29.7 us  [swap(): return lax.all_to_all(block, axes, 0, 0, tiled=True)]
    all_to_all x1 -> x0, waiting for transfers between devices: 7.36 us -> none  [swap(): return lax.all_to_all(block, axes, 0, 0, tiled=True)]
    ppermute x1 -> x3, waiting for transfers between devices: 0.01 us -> 4.44 us  [the longest x1 2.5 us: body(): beside = lax.ppermute(mine, ('zh',), [(i, i ^ 1) for i in range(4)])]
    ppermute x3, starting transfers between devices: 4.44 us -> 8.69 us  [body(): lax.ppermute(both, ('zl',), [(i, i + d) for i in range(4 - d)])]
    ppermute x3, waiting for transfers between devices: 1.31 us -> 0.01 us  [body(): lax.ppermute(both, ('zl',), [(i, i + d) for i in range(4 - d)])]
    ppermute x1, starting transfers between devices: 3.73 us -> 4.94 us  [body(): mate = lax.ppermute(total, ('c',), [(0, 1), (1, 0)])]
  transfers between devices with their start and end apart: 9 -> 10, of which waited for: 3 -> 3; matrix products, arithmetic and copies ran while one was open for 0% -> 0% of each run, Pallas kernels for 10% -> 12%
where the time goes in v3:
time: 101 us; the launch traced here: 100 us
  starting transfers between devices  42.7 us (42%)
  blocking collectives  29.7 us (29%)
  Pallas kernels  19.8 us (20%)
  waiting for transfers between devices  5.32 us (5%)
  local copies, waits for them, and re-layouts  2.35 us (2%)
    all_to_all x2, blocking collectives, swap(): return lax.all_to_all(block, axes, 0, 0, tiled=True)  29.7 us
    pallas_call x10, Pallas kernels, run(): pl.pallas_call(kernel, out_shape=[jax.ShapeDtypeStruct(s, F32) for s in o...  19.8 us
    ppermute x1, starting transfers between devices, body(): beside = lax.ppermute(mine, ('zh',), [(i, i ^ 1) for i in range(4)])  8.81 us
    ppermute x3, starting transfers between devices, body(): lax.ppermute(both, ('zl',), [(i, i + d) for i in range(4 - d)])  8.69 us
    ppermute x1, starting transfers between devices, body(): other_half = lax.ppermute(half, ('zh',), [(i, i ^ 3) for i in range(4)])  7.55 us
    ppermute x2, starting transfers between devices, body(): mate = [lax.ppermute(part, SPACE, inside) for part in (first, rest)]  6.8 us
    ppermute x1, starting transfers between devices, body(): mate = lax.ppermute(total, ('c',), [(0, 1), (1, 0)])  4.94 us
    ppermute x1, starting transfers between devices, body(): other = lax.ppermute(sent, SPACE, across)  4.59 us
  transfers between devices with their start and end apart: 10, of which 3 were waited for; matrix products, arithmetic and copies ran while one was open for 0% of the time, Pallas kernels for 12%

profile of v3, /device:TPU:1, one launch (start us, length us, event | category | flops | bytes accessed | tf_op | source)
XLA Modules:
  0.0 100.1 jit_solution(13135145023496399883)
XLA Ops:
  0.0 1.0 copy-done
  1.0 0.7 copy-done.3
  2.3 4.6 %collective-permute-start = (f32[752,128]{1,0:T(8,128)S(1)}, f32[752,128]{1,0:T(8,128)S(1)}, u32[]{:S(2)}, u32[]{:S(2)}) collective-permute-start(f32[752,128]{1,0:T(8,128)S(1)} %get-tuple-element.22), channel_id=1, source_target_pairs={{1,2},{3,4},{5,6},{7,8},{9,10},{11,12},{13,14},{15,16},{17,18},{19... | collective-permute-start | bytes 1155080 | tf_op jit(solution)/shard_map/ppermute | solution.py:520
  6.9 4.9 %collective-permute-start.1 = (f32[512,128]{1,0:T(8,128)S(1)}, f32[512,128]{1,0:T(8,128)S(1)}, u32[]{:S(2)}, u32[]{:S(2)}) collective-permute-start(f32[512,128]{1,0:T(8,128)S(1)} %get-tuple-element.20.own_first), channel_id=1, source_target_pairs={{0,1},{1,0},{2,3},{3,2},{4,5},{5,4},{6,7},{7,6},{8,9},{9,8},{10,11... | collective-permute-start | bytes 786440 | tf_op jit(solution)/shard_map/ppermute | solution.py:526
  11.8 1.9 %collective-permute-start.2 = (f32[272,128]{1,0:T(8,128)S(1)}, f32[272,128]{1,0:T(8,128)S(1)}, u32[]{:S(2)}, u32[]{:S(2)}) collective-permute-start(f32[272,128]{1,0:T(8,128)S(1)} %get-tuple-element.21.own_rest), channel_id=1, source_target_pairs={{0,1},{1,0},{2,3},{3,2},{4,5},{5,4},{6,7},{7,6},{8,9},{9,8},{10,11... | collective-permute-start | bytes 417800 | tf_op jit(solution)/shard_map/ppermute | solution.py:526
  13.7 1.3 %collective-permute-start.3 = (f32[48,128]{1,0:T(8,128)S(1)}, f32[48,128]{1,0:T(8,128)S(1)}, u32[]{:S(2)}, u32[]{:S(2)}) collective-permute-start(f32[48,128]{1,0:T(8,128)S(1)} %get-tuple-element.28), channel_id=1, source_target_pairs={{32,0},{64,32},{96,64},{128,96},{160,128},{192,160},{224,192},{256... | collective-permute-start | bytes 73736 | tf_op jit(solution)/shard_map/ppermute | solution.py:521
  15.1 7.7 %shard_map.57 = (f32[16,128]{1,0:T(8,128)S(1)}, f32[16,128]{1,0:T(8,128)S(1)}) custom-call(f32[16,16]{1,0:T(8,128)S(1)} %copy-done.1, f32[1,16]{1,0:T(1,128)S(1)} %bitcast.18), custom_call_target="tpu_custom_call" | custom-call | flops 10485760 | bytes 1048576 | tf_op jit(solution)/shard_map/pallas_call | solution.py:492
  23.5 2.6 %shard_map.56 = (f32[20,2,8,128]{3,2,1,0:T(8,128)S(1)}, f32[20,2,8,128]{3,2,1,0:T(8,128)S(1)}, f32[20,2,8,128]{3,2,1,0:T(8,128)S(1)}, f32[1,128]{1,0:T(1,128)S(1)}) custom-call(f32[512,128]{1,0:T(8,128)S(1)} %get-tuple-element.20.own_first, f32[272,128]{1,0:T(8,128)S(1)} %get-tuple-element.21.own_rest, f32[512,128]{1,0:T(8,128)S(1)} %collective-permute-done.1.mate_first, ...), custom_call_target="tpu_custom_call" | custom-call | flops 4194304 | bytes 1048576 | tf_op jit(solution)/shard_map/pallas_call | solution.py:492
  26.1 2.8 %shard_map.58 = (f32[48,16,128]{2,1,0:T(8,128)S(1)}, f32[128,128]{1,0:T(8,128)S(1)}) custom-call(f32[512,128]{1,0:T(8,128)S(1)} %get-tuple-element.20.own_first, f32[272,128]{1,0:T(8,128)S(1)} %get-tuple-element.21.own_rest, f32[752,128]{1,0:T(8,128)S(1)} %collective-permute-done.other, f32[20,2,8,128]{3,2,1,0:T(8,128)S(1)} %get-tuple-element.23.h_in, ...), custom_call_target="tpu_custom_call" | custom-call | flops 1048576 | bytes 1048576 | tf_op jit(solution)/shard_map/pallas_call | solution.py:492
  28.9 18.6 %all_to_all.22 = f32[32,4,128]{2,1,0:T(4,128)S(1)} all-to-all(f32[32,4,128]{2,1,0:T(4,128)S(1)} %bitcast.12), channel_id=1, replica_groups=mesh['zl'=4,'x'=4,'zh'=4,'y'=4,'c'=2] {'x','y','c'}, dimensions={0} | all-to-all | bytes 131072 | tf_op jit(solution)/shard_map/all_to_all | solution.py:506
  47.5 8.8 %collective-permute-start.4 = (f32[56,128]{1,0:T(8,128)S(1)}, f32[56,128]{1,0:T(8,128)S(1)}, u32[]{:S(2)}, u32[]{:S(2)}) collective-permute-start(f32[56,128]{1,0:T(8,128)S(1)} %shard_map.59), channel_id=1, source_target_pairs={{0,8},{8,0},{16,24},{24,16},{1,9},{9,1},{17,25},{25,17},{2,10},{10... | collective-permute-start | bytes 86024 | tf_op jit(solution)/shard_map/ppermute | solution.py:542
  56.3 2.5 %collective-permute-done.4 = f32[56,128]{1,0:T(8,128)S(1)} collective-permute-done((f32[56,128]{1,0:T(8,128)S(1)}, f32[56,128]{1,0:T(8,128)S(1)}, u32[]{:S(2)}, u32[]{:S(2)}) %collective-permute-start.4) | collective-permute-done | bytes 28704 | tf_op jit(solution)/shard_map/ppermute | solution.py:542
  58.9 7.6 %collective-permute-start.5 = (f32[112,128]{1,0:T(8,128)S(1)}, f32[112,128]{1,0:T(8,128)S(1)}, u32[]{:S(2)}, u32[]{:S(2)}) collective-permute-start(f32[112,128]{1,0:T(8,128)S(1)} %pad_maximum_fusion.half), channel_id=1, source_target_pairs={{0,24},{8,16},{16,8},{24,0},{1,25},{9,17},{17,9},{25,1},{2,26},{10... | collective-permute-start | bytes 172040 | tf_op jit(solution)/shard_map/ppermute | solution.py:544
  66.4 1.9 %collective-permute-done.5.other_half = f32[112,128]{1,0:T(8,128)S(1)} collective-permute-done((f32[112,128]{1,0:T(8,128)S(1)}, f32[112,128]{1,0:T(8,128)S(1)}, u32[]{:S(2)}, u32[]{:S(2)}) %collective-permute-start.5) | collective-permute-done | bytes 57376 | tf_op jit(solution)/shard_map/ppermute | solution.py:544
  68.8 4.9 %collective-permute-start.6 = (f32[96,128]{1,0:T(8,128)S(1)}, f32[96,128]{1,0:T(8,128)S(1)}, u32[]{:S(2)}, u32[]{:S(2)}) collective-permute-start(f32[96,128]{1,0:T(8,128)S(1)} %get-tuple-element.32.total), channel_id=1, source_target_pairs={{0,1},{1,0},{2,3},{3,2},{4,5},{5,4},{6,7},{7,6},{8,9},{9,8},{10,11... | collective-permute-start | bytes 147464 | tf_op jit(solution)/shard_map/ppermute | solution.py:548
  73.7 0.9 collective-permute-done.6.mate
  74.6 0.7 shard_map.61
  75.3 5.2 %collective-permute-start.9 = (f32[96,128]{1,0:T(8,128)S(1)}, f32[96,128]{1,0:T(8,128)S(1)}, u32[]{:S(2)}, u32[]{:S(2)}) collective-permute-start(f32[96,128]{1,0:T(8,128)S(1)} %shard_map.61), channel_id=1, source_target_pairs={{0,384},{1,385},{2,386},{3,387},{4,388},{5,389},{6,390},{7,391},{8... | collective-permute-start | bytes 147464 | tf_op jit(solution)/shard_map/ppermute | solution.py:551
  80.5 1.3 %collective-permute-start.8 = (f32[96,128]{1,0:T(8,128)S(1)}, f32[96,128]{1,0:T(8,128)S(1)}, u32[]{:S(2)}, u32[]{:S(2)}) collective-permute-start(f32[96,128]{1,0:T(8,128)S(1)} %shard_map.61), channel_id=1, source_target_pairs={{0,256},{128,384},{1,257},{129,385},{2,258},{130,386},{3,259},{131... | collective-permute-start | bytes 147464 | tf_op jit(solution)/shard_map/ppermute | solution.py:551
  81.8 2.2 %collective-permute-start.7 = (f32[96,128]{1,0:T(8,128)S(1)}, f32[96,128]{1,0:T(8,128)S(1)}, u32[]{:S(2)}, u32[]{:S(2)}) collective-permute-start(f32[96,128]{1,0:T(8,128)S(1)} %shard_map.61), channel_id=1, source_target_pairs={{0,128},{128,256},{256,384},{1,129},{129,257},{257,385},{2,130},{1... | collective-permute-start | bytes 147464 | tf_op jit(solution)/shard_map/ppermute | solution.py:551
  84.0 1.3 %shard_map.62.earlier = f32[96,128]{1,0:T(8,128)S(1)} custom-call(f32[96,128]{1,0:T(8,128)S(1)} %collective-permute-done.8.two, f32[96,128]{1,0:T(8,128)S(1)} %collective-permute-done.9.three, f32[32,128]{1,0:T(8,128)S(1)} %get-tuple-element.33.mask, f32[16,128]{1,0:T(8,128)S(1)} %get-tuple-element.31.values, s32[1,128]{1,0:T(1,128)S(1)} %bitcast.16), custom_call_target="tpu_custom_call" | custom-call | flops 1048576 | bytes 1048576 | tf_op jit(solution)/shard_map/pallas_call | solution.py:492
  85.3 2.6 %shard_map.63 = f32[128,128]{1,0:T(8,128)S(1)} custom-call(f32[96,128]{1,0:T(8,128)S(1)} %collective-permute-done.7.one, f32[96,128]{1,0:T(8,128)S(1)} %shard_map.62.earlier, f32[96,128]{1,0:T(8,128)S(1)} %collective-permute-done.6.mate, f32[192,128]{1,0:T(8,128)S(1)} %get-tuple-element.34.jumps, f32[32,128]{1,0:T(8,128)S(1)} %get-tuple-element.33.mask, ...), custom_call_target="tpu_custom_call" | custom-call | flops 1048576 | bytes 1048576 | tf_op jit(solution)/shard_map/pallas_call | solution.py:492
  87.9 11.0 %all_to_all.23 = f32[32,4,128]{2,1,0:T(4,128)S(1)} all-to-all(f32[32,4,128]{2,1,0:T(4,128)S(1)} %bitcast.11), channel_id=1, replica_groups=mesh['zl'=4,'x'=4,'zh'=4,'y'=4,'c'=2] {'x','y','c'}, dimensions={0} | all-to-all | bytes 131072 | tf_op jit(solution)/shard_map/all_to_all | solution.py:506
  99.0 1.1 %shard_map.64 = f32[768,128]{1,0:T(8,128)} custom-call(f32[48,16,128]{2,1,0:T(8,128)S(1)} %get-tuple-element.29.fine, f32[128,128]{1,0:T(8,128)S(1)} %bitcast.9, f32[16,128]{1,0:T(8,128)S(1)} %get-tuple-element.27.vectors, f32[1,16]{1,0:T(1,128)S(1)} %bitcast.21), custom_call_target="tpu_custom_call" | custom-call | flops 1048576 | bytes 1048576 | tf_op jit(solution)/shard_map/pallas_call | solution.py:492
  (19 shorter events, 1.7 us)
Async XLA Ops:
  0.0 1.0 copy-start
  1.0 0.7 copy-start.3
  2.3 12.7 %copy-start.1 = (f32[16,16]{1,0:T(8,128)S(1)}, f32[16,16]{1,0:T(8,128)}, u32[]{:S(2)}) copy-start(f32[16,16]{1,0:T(8,128)} %coupling.5) | copy-start | bytes 3076
  2.3 23.8 %collective-permute-start = (f32[752,128]{1,0:T(8,128)S(1)}, f32[752,128]{1,0:T(8,128)S(1)}, u32[]{:S(2)}, u32[]{:S(2)}) collective-permute-start(f32[752,128]{1,0:T(8,128)S(1)} %get-tuple-element.22), channel_id=1, source_target_pairs={{1,2},{3,4},{5,6},{7,8},{9,10},{11,12},{13,14},{15,16},{17,18},{19... | collective-permute-start | bytes 1155080 | tf_op jit(solution)/shard_map/ppermute | solution.py:520
  6.9 15.9 %collective-permute-start.1 = (f32[512,128]{1,0:T(8,128)S(1)}, f32[512,128]{1,0:T(8,128)S(1)}, u32[]{:S(2)}, u32[]{:S(2)}) collective-permute-start(f32[512,128]{1,0:T(8,128)S(1)} %get-tuple-element.20.own_first), channel_id=1, source_target_pairs={{0,1},{1,0},{2,3},{3,2},{4,5},{5,4},{6,7},{7,6},{8,9},{9,8},{10,11... | collective-permute-start | bytes 786440 | tf_op jit(solution)/shard_map/ppermute | solution.py:526
  11.8 11.0 %collective-permute-start.2 = (f32[272,128]{1,0:T(8,128)S(1)}, f32[272,128]{1,0:T(8,128)S(1)}, u32[]{:S(2)}, u32[]{:S(2)}) collective-permute-start(f32[272,128]{1,0:T(8,128)S(1)} %get-tuple-element.21.own_rest), channel_id=1, source_target_pairs={{0,1},{1,0},{2,3},{3,2},{4,5},{5,4},{6,7},{7,6},{8,9},{9,8},{10,11... | collective-permute-start | bytes 417800 | tf_op jit(solution)/shard_map/ppermute | solution.py:526
  13.7 1.3 %copy-start.4 = (f32[16]{0:T(128)S(1)}, f32[16]{0:T(128)}, u32[]{:S(2)}) copy-start(f32[16]{0:T(128)} %param.9) | copy-start | bytes 196
  13.7 12.3 %collective-permute-start.3 = (f32[48,128]{1,0:T(8,128)S(1)}, f32[48,128]{1,0:T(8,128)S(1)}, u32[]{:S(2)}, u32[]{:S(2)}) collective-permute-start(f32[48,128]{1,0:T(8,128)S(1)} %get-tuple-element.28), channel_id=1, source_target_pairs={{32,0},{64,32},{96,64},{128,96},{160,128},{192,160},{224,192},{256... | collective-permute-start | bytes 73736 | tf_op jit(solution)/shard_map/ppermute | solution.py:521
  22.8 0.7 copy-start.2
  47.5 11.3 %collective-permute-start.4 = (f32[56,128]{1,0:T(8,128)S(1)}, f32[56,128]{1,0:T(8,128)S(1)}, u32[]{:S(2)}, u32[]{:S(2)}) collective-permute-start(f32[56,128]{1,0:T(8,128)S(1)} %shard_map.59), channel_id=1, source_target_pairs={{0,8},{8,0},{16,24},{24,16},{1,9},{9,1},{17,25},{25,17},{2,10},{10... | collective-permute-start | bytes 86024 | tf_op jit(solution)/shard_map/ppermute | solution.py:542
  58.9 9.5 %collective-permute-start.5 = (f32[112,128]{1,0:T(8,128)S(1)}, f32[112,128]{1,0:T(8,128)S(1)}, u32[]{:S(2)}, u32[]{:S(2)}) collective-permute-start(f32[112,128]{1,0:T(8,128)S(1)} %pad_maximum_fusion.half), channel_id=1, source_target_pairs={{0,24},{8,16},{16,8},{24,0},{1,25},{9,17},{17,9},{25,1},{2,26},{10... | collective-permute-start | bytes 172040 | tf_op jit(solution)/shard_map/ppermute | solution.py:544
  68.8 5.8 %collective-permute-start.6 = (f32[96,128]{1,0:T(8,128)S(1)}, f32[96,128]{1,0:T(8,128)S(1)}, u32[]{:S(2)}, u32[]{:S(2)}) collective-permute-start(f32[96,128]{1,0:T(8,128)S(1)} %get-tuple-element.32.total), channel_id=1, source_target_pairs={{0,1},{1,0},{2,3},{3,2},{4,5},{5,4},{6,7},{7,6},{8,9},{9,8},{10,11... | collective-permute-start | bytes 147464 | tf_op jit(solution)/shard_map/ppermute | solution.py:548
  75.3 8.7 %collective-permute-start.9 = (f32[96,128]{1,0:T(8,128)S(1)}, f32[96,128]{1,0:T(8,128)S(1)}, u32[]{:S(2)}, u32[]{:S(2)}) collective-permute-start(f32[96,128]{1,0:T(8,128)S(1)} %shard_map.61), channel_id=1, source_target_pairs={{0,384},{1,385},{2,386},{3,387},{4,388},{5,389},{6,390},{7,391},{8... | collective-permute-start | bytes 147464 | tf_op jit(solution)/shard_map/ppermute | solution.py:551
  80.5 3.5 %collective-permute-start.8 = (f32[96,128]{1,0:T(8,128)S(1)}, f32[96,128]{1,0:T(8,128)S(1)}, u32[]{:S(2)}, u32[]{:S(2)}) collective-permute-start(f32[96,128]{1,0:T(8,128)S(1)} %shard_map.61), channel_id=1, source_target_pairs={{0,256},{128,384},{1,257},{129,385},{2,258},{130,386},{3,259},{131... | collective-permute-start | bytes 147464 | tf_op jit(solution)/shard_map/ppermute | solution.py:551
  81.8 3.5 %collective-permute-start.7 = (f32[96,128]{1,0:T(8,128)S(1)}, f32[96,128]{1,0:T(8,128)S(1)}, u32[]{:S(2)}, u32[]{:S(2)}) collective-permute-start(f32[96,128]{1,0:T(8,128)S(1)} %shard_map.61), channel_id=1, source_target_pairs={{0,128},{128,256},{256,384},{1,129},{129,257},{257,385},{2,130},{1... | collective-permute-start | bytes 147464 | tf_op jit(solution)/shard_map/ppermute | solution.py:551

commit v4 on v3

--- a/solution.py
+++ b/solution.py
@@ -60,17 +60,16 @@
 MASK_AT = LAYERS * (3 * BAND - 2)
 
 
-def pack_kernel(state, mask, sent, first, rest, restricted, rows, sems):
+def pack_kernel(state, mask, sent, first, rest, restricted, sems):
     copies = [
         pltpu.make_async_copy(state.at[pl.ds(0, CUT)], first, sems.at[0]),
         pltpu.make_async_copy(state.at[pl.ds(CUT, MASK - CUT)], rest.at[pl.ds(0, MASK - CUT)], sems.at[1]),
-        pltpu.make_async_copy(mask, rows, sems.at[2]),
+        pltpu.make_async_copy(mask, rest.at[pl.ds(MASK - CUT, BAND)], sems.at[2]),
     ]
     for copy in copies:
         copy.start()
     for copy in copies:
         copy.wait()
-    rest[MASK - CUT :, :] = rows[...].astype(F32)
 
     def row_of(f, r):
         if f < 2:
@@ -358,15 +357,21 @@
         down = jnp.where(bottom, 0.0, down)
         return [x[1] - down, x[2] - x[0], x[3] - x[1], up - x[2]]
 
+    kept = [keep * m for m in masks]
+    turned = [m * f for m, f in zip(masks, coriolis)]
+    pushed = [(0.5 * value) * m for m in masks]
+    spread = [0.5 * m for m in masks]
+
     def propagate(state):
         h, u, v = state
         for _ in range(2):
-            p = [(0.5 * value) * x for x in h]
-            north_p = north(p, 1.0)
-            u = [masks[i] * (keep * u[i] + coriolis[i] * v[i] - east(p[i])) for i in range(4)]
-            v = [masks[i] * (keep * v[i] - coriolis[i] * u[i] - north_p[i]) for i in range(4)]
+            north_h = north(h, 1.0)
+            slow = [kept[i] * v[i] - pushed[i] * north_h[i] for i in range(4)]
+            u = [(kept[i] * u[i] + turned[i] * v[i]) - pushed[i] * east(h[i]) for i in range(4)]
+            v = [slow[i] - turned[i] * u[i] for i in range(4)]
+            rest = [masks[i] * h[i] - spread[i] * east(u[i]) for i in range(4)]
             north_v = north(v, -1.0)
-            h = [masks[i] * (h[i] - 0.5 * (east(u[i]) + north_v[i])) for i in range(4)]
+            h = [rest[i] - spread[i] * north_v[i] for i in range(4)]
         return [h, u, v]
 
     return propagate
@@ -426,16 +431,21 @@
     mine, theirs = load_state(total), load_state(mate)
     earlier = [[jnp.where(odd, t, m) for m, t in zip(a, b)] for a, b in zip(mine, theirs)]
     later = [[jnp.where(odd, m, t) for m, t in zip(a, b)] for a, b in zip(mine, theirs)]
-    store_state(both, add_state(propagate(propagate(earlier)), later))
-
-
-def earlier_kernel(two, three, mask, values, fold, out):
+    trips = jnp.where(lax.axis_index("zl") < 3, 1, 0)
+    state = lax.fori_loop(0, trips, lambda _, s: propagate(propagate(s)), earlier)
+    store_state(both, add_state(state, later))
+
+
+def repeat(wanted, propagate, state):
+    return lax.fori_loop(0, jnp.where(wanted, 2, 0), lambda _, s: propagate(propagate(s)), state)
+
+
+def earlier_kernel(three, mask, values, fold, out):
     propagate = coarse_tools(values[pl.ds(mode_index(), 1), :], load_masks(mask), fold)
-    state = lax.fori_loop(0, 2, lambda _, s: propagate(propagate(s)), load_state(three))
-    store_state(out, add_state(state, load_state(two)))
-
-
-def chain_kernel(one, earlier, mate, jumps, mask, values, fold, chunk):
+    store_state(out, repeat(lax.axis_index("zl") == 3, propagate, load_state(three)))
+
+
+def chain_kernel(one, two, earlier, mate, jumps, mask, values, fold, chunk):
     quarter = lax.axis_index("zh")
     core = core_index()
     propagate = coarse_tools(values[pl.ds(mode_index(), 1), :], load_masks(mask), fold)
@@ -443,7 +453,8 @@
     def twice(state):
         return propagate(propagate(state))
 
-    state = lax.fori_loop(0, 2, lambda _, s: twice(s), load_state(earlier))
+    state = add_state(load_state(earlier), load_state(two))
+    state = repeat(lax.axis_index("zl") >= 2, propagate, state)
     state = add_state(state, load_state(one))
     state = lax.fori_loop(0, core, lambda _, s: add_state(twice(s), load_state(mate)), state)
     seg = iota((8, ZONAL), 1) % 4
@@ -510,9 +521,9 @@
     sent, first, rest, restricted = call(
         pack_kernel,
         [(MASK_AT + BAND, ZONAL), (CUT, ZONAL), (MASK + BAND - CUT, ZONAL), (3 * LAYERS, ZONAL)],
-        [pltpu.VMEM((BAND, ZONAL), jnp.int32), pltpu.SemaphoreType.DMA((3,))],
+        [pltpu.SemaphoreType.DMA((3,))],
         spaces=(pl.ANY, pl.ANY),
-    )(start_state.reshape(MASK, ZONAL), land_mask)
+    )(start_state.reshape(MASK, ZONAL), land_mask.astype(F32))
     fold = fold_map.reshape(1, ZONAL)
     depth_row = depths.reshape(1, LAYERS)
     across = [(i, i + 1) for i in range(1, BANDS - 1, 2)]
@@ -550,9 +561,9 @@
     three, two, one = (
         lax.ppermute(both, ("zl",), [(i, i + d) for i in range(4 - d)]) for d in (3, 2, 1)
     )
-    (earlier,) = call(earlier_kernel, [(96, ZONAL)])(two, three, mask, values, fold)
+    (earlier,) = call(earlier_kernel, [(96, ZONAL)])(three, mask, values, fold)
     (chunk,) = call(chain_kernel, [(4 * BANDS, ZONAL)])(
-        one, earlier, mate, jumps, mask, values, fold
+        one, two, earlier, mate, jumps, mask, values, fold
     )
     change = swap(chunk, PLANE)
     (result,) = call(

time: 101 us -> 97.2 us (0.962)
  Pallas kernels: 19.8 us -> 15.8 us
  starting transfers between devices: 42.7 us -> 40.4 us
  blocking collectives: 29.7 us -> 31.4 us
  waiting for transfers between devices: 5.32 us -> 6.54 us
    pallas_call x10, Pallas kernels: 19.8 us -> 15.8 us  [run(): pl.pallas_call(kernel, out_shape=[jax.ShapeDtypeStruct(s, F32) for s in o...]
    ppermute x1, starting transfers between devices: 4.94 us -> 2.78 us  [body(): mate = lax.ppermute(total, ('c',), [(0, 1), (1, 0)])]
    all_to_all x2, blocking collectives: 29.7 us -> 31.4 us  [swap(): return lax.all_to_all(block, axes, 0, 0, tiled=True)]
    ppermute x1, waiting for transfers between devices: 1.94 us -> 3.11 us  [body(): other_half = lax.ppermute(half, ('zh',), [(i, i ^ 3) for i in range(4)])]
    ppermute x3, starting transfers between devices: 8.69 us -> 7.54 us  [body(): lax.ppermute(both, ('zl',), [(i, i + d) for i in range(4 - d)])]
    ppermute x3, waiting for transfers between devices: 0.01 us -> 1.08 us  [body(): lax.ppermute(both, ('zl',), [(i, i + d) for i in range(4 - d)])]
    ppermute x1, starting transfers between devices: 7.55 us -> 8.59 us  [body(): other_half = lax.ppermute(half, ('zh',), [(i, i ^ 3) for i in range(4)])]
    ppermute x1, waiting for transfers between devices: 2.5 us -> 1.48 us  [body(): beside = lax.ppermute(mine, ('zh',), [(i, i ^ 1) for i in range(4)])]
  transfers between devices with their start and end apart: 10 -> 10, of which waited for: 3 -> 4; matrix products, arithmetic and copies ran while one was open for 0% -> 0% of each run, Pallas kernels for 12% -> 9%
where the time goes in v4:
time: 97.2 us; the launch traced here: 96.7 us
  starting transfers between devices  40.4 us (42%)
  blocking collectives  31.4 us (32%)
  Pallas kernels  15.8 us (16%)
  waiting for transfers between devices  6.54 us (7%)
  local copies, waits for them, and re-layouts  1.65 us (2%)
    all_to_all x2, blocking collectives, swap(): return lax.all_to_all(block, axes, 0, 0, tiled=True)  31.4 us
    pallas_call x10, Pallas kernels, run(): pl.pallas_call(kernel, out_shape=[jax.ShapeDtypeStruct(s, F32) for s in o...  15.8 us
    ppermute x1, starting transfers between devices, body(): beside = lax.ppermute(mine, ('zh',), [(i, i ^ 1) for i in range(4)])  8.81 us
    ppermute x1, starting transfers between devices, body(): other_half = lax.ppermute(half, ('zh',), [(i, i ^ 3) for i in range(4)])  8.59 us
    ppermute x3, starting transfers between devices, body(): lax.ppermute(both, ('zl',), [(i, i + d) for i in range(4 - d)])  7.54 us
    ppermute x2, starting transfers between devices, body(): mate = [lax.ppermute(part, SPACE, inside) for part in (first, rest)]  6.8 us
    ppermute x1, starting transfers between devices, body(): other = lax.ppermute(sent, SPACE, across)  4.59 us
    ppermute x1, waiting for transfers between devices, body(): other_half = lax.ppermute(half, ('zh',), [(i, i ^ 3) for i in range(4)])  3.11 us
  transfers between devices with their start and end apart: 10, of which 4 were waited for; matrix products, arithmetic and copies ran while one was open for 0% of the time, Pallas kernels for 9%

profile of v4, /device:TPU:1, one launch (start us, length us, event | category | flops | bytes accessed | tf_op | source)
XLA Modules:
  0.0 96.7 jit_solution(7125144630513355868)
XLA Ops:
  0.0 0.7 convert_element_type.3.mask
  0.7 1.0 %copy-done = f32[1,3,16,16,128]{4,3,2,1,0:T(8,128)S(1)} copy-done((f32[1,3,16,16,128]{4,3,2,1,0:T(8,128)S(1)}, f32[1,3,16,16,128]{4,3,2,1,0:T(8,128)}, u32[]{:S(2)}) %copy-start) | copy-done | bytes 393240
  2.3 4.6 %collective-permute-start = (f32[752,128]{1,0:T(8,128)S(1)}, f32[752,128]{1,0:T(8,128)S(1)}, u32[]{:S(2)}, u32[]{:S(2)}) collective-permute-start(f32[752,128]{1,0:T(8,128)S(1)} %get-tuple-element.22), channel_id=1, source_target_pairs={{1,2},{3,4},{5,6},{7,8},{9,10},{11,12},{13,14},{15,16},{17,18},{19... | collective-permute-start | bytes 1155080 | tf_op jit(solution)/shard_map/ppermute | solution.py:531
  6.9 4.9 %collective-permute-start.1 = (f32[512,128]{1,0:T(8,128)S(1)}, f32[512,128]{1,0:T(8,128)S(1)}, u32[]{:S(2)}, u32[]{:S(2)}) collective-permute-start(f32[512,128]{1,0:T(8,128)S(1)} %get-tuple-element.20.own_first), channel_id=1, source_target_pairs={{0,1},{1,0},{2,3},{3,2},{4,5},{5,4},{6,7},{7,6},{8,9},{9,8},{10,11... | collective-permute-start | bytes 786440 | tf_op jit(solution)/shard_map/ppermute | solution.py:537
  11.8 1.9 %collective-permute-start.2 = (f32[272,128]{1,0:T(8,128)S(1)}, f32[272,128]{1,0:T(8,128)S(1)}, u32[]{:S(2)}, u32[]{:S(2)}) collective-permute-start(f32[272,128]{1,0:T(8,128)S(1)} %get-tuple-element.21.own_rest), channel_id=1, source_target_pairs={{0,1},{1,0},{2,3},{3,2},{4,5},{5,4},{6,7},{7,6},{8,9},{9,8},{10,11... | collective-permute-start | bytes 417800 | tf_op jit(solution)/shard_map/ppermute | solution.py:537
  13.7 1.3 %collective-permute-start.3 = (f32[48,128]{1,0:T(8,128)S(1)}, f32[48,128]{1,0:T(8,128)S(1)}, u32[]{:S(2)}, u32[]{:S(2)}) collective-permute-start(f32[48,128]{1,0:T(8,128)S(1)} %get-tuple-element.28), channel_id=1, source_target_pairs={{32,0},{64,32},{96,64},{128,96},{160,128},{192,160},{224,192},{256... | collective-permute-start | bytes 73736 | tf_op jit(solution)/shard_map/ppermute | solution.py:532
  15.1 6.2 %shard_map.57 = (f32[16,128]{1,0:T(8,128)S(1)}, f32[16,128]{1,0:T(8,128)S(1)}) custom-call(f32[16,16]{1,0:T(8,128)S(1)} %copy-done.1, f32[1,16]{1,0:T(1,128)S(1)} %bitcast.18), custom_call_target="tpu_custom_call" | custom-call | flops 10485760 | bytes 1048576 | tf_op jit(solution)/shard_map/pallas_call | solution.py:503
  22.0 2.6 %shard_map.56 = (f32[20,2,8,128]{3,2,1,0:T(8,128)S(1)}, f32[20,2,8,128]{3,2,1,0:T(8,128)S(1)}, f32[20,2,8,128]{3,2,1,0:T(8,128)S(1)}, f32[1,128]{1,0:T(1,128)S(1)}) custom-call(f32[512,128]{1,0:T(8,128)S(1)} %get-tuple-element.20.own_first, f32[272,128]{1,0:T(8,128)S(1)} %get-tuple-element.21.own_rest, f32[512,128]{1,0:T(8,128)S(1)} %collective-permute-done.1.mate_first, ...), custom_call_target="tpu_custom_call" | custom-call | flops 4194304 | bytes 1048576 | tf_op jit(solution)/shard_map/pallas_call | solution.py:503
  24.6 2.8 %shard_map.58 = (f32[48,16,128]{2,1,0:T(8,128)S(1)}, f32[128,128]{1,0:T(8,128)S(1)}) custom-call(f32[512,128]{1,0:T(8,128)S(1)} %get-tuple-element.20.own_first, f32[272,128]{1,0:T(8,128)S(1)} %get-tuple-element.21.own_rest, f32[752,128]{1,0:T(8,128)S(1)} %collective-permute-done.other, f32[20,2,8,128]{3,2,1,0:T(8,128)S(1)} %get-tuple-element.23.h_in, ...), custom_call_target="tpu_custom_call" | custom-call | flops 1048576 | bytes 1048576 | tf_op jit(solution)/shard_map/pallas_call | solution.py:503
  27.4 20.1 %all_to_all.22 = f32[32,4,128]{2,1,0:T(4,128)S(1)} all-to-all(f32[32,4,128]{2,1,0:T(4,128)S(1)} %bitcast.12), channel_id=1, replica_groups=mesh['zl'=4,'x'=4,'zh'=4,'y'=4,'c'=2] {'x','y','c'}, dimensions={0} | all-to-all | bytes 131072 | tf_op jit(solution)/shard_map/all_to_all | solution.py:517
  47.5 8.8 %collective-permute-start.4 = (f32[56,128]{1,0:T(8,128)S(1)}, f32[56,128]{1,0:T(8,128)S(1)}, u32[]{:S(2)}, u32[]{:S(2)}) collective-permute-start(f32[56,128]{1,0:T(8,128)S(1)} %shard_map.59), channel_id=1, source_target_pairs={{0,8},{8,0},{16,24},{24,16},{1,9},{9,1},{17,25},{25,17},{2,10},{10... | collective-permute-start | bytes 86024 | tf_op jit(solution)/shard_map/ppermute | solution.py:553
  56.4 1.5 %collective-permute-done.4 = f32[56,128]{1,0:T(8,128)S(1)} collective-permute-done((f32[56,128]{1,0:T(8,128)S(1)}, f32[56,128]{1,0:T(8,128)S(1)}, u32[]{:S(2)}, u32[]{:S(2)}) %collective-permute-start.4) | collective-permute-done | bytes 28704 | tf_op jit(solution)/shard_map/ppermute | solution.py:553
  57.8 8.6 %collective-permute-start.5 = (f32[112,128]{1,0:T(8,128)S(1)}, f32[112,128]{1,0:T(8,128)S(1)}, u32[]{:S(2)}, u32[]{:S(2)}) collective-permute-start(f32[112,128]{1,0:T(8,128)S(1)} %pad_maximum_fusion.half), channel_id=1, source_target_pairs={{0,24},{8,16},{16,8},{24,0},{1,25},{9,17},{17,9},{25,1},{2,26},{10... | collective-permute-start | bytes 172040 | tf_op jit(solution)/shard_map/ppermute | solution.py:555
  66.4 3.1 %collective-permute-done.5.other_half = f32[112,128]{1,0:T(8,128)S(1)} collective-permute-done((f32[112,128]{1,0:T(8,128)S(1)}, f32[112,128]{1,0:T(8,128)S(1)}, u32[]{:S(2)}, u32[]{:S(2)}) %collective-permute-start.5) | collective-permute-done | bytes 57376 | tf_op jit(solution)/shard_map/ppermute | solution.py:555
  69.9 2.8 %collective-permute-start.6 = (f32[96,128]{1,0:T(8,128)S(1)}, f32[96,128]{1,0:T(8,128)S(1)}, u32[]{:S(2)}, u32[]{:S(2)}) collective-permute-start(f32[96,128]{1,0:T(8,128)S(1)} %get-tuple-element.32.total), channel_id=1, source_target_pairs={{0,1},{1,0},{2,3},{3,2},{4,5},{5,4},{6,7},{7,6},{8,9},{9,8},{10,11... | collective-permute-start | bytes 147464 | tf_op jit(solution)/shard_map/ppermute | solution.py:559
  72.7 0.9 collective-permute-done.6.mate
  73.6 0.7 shard_map.61
  74.3 4.1 %collective-permute-start.9 = (f32[96,128]{1,0:T(8,128)S(1)}, f32[96,128]{1,0:T(8,128)S(1)}, u32[]{:S(2)}, u32[]{:S(2)}) collective-permute-start(f32[96,128]{1,0:T(8,128)S(1)} %shard_map.61), channel_id=1, source_target_pairs={{0,384},{1,385},{2,386},{3,387},{4,388},{5,389},{6,390},{7,391},{8... | collective-permute-start | bytes 147464 | tf_op jit(solution)/shard_map/ppermute | solution.py:562
  78.3 1.3 %collective-permute-start.8 = (f32[96,128]{1,0:T(8,128)S(1)}, f32[96,128]{1,0:T(8,128)S(1)}, u32[]{:S(2)}, u32[]{:S(2)}) collective-permute-start(f32[96,128]{1,0:T(8,128)S(1)} %shard_map.61), channel_id=1, source_target_pairs={{0,256},{128,384},{1,257},{129,385},{2,258},{130,386},{3,259},{131... | collective-permute-start | bytes 147464 | tf_op jit(solution)/shard_map/ppermute | solution.py:562
  79.6 2.2 %collective-permute-start.7 = (f32[96,128]{1,0:T(8,128)S(1)}, f32[96,128]{1,0:T(8,128)S(1)}, u32[]{:S(2)}, u32[]{:S(2)}) collective-permute-start(f32[96,128]{1,0:T(8,128)S(1)} %shard_map.61), channel_id=1, source_target_pairs={{0,128},{128,256},{256,384},{1,129},{129,257},{257,385},{2,130},{1... | collective-permute-start | bytes 147464 | tf_op jit(solution)/shard_map/ppermute | solution.py:562
  81.9 1.1 %collective-permute-done.7.one = f32[96,128]{1,0:T(8,128)S(1)} collective-permute-done((f32[96,128]{1,0:T(8,128)S(1)}, f32[96,128]{1,0:T(8,128)S(1)}, u32[]{:S(2)}, u32[]{:S(2)}) %collective-permute-start.7) | collective-permute-done | bytes 49184 | tf_op jit(solution)/shard_map/ppermute | solution.py:562
  83.0 1.4 %shard_map.63 = f32[128,128]{1,0:T(8,128)S(1)} custom-call(f32[96,128]{1,0:T(8,128)S(1)} %collective-permute-done.7.one, f32[96,128]{1,0:T(8,128)S(1)} %collective-permute-done.8.two, f32[96,128]{1,0:T(8,128)S(1)} %shard_map.62.earlier, f32[96,128]{1,0:T(8,128)S(1)} %collective-permute-done.6.mate, f32[192,128]{1,0:T(8,128)S(1)} %get-tuple-element.34.jumps, ...), custom_call_target="tpu_custom_call" | custom-call | flops 1048576 | bytes 1048576 | tf_op jit(solution)/shard_map/pallas_call | solution.py:503
  84.4 11.2 %all_to_all.23 = f32[32,4,128]{2,1,0:T(4,128)S(1)} all-to-all(f32[32,4,128]{2,1,0:T(4,128)S(1)} %bitcast.11), channel_id=1, replica_groups=mesh['zl'=4,'x'=4,'zh'=4,'y'=4,'c'=2] {'x','y','c'}, dimensions={0} | all-to-all | bytes 131072 | tf_op jit(solution)/shard_map/all_to_all | solution.py:517
  95.6 1.1 %shard_map.64 = f32[768,128]{1,0:T(8,128)} custom-call(f32[48,16,128]{2,1,0:T(8,128)S(1)} %get-tuple-element.29.fine, f32[128,128]{1,0:T(8,128)S(1)} %bitcast.9, f32[16,128]{1,0:T(8,128)S(1)} %get-tuple-element.27.vectors, f32[1,16]{1,0:T(1,128)S(1)} %bitcast.21), custom_call_target="tpu_custom_call" | custom-call | flops 1048576 | bytes 1048576 | tf_op jit(solution)/shard_map/pallas_call | solution.py:503
  (18 shorter events, 1.7 us)
Async XLA Ops:
  0.7 1.0 %copy-start = (f32[1,3,16,16,128]{4,3,2,1,0:T(8,128)S(1)}, f32[1,3,16,16,128]{4,3,2,1,0:T(8,128)}, u32[]{:S(2)}) copy-start(f32[1,3,16,16,128]{4,3,2,1,0:T(8,128)} %param.5) | copy-start | bytes 1179652
  2.3 12.7 %copy-start.1 = (f32[16,16]{1,0:T(8,128)S(1)}, f32[16,16]{1,0:T(8,128)}, u32[]{:S(2)}) copy-start(f32[16,16]{1,0:T(8,128)} %coupling.5) | copy-start | bytes 3076
  2.3 22.3 %collective-permute-start = (f32[752,128]{1,0:T(8,128)S(1)}, f32[752,128]{1,0:T(8,128)S(1)}, u32[]{:S(2)}, u32[]{:S(2)}) collective-permute-start(f32[752,128]{1,0:T(8,128)S(1)} %get-tuple-element.22), channel_id=1, source_target_pairs={{1,2},{3,4},{5,6},{7,8},{9,10},{11,12},{13,14},{15,16},{17,18},{19... | collective-permute-start | bytes 1155080 | tf_op jit(solution)/shard_map/ppermute | solution.py:531
  6.9 14.4 %collective-permute-start.1 = (f32[512,128]{1,0:T(8,128)S(1)}, f32[512,128]{1,0:T(8,128)S(1)}, u32[]{:S(2)}, u32[]{:S(2)}) collective-permute-start(f32[512,128]{1,0:T(8,128)S(1)} %get-tuple-element.20.own_first), channel_id=1, source_target_pairs={{0,1},{1,0},{2,3},{3,2},{4,5},{5,4},{6,7},{7,6},{8,9},{9,8},{10,11... | collective-permute-start | bytes 786440 | tf_op jit(solution)/shard_map/ppermute | solution.py:537
  11.8 9.5 %collective-permute-start.2 = (f32[272,128]{1,0:T(8,128)S(1)}, f32[272,128]{1,0:T(8,128)S(1)}, u32[]{:S(2)}, u32[]{:S(2)}) collective-permute-start(f32[272,128]{1,0:T(8,128)S(1)} %get-tuple-element.21.own_rest), channel_id=1, source_target_pairs={{0,1},{1,0},{2,3},{3,2},{4,5},{5,4},{6,7},{7,6},{8,9},{9,8},{10,11... | collective-permute-start | bytes 417800 | tf_op jit(solution)/shard_map/ppermute | solution.py:537
  13.7 1.3 %copy-start.3 = (f32[16]{0:T(128)S(1)}, f32[16]{0:T(128)}, u32[]{:S(2)}) copy-start(f32[16]{0:T(128)} %param.9) | copy-start | bytes 196
  13.7 10.8 %collective-permute-start.3 = (f32[48,128]{1,0:T(8,128)S(1)}, f32[48,128]{1,0:T(8,128)S(1)}, u32[]{:S(2)}, u32[]{:S(2)}) collective-permute-start(f32[48,128]{1,0:T(8,128)S(1)} %get-tuple-element.28), channel_id=1, source_target_pairs={{32,0},{64,32},{96,64},{128,96},{160,128},{192,160},{224,192},{256... | collective-permute-start | bytes 73736 | tf_op jit(solution)/shard_map/ppermute | solution.py:532
  21.3 0.7 copy-start.2
  47.5 10.3 %collective-permute-start.4 = (f32[56,128]{1,0:T(8,128)S(1)}, f32[56,128]{1,0:T(8,128)S(1)}, u32[]{:S(2)}, u32[]{:S(2)}) collective-permute-start(f32[56,128]{1,0:T(8,128)S(1)} %shard_map.59), channel_id=1, source_target_pairs={{0,8},{8,0},{16,24},{24,16},{1,9},{9,1},{17,25},{25,17},{2,10},{10... | collective-permute-start | bytes 86024 | tf_op jit(solution)/shard_map/ppermute | solution.py:553
  57.8 11.7 %collective-permute-start.5 = (f32[112,128]{1,0:T(8,128)S(1)}, f32[112,128]{1,0:T(8,128)S(1)}, u32[]{:S(2)}, u32[]{:S(2)}) collective-permute-start(f32[112,128]{1,0:T(8,128)S(1)} %pad_maximum_fusion.half), channel_id=1, source_target_pairs={{0,24},{8,16},{16,8},{24,0},{1,25},{9,17},{17,9},{25,1},{2,26},{10... | collective-permute-start | bytes 172040 | tf_op jit(solution)/shard_map/ppermute | solution.py:555
  69.9 3.7 %collective-permute-start.6 = (f32[96,128]{1,0:T(8,128)S(1)}, f32[96,128]{1,0:T(8,128)S(1)}, u32[]{:S(2)}, u32[]{:S(2)}) collective-permute-start(f32[96,128]{1,0:T(8,128)S(1)} %get-tuple-element.32.total), channel_id=1, source_target_pairs={{0,1},{1,0},{2,3},{3,2},{4,5},{5,4},{6,7},{7,6},{8,9},{9,8},{10,11... | collective-permute-start | bytes 147464 | tf_op jit(solution)/shard_map/ppermute | solution.py:559
  74.3 7.6 %collective-permute-start.9 = (f32[96,128]{1,0:T(8,128)S(1)}, f32[96,128]{1,0:T(8,128)S(1)}, u32[]{:S(2)}, u32[]{:S(2)}) collective-permute-start(f32[96,128]{1,0:T(8,128)S(1)} %shard_map.61), channel_id=1, source_target_pairs={{0,384},{1,385},{2,386},{3,387},{4,388},{5,389},{6,390},{7,391},{8... | collective-permute-start | bytes 147464 | tf_op jit(solution)/shard_map/ppermute | solution.py:562
  78.3 3.6 %collective-permute-start.8 = (f32[96,128]{1,0:T(8,128)S(1)}, f32[96,128]{1,0:T(8,128)S(1)}, u32[]{:S(2)}, u32[]{:S(2)}) collective-permute-start(f32[96,128]{1,0:T(8,128)S(1)} %shard_map.61), channel_id=1, source_target_pairs={{0,256},{128,384},{1,257},{129,385},{2,258},{130,386},{3,259},{131... | collective-permute-start | bytes 147464 | tf_op jit(solution)/shard_map/ppermute | solution.py:562
  79.6 3.4 %collective-permute-start.7 = (f32[96,128]{1,0:T(8,128)S(1)}, f32[96,128]{1,0:T(8,128)S(1)}, u32[]{:S(2)}, u32[]{:S(2)}) collective-permute-start(f32[96,128]{1,0:T(8,128)S(1)} %shard_map.61), channel_id=1, source_target_pairs={{0,128},{128,256},{256,384},{1,129},{129,257},{257,385},{2,130},{1... | collective-permute-start | bytes 147464 | tf_op jit(solution)/shard_map/ppermute | solution.py:562

commit v5 on v4

--- a/solution.py
+++ b/solution.py
@@ -399,9 +399,13 @@
 
 
 def collect_kernel(spread, out):
-    for part in range(PARTS):
-        at = core_index() * 64 + part + (1 if part > 3 else 0) * 28
-        out[part * 8 : part * 8 + 8, :] = spread[pl.ds(at, 8, stride=4), :]
+    for core in range(2):
+
+        @pl.when(core_index() == core)
+        def _():
+            for part in range(PARTS):
+                at = core * 64 + part + (28 if part > 3 else 0)
+                out[part * 8 : part * 8 + 8, :] = spread[pl.ds(at, 8, stride=4), :]
 
 
 def pair_kernel(half, other_half, values, fold, jumps, mask_out, total):
@@ -461,12 +465,19 @@
     chunk[...] = jnp.zeros_like(chunk)
     for x in range(2):
         state = propagate(state)
+        packed = []
         for f in range(3):
-            packed = None
-            for cr in range(4):
-                piece = pltpu.roll(state[f][cr], lax.rem(cr - quarter + ZONAL, ZONAL), 1)
-                packed = piece if cr == 0 else jnp.where(seg == cr, piece, packed)
-            chunk[pl.ds((2 * core + x) * 32 + f, 8, stride=4), :] = packed
+            pieces = [pltpu.roll(state[f][cr], lax.rem(cr - quarter + ZONAL, ZONAL), 1) for cr in range(4)]
+            packed.append(pieces[0])
+            for cr in range(1, 4):
+                packed[f] = jnp.where(seg == cr, pieces[cr], packed[f])
+        for which in range(2):
+
+            @pl.when(core == which)
+            def _():
+                for f in range(3):
+                    chunk[pl.ds((2 * which + x) * 32 + f, 8, stride=4), :] = packed[f]
+
         if x == 0:
             state = add_state(state, load_state(jumps))
 
@@ -479,10 +490,14 @@
     lane = iota((LAYERS, ZONAL), 1)
     copies = []
     for f in range(3):
-        in_modes = gathered[pl.ds(half * 4 + f, LAYERS, stride=8), :]
+        in_modes = jnp.where(
+            half == 0, gathered[pl.ds(f, LAYERS, stride=8), :], gathered[pl.ds(4 + f, LAYERS, stride=8), :]
+        )
+        (top, rest), (mode_top, mode_rest) = two_parts(in_modes), two_parts(vectors[:, :LAYERS])
         change = lax.dot_general(
-            vectors[:, :LAYERS], in_modes, (((0,), (0,)), ((), ())),
-            precision=HIGHEST, preferred_element_type=F32,
+            jnp.concatenate([mode_top, mode_top, mode_rest], axis=0),
+            jnp.concatenate([top, rest, top], axis=0),
+            (((0,), (0,)), ((), ())), preferred_element_type=F32,
         )
         change = change * root if f == 0 else change / root
         for cr in range(4):

time: 97.2 us -> 98.7 us (1.015)
  starting transfers between devices: 40.4 us -> 42.1 us
  Pallas kernels: 15.8 us -> 17.4 us
  blocking collectives: 31.4 us -> 29.9 us
    ppermute x1, starting transfers between devices: 2.78 us -> 4.94 us  [body(): mate = lax.ppermute(total, ('c',), [(0, 1), (1, 0)])]
    pallas_call x10, Pallas kernels: 15.8 us -> 17.4 us  [run(): pl.pallas_call(kernel, out_shape=[jax.ShapeDtypeStruct(s, F32) for s in o...]
    all_to_all x2, blocking collectives: 31.4 us -> 29.9 us  [swap(): return lax.all_to_all(block, axes, 0, 0, tiled=True)]
    ppermute x1, waiting for transfers between devices: 3.11 us -> 1.94 us  [body(): other_half = lax.ppermute(half, ('zh',), [(i, i ^ 3) for i in range(4)])]
    ppermute x1, starting transfers between devices: 8.59 us -> 7.55 us  [body(): other_half = lax.ppermute(half, ('zh',), [(i, i ^ 3) for i in range(4)])]
    ppermute x1, waiting for transfers between devices: 1.48 us -> 2.5 us  [body(): beside = lax.ppermute(mine, ('zh',), [(i, i ^ 1) for i in range(4)])]
  transfers between devices with their start and end apart: 10 -> 10, of which waited for: 4 -> 4; matrix products, arithmetic and copies ran while one was open for 0% -> 0% of each run, Pallas kernels for 9% -> 11%
where the time goes in v5:
time: 98.7 us; the launch traced here: 98.2 us
  starting transfers between devices  42.1 us (43%)
  blocking collectives  29.9 us (30%)
  Pallas kernels  17.4 us (18%)
  waiting for transfers between devices  6.39 us (6%)
  local copies, waits for them, and re-layouts  1.65 us (2%)
    all_to_all x2, blocking collectives, swap(): return lax.all_to_all(block, axes, 0, 0, tiled=True)  29.9 us
    pallas_call x10, Pallas kernels, run(): pl.pallas_call(kernel, out_shape=[jax.ShapeDtypeStruct(s, F32) for s in o...  17.4 us
    ppermute x1, starting transfers between devices, body(): beside = lax.ppermute(mine, ('zh',), [(i, i ^ 1) for i in range(4)])  8.81 us
    ppermute x3, starting transfers between devices, body(): lax.ppermute(both, ('zl',), [(i, i + d) for i in range(4 - d)])  8.07 us
    ppermute x1, starting transfers between devices, body(): other_half = lax.ppermute(half, ('zh',), [(i, i ^ 3) for i in range(4)])  7.55 us
    ppermute x2, starting transfers between devices, body(): mate = [lax.ppermute(part, SPACE, inside) for part in (first, rest)]  6.8 us
    ppermute x1, starting transfers between devices, body(): mate = lax.ppermute(total, ('c',), [(0, 1), (1, 0)])  4.94 us
    ppermute x1, starting transfers between devices, body(): other = lax.ppermute(sent, SPACE, across)  4.59 us
  transfers between devices with their start and end apart: 10, of which 4 were waited for; matrix products, arithmetic and copies ran while one was open for 0% of the time, Pallas kernels for 11%

profile of v5, /device:TPU:1, one launch (start us, length us, event | category | flops | bytes accessed | tf_op | source)
XLA Modules:
  0.0 98.2 jit_solution(6905078990197970854)
XLA Ops:
  0.0 0.7 convert_element_type.3.mask
  0.7 1.0 %copy-done = f32[1,3,16,16,128]{4,3,2,1,0:T(8,128)S(1)} copy-done((f32[1,3,16,16,128]{4,3,2,1,0:T(8,128)S(1)}, f32[1,3,16,16,128]{4,3,2,1,0:T(8,128)}, u32[]{:S(2)}) %copy-start) | copy-done | bytes 393240
  2.3 4.6 %collective-permute-start = (f32[752,128]{1,0:T(8,128)S(1)}, f32[752,128]{1,0:T(8,128)S(1)}, u32[]{:S(2)}, u32[]{:S(2)}) collective-permute-start(f32[752,128]{1,0:T(8,128)S(1)} %get-tuple-element.22), channel_id=1, source_target_pairs={{1,2},{3,4},{5,6},{7,8},{9,10},{11,12},{13,14},{15,16},{17,18},{19... | collective-permute-start | bytes 1155080 | tf_op jit(solution)/shard_map/ppermute | solution.py:546
  6.9 4.9 %collective-permute-start.1 = (f32[512,128]{1,0:T(8,128)S(1)}, f32[512,128]{1,0:T(8,128)S(1)}, u32[]{:S(2)}, u32[]{:S(2)}) collective-permute-start(f32[512,128]{1,0:T(8,128)S(1)} %get-tuple-element.20.own_first), channel_id=1, source_target_pairs={{0,1},{1,0},{2,3},{3,2},{4,5},{5,4},{6,7},{7,6},{8,9},{9,8},{10,11... | collective-permute-start | bytes 786440 | tf_op jit(solution)/shard_map/ppermute | solution.py:552
  11.8 1.9 %collective-permute-start.2 = (f32[272,128]{1,0:T(8,128)S(1)}, f32[272,128]{1,0:T(8,128)S(1)}, u32[]{:S(2)}, u32[]{:S(2)}) collective-permute-start(f32[272,128]{1,0:T(8,128)S(1)} %get-tuple-element.21.own_rest), channel_id=1, source_target_pairs={{0,1},{1,0},{2,3},{3,2},{4,5},{5,4},{6,7},{7,6},{8,9},{9,8},{10,11... | collective-permute-start | bytes 417800 | tf_op jit(solution)/shard_map/ppermute | solution.py:552
  13.7 1.3 %collective-permute-start.3 = (f32[48,128]{1,0:T(8,128)S(1)}, f32[48,128]{1,0:T(8,128)S(1)}, u32[]{:S(2)}, u32[]{:S(2)}) collective-permute-start(f32[48,128]{1,0:T(8,128)S(1)} %get-tuple-element.28), channel_id=1, source_target_pairs={{32,0},{64,32},{96,64},{128,96},{160,128},{192,160},{224,192},{256... | collective-permute-start | bytes 73736 | tf_op jit(solution)/shard_map/ppermute | solution.py:547
  15.1 7.7 %shard_map.57 = (f32[16,128]{1,0:T(8,128)S(1)}, f32[16,128]{1,0:T(8,128)S(1)}) custom-call(f32[16,16]{1,0:T(8,128)S(1)} %copy-done.1, f32[1,16]{1,0:T(1,128)S(1)} %bitcast.18), custom_call_target="tpu_custom_call" | custom-call | flops 10485760 | bytes 1048576 | tf_op jit(solution)/shard_map/pallas_call | solution.py:518
  23.5 2.6 %shard_map.56 = (f32[20,2,8,128]{3,2,1,0:T(8,128)S(1)}, f32[20,2,8,128]{3,2,1,0:T(8,128)S(1)}, f32[20,2,8,128]{3,2,1,0:T(8,128)S(1)}, f32[1,128]{1,0:T(1,128)S(1)}) custom-call(f32[512,128]{1,0:T(8,128)S(1)} %get-tuple-element.20.own_first, f32[272,128]{1,0:T(8,128)S(1)} %get-tuple-element.21.own_rest, f32[512,128]{1,0:T(8,128)S(1)} %collective-permute-done.1.mate_first, ...), custom_call_target="tpu_custom_call" | custom-call | flops 4194304 | bytes 1048576 | tf_op jit(solution)/shard_map/pallas_call | solution.py:518
  26.1 2.8 %shard_map.58 = (f32[48,16,128]{2,1,0:T(8,128)S(1)}, f32[128,128]{1,0:T(8,128)S(1)}) custom-call(f32[512,128]{1,0:T(8,128)S(1)} %get-tuple-element.20.own_first, f32[272,128]{1,0:T(8,128)S(1)} %get-tuple-element.21.own_rest, f32[752,128]{1,0:T(8,128)S(1)} %collective-permute-done.other, f32[20,2,8,128]{3,2,1,0:T(8,128)S(1)} %get-tuple-element.23.h_in, ...), custom_call_target="tpu_custom_call" | custom-call | flops 1048576 | bytes 1048576 | tf_op jit(solution)/shard_map/pallas_call | solution.py:518
  28.9 18.6 %all_to_all.22 = f32[32,4,128]{2,1,0:T(4,128)S(1)} all-to-all(f32[32,4,128]{2,1,0:T(4,128)S(1)} %bitcast.12), channel_id=1, replica_groups=mesh['zl'=4,'x'=4,'zh'=4,'y'=4,'c'=2] {'x','y','c'}, dimensions={0} | all-to-all | bytes 131072 | tf_op jit(solution)/shard_map/all_to_all | solution.py:532
  47.5 8.8 %collective-permute-start.4 = (f32[56,128]{1,0:T(8,128)S(1)}, f32[56,128]{1,0:T(8,128)S(1)}, u32[]{:S(2)}, u32[]{:S(2)}) collective-permute-start(f32[56,128]{1,0:T(8,128)S(1)} %shard_map.59), channel_id=1, source_target_pairs={{0,8},{8,0},{16,24},{24,16},{1,9},{9,1},{17,25},{25,17},{2,10},{10... | collective-permute-start | bytes 86024 | tf_op jit(solution)/shard_map/ppermute | solution.py:568
  56.4 2.5 %collective-permute-done.4 = f32[56,128]{1,0:T(8,128)S(1)} collective-permute-done((f32[56,128]{1,0:T(8,128)S(1)}, f32[56,128]{1,0:T(8,128)S(1)}, u32[]{:S(2)}, u32[]{:S(2)}) %collective-permute-start.4) | collective-permute-done | bytes 28704 | tf_op jit(solution)/shard_map/ppermute | solution.py:568
  58.9 7.6 %collective-permute-start.5 = (f32[112,128]{1,0:T(8,128)S(1)}, f32[112,128]{1,0:T(8,128)S(1)}, u32[]{:S(2)}, u32[]{:S(2)}) collective-permute-start(f32[112,128]{1,0:T(8,128)S(1)} %pad_maximum_fusion.half), channel_id=1, source_target_pairs={{0,24},{8,16},{16,8},{24,0},{1,25},{9,17},{17,9},{25,1},{2,26},{10... | collective-permute-start | bytes 172040 | tf_op jit(solution)/shard_map/ppermute | solution.py:570
  66.4 1.9 %collective-permute-done.5.other_half = f32[112,128]{1,0:T(8,128)S(1)} collective-permute-done((f32[112,128]{1,0:T(8,128)S(1)}, f32[112,128]{1,0:T(8,128)S(1)}, u32[]{:S(2)}, u32[]{:S(2)}) %collective-permute-start.5) | collective-permute-done | bytes 57376 | tf_op jit(solution)/shard_map/ppermute | solution.py:570
  68.8 4.9 %collective-permute-start.6 = (f32[96,128]{1,0:T(8,128)S(1)}, f32[96,128]{1,0:T(8,128)S(1)}, u32[]{:S(2)}, u32[]{:S(2)}) collective-permute-start(f32[96,128]{1,0:T(8,128)S(1)} %get-tuple-element.32.total), channel_id=1, source_target_pairs={{0,1},{1,0},{2,3},{3,2},{4,5},{5,4},{6,7},{7,6},{8,9},{9,8},{10,11... | collective-permute-start | bytes 147464 | tf_op jit(solution)/shard_map/ppermute | solution.py:574
  73.7 0.9 collective-permute-done.6.mate
  74.6 0.7 shard_map.61
  75.3 4.6 %collective-permute-start.9 = (f32[96,128]{1,0:T(8,128)S(1)}, f32[96,128]{1,0:T(8,128)S(1)}, u32[]{:S(2)}, u32[]{:S(2)}) collective-permute-start(f32[96,128]{1,0:T(8,128)S(1)} %shard_map.61), channel_id=1, source_target_pairs={{0,384},{1,385},{2,386},{3,387},{4,388},{5,389},{6,390},{7,391},{8... | collective-permute-start | bytes 147464 | tf_op jit(solution)/shard_map/ppermute | solution.py:577
  79.8 1.3 %collective-permute-start.8 = (f32[96,128]{1,0:T(8,128)S(1)}, f32[96,128]{1,0:T(8,128)S(1)}, u32[]{:S(2)}, u32[]{:S(2)}) collective-permute-start(f32[96,128]{1,0:T(8,128)S(1)} %shard_map.61), channel_id=1, source_target_pairs={{0,256},{128,384},{1,257},{129,385},{2,258},{130,386},{3,259},{131... | collective-permute-start | bytes 147464 | tf_op jit(solution)/shard_map/ppermute | solution.py:577
  81.1 2.2 %collective-permute-start.7 = (f32[96,128]{1,0:T(8,128)S(1)}, f32[96,128]{1,0:T(8,128)S(1)}, u32[]{:S(2)}, u32[]{:S(2)}) collective-permute-start(f32[96,128]{1,0:T(8,128)S(1)} %shard_map.61), channel_id=1, source_target_pairs={{0,128},{128,256},{256,384},{1,129},{129,257},{257,385},{2,130},{1... | collective-permute-start | bytes 147464 | tf_op jit(solution)/shard_map/ppermute | solution.py:577
  83.4 1.1 %collective-permute-done.7.one = f32[96,128]{1,0:T(8,128)S(1)} collective-permute-done((f32[96,128]{1,0:T(8,128)S(1)}, f32[96,128]{1,0:T(8,128)S(1)}, u32[]{:S(2)}, u32[]{:S(2)}) %collective-permute-start.7) | collective-permute-done | bytes 49184 | tf_op jit(solution)/shard_map/ppermute | solution.py:577
  84.5 1.4 %shard_map.63 = f32[128,128]{1,0:T(8,128)S(1)} custom-call(f32[96,128]{1,0:T(8,128)S(1)} %collective-permute-done.7.one, f32[96,128]{1,0:T(8,128)S(1)} %collective-permute-done.8.two, f32[96,128]{1,0:T(8,128)S(1)} %shard_map.62.earlier, f32[96,128]{1,0:T(8,128)S(1)} %collective-permute-done.6.mate, f32[192,128]{1,0:T(8,128)S(1)} %get-tuple-element.34.jumps, ...), custom_call_target="tpu_custom_call" | custom-call | flops 1048576 | bytes 1048576 | tf_op jit(solution)/shard_map/pallas_call | solution.py:518
  85.9 11.2 %all_to_all.23 = f32[32,4,128]{2,1,0:T(4,128)S(1)} all-to-all(f32[32,4,128]{2,1,0:T(4,128)S(1)} %bitcast.11), channel_id=1, replica_groups=mesh['zl'=4,'x'=4,'zh'=4,'y'=4,'c'=2] {'x','y','c'}, dimensions={0} | all-to-all | bytes 131072 | tf_op jit(solution)/shard_map/all_to_all | solution.py:532
  97.2 1.0 %shard_map.64 = f32[768,128]{1,0:T(8,128)} custom-call(f32[48,16,128]{2,1,0:T(8,128)S(1)} %get-tuple-element.29.fine, f32[128,128]{1,0:T(8,128)S(1)} %bitcast.9, f32[16,128]{1,0:T(8,128)S(1)} %get-tuple-element.27.vectors, f32[1,16]{1,0:T(1,128)S(1)} %bitcast.21), custom_call_target="tpu_custom_call" | custom-call | flops 1048576 | bytes 1048576 | tf_op jit(solution)/shard_map/pallas_call | solution.py:518
  (18 shorter events, 1.7 us)
Async XLA Ops:
  0.7 1.0 %copy-start = (f32[1,3,16,16,128]{4,3,2,1,0:T(8,128)S(1)}, f32[1,3,16,16,128]{4,3,2,1,0:T(8,128)}, u32[]{:S(2)}) copy-start(f32[1,3,16,16,128]{4,3,2,1,0:T(8,128)} %param.5) | copy-start | bytes 1179652
  2.3 12.7 %copy-start.1 = (f32[16,16]{1,0:T(8,128)S(1)}, f32[16,16]{1,0:T(8,128)}, u32[]{:S(2)}) copy-start(f32[16,16]{1,0:T(8,128)} %coupling.5) | copy-start | bytes 3076
  2.3 23.8 %collective-permute-start = (f32[752,128]{1,0:T(8,128)S(1)}, f32[752,128]{1,0:T(8,128)S(1)}, u32[]{:S(2)}, u32[]{:S(2)}) collective-permute-start(f32[752,128]{1,0:T(8,128)S(1)} %get-tuple-element.22), channel_id=1, source_target_pairs={{1,2},{3,4},{5,6},{7,8},{9,10},{11,12},{13,14},{15,16},{17,18},{19... | collective-permute-start | bytes 1155080 | tf_op jit(solution)/shard_map/ppermute | solution.py:546
  6.9 15.9 %collective-permute-start.1 = (f32[512,128]{1,0:T(8,128)S(1)}, f32[512,128]{1,0:T(8,128)S(1)}, u32[]{:S(2)}, u32[]{:S(2)}) collective-permute-start(f32[512,128]{1,0:T(8,128)S(1)} %get-tuple-element.20.own_first), channel_id=1, source_target_pairs={{0,1},{1,0},{2,3},{3,2},{4,5},{5,4},{6,7},{7,6},{8,9},{9,8},{10,11... | collective-permute-start | bytes 786440 | tf_op jit(solution)/shard_map/ppermute | solution.py:552
  11.8 11.0 %collective-permute-start.2 = (f32[272,128]{1,0:T(8,128)S(1)}, f32[272,128]{1,0:T(8,128)S(1)}, u32[]{:S(2)}, u32[]{:S(2)}) collective-permute-start(f32[272,128]{1,0:T(8,128)S(1)} %get-tuple-element.21.own_rest), channel_id=1, source_target_pairs={{0,1},{1,0},{2,3},{3,2},{4,5},{5,4},{6,7},{7,6},{8,9},{9,8},{10,11... | collective-permute-start | bytes 417800 | tf_op jit(solution)/shard_map/ppermute | solution.py:552
  13.7 1.3 %copy-start.3 = (f32[16]{0:T(128)S(1)}, f32[16]{0:T(128)}, u32[]{:S(2)}) copy-start(f32[16]{0:T(128)} %param.9) | copy-start | bytes 196
  13.7 12.3 %collective-permute-start.3 = (f32[48,128]{1,0:T(8,128)S(1)}, f32[48,128]{1,0:T(8,128)S(1)}, u32[]{:S(2)}, u32[]{:S(2)}) collective-permute-start(f32[48,128]{1,0:T(8,128)S(1)} %get-tuple-element.28), channel_id=1, source_target_pairs={{32,0},{64,32},{96,64},{128,96},{160,128},{192,160},{224,192},{256... | collective-permute-start | bytes 73736 | tf_op jit(solution)/shard_map/ppermute | solution.py:547
  22.8 0.7 copy-start.2
  47.5 11.3 %collective-permute-start.4 = (f32[56,128]{1,0:T(8,128)S(1)}, f32[56,128]{1,0:T(8,128)S(1)}, u32[]{:S(2)}, u32[]{:S(2)}) collective-permute-start(f32[56,128]{1,0:T(8,128)S(1)} %shard_map.59), channel_id=1, source_target_pairs={{0,8},{8,0},{16,24},{24,16},{1,9},{9,1},{17,25},{25,17},{2,10},{10... | collective-permute-start | bytes 86024 | tf_op jit(solution)/shard_map/ppermute | solution.py:568
  58.9 9.5 %collective-permute-start.5 = (f32[112,128]{1,0:T(8,128)S(1)}, f32[112,128]{1,0:T(8,128)S(1)}, u32[]{:S(2)}, u32[]{:S(2)}) collective-permute-start(f32[112,128]{1,0:T(8,128)S(1)} %pad_maximum_fusion.half), channel_id=1, source_target_pairs={{0,24},{8,16},{16,8},{24,0},{1,25},{9,17},{17,9},{25,1},{2,26},{10... | collective-permute-start | bytes 172040 | tf_op jit(solution)/shard_map/ppermute | solution.py:570
  68.8 5.8 %collective-permute-start.6 = (f32[96,128]{1,0:T(8,128)S(1)}, f32[96,128]{1,0:T(8,128)S(1)}, u32[]{:S(2)}, u32[]{:S(2)}) collective-permute-start(f32[96,128]{1,0:T(8,128)S(1)} %get-tuple-element.32.total), channel_id=1, source_target_pairs={{0,1},{1,0},{2,3},{3,2},{4,5},{5,4},{6,7},{7,6},{8,9},{9,8},{10,11... | collective-permute-start | bytes 147464 | tf_op jit(solution)/shard_map/ppermute | solution.py:574
  75.3 8.1 %collective-permute-start.9 = (f32[96,128]{1,0:T(8,128)S(1)}, f32[96,128]{1,0:T(8,128)S(1)}, u32[]{:S(2)}, u32[]{:S(2)}) collective-permute-start(f32[96,128]{1,0:T(8,128)S(1)} %shard_map.61), channel_id=1, source_target_pairs={{0,384},{1,385},{2,386},{3,387},{4,388},{5,389},{6,390},{7,391},{8... | collective-permute-start | bytes 147464 | tf_op jit(solution)/shard_map/ppermute | solution.py:577
  79.8 3.6 %collective-permute-start.8 = (f32[96,128]{1,0:T(8,128)S(1)}, f32[96,128]{1,0:T(8,128)S(1)}, u32[]{:S(2)}, u32[]{:S(2)}) collective-permute-start(f32[96,128]{1,0:T(8,128)S(1)} %shard_map.61), channel_id=1, source_target_pairs={{0,256},{128,384},{1,257},{129,385},{2,258},{130,386},{3,259},{131... | collective-permute-start | bytes 147464 | tf_op jit(solution)/shard_map/ppermute | solution.py:577
  81.1 3.4 %collective-permute-start.7 = (f32[96,128]{1,0:T(8,128)S(1)}, f32[96,128]{1,0:T(8,128)S(1)}, u32[]{:S(2)}, u32[]{:S(2)}) collective-permute-start(f32[96,128]{1,0:T(8,128)S(1)} %shard_map.61), channel_id=1, source_target_pairs={{0,128},{128,256},{256,384},{1,129},{129,257},{257,385},{2,130},{1... | collective-permute-start | bytes 147464 | tf_op jit(solution)/shard_map/ppermute | solution.py:577

commit v6 on v5

--- a/solution.py
+++ b/solution.py
@@ -411,7 +411,7 @@
 def pair_kernel(half, other_half, values, fold, jumps, mask_out, total):
     seg = iota((8, ZONAL), 1) % 4
     zh = lax.axis_index("zh")
-    quarters = [(half, 0, zh), (half, PARTS * 8, zh ^ 1), (other_half, 0, zh ^ 3), (other_half, PARTS * 8, zh ^ 2)]
+    quarters = [(half, 0, zh), (half, PARTS * 8, zh ^ 3), (other_half, 0, zh ^ 1), (other_half, PARTS * 8, zh ^ 2)]
     for part in range(PARTS):
         rows = [None] * 4
         for ref, begin, quarter in quarters:
@@ -565,9 +565,9 @@
 
     spread = swap(chunk, PLANE)
     (mine,) = call(collect_kernel, [(PARTS * 8, ZONAL)])(spread)
-    beside = lax.ppermute(mine, ("zh",), [(i, i ^ 1) for i in range(4)])
+    beside = lax.ppermute(mine, ("zh",), [(i, i ^ 3) for i in range(4)])
     half = jnp.concatenate([mine, beside], axis=0)
-    other_half = lax.ppermute(half, ("zh",), [(i, i ^ 3) for i in range(4)])
+    other_half = lax.ppermute(half, ("zh",), [(i, i ^ 1) for i in range(4)])
     jumps, mask, total = call(
         pair_kernel, [(192, ZONAL), (32, ZONAL), (96, ZONAL)]
     )(half, other_half, values, fold)

time: 98.7 us -> 96.7 us (0.980)
  blocking collectives: 29.9 us -> 31.5 us
  starting transfers between devices: 42.1 us -> 40.6 us
  Pallas kernels: 17.4 us -> 15.9 us
  waiting for transfers between devices: 6.39 us -> 5.38 us
    ppermute x3, starting transfers between devices: 8.07 us -> 5.72 us  [body(): lax.ppermute(both, ('zl',), [(i, i + d) for i in range(4 - d)])]
    all_to_all x2, blocking collectives: 29.9 us -> 31.5 us  [swap(): return lax.all_to_all(block, axes, 0, 0, tiled=True)]
    pallas_call x10, Pallas kernels: 17.4 us -> 15.9 us  [run(): pl.pallas_call(kernel, out_shape=[jax.ShapeDtypeStruct(s, F32) for s in o...]
    ppermute x2, starting transfers between devices: 16.4 us -> 17.6 us  [the longest x1 9.54 us: body(): other_half = lax.ppermute(half, ('zh',), [(i, i ^ 1) for i in range(4)])]
    ppermute x2, waiting for transfers between devices: 4.44 us -> 3.43 us  [the longest x1 2.17 us: body(): other_half = lax.ppermute(half, ('zh',), [(i, i ^ 1) for i in range(4)])]
  transfers between devices with their start and end apart: 10 -> 10, of which waited for: 4 -> 4; matrix products, arithmetic and copies ran while one was open for 0% -> 0% of each run, Pallas kernels for 11% -> 9%
where the time goes in v6:
time: 96.7 us; the launch traced here: 95.9 us
  starting transfers between devices  40.6 us (42%)
  blocking collectives  31.5 us (33%)
  Pallas kernels  15.9 us (16%)
  waiting for transfers between devices  5.38 us (6%)
  local copies, waits for them, and re-layouts  1.65 us (2%)
    all_to_all x2, blocking collectives, swap(): return lax.all_to_all(block, axes, 0, 0, tiled=True)  31.5 us
    pallas_call x10, Pallas kernels, run(): pl.pallas_call(kernel, out_shape=[jax.ShapeDtypeStruct(s, F32) for s in o...  15.9 us
    ppermute x1, starting transfers between devices, body(): other_half = lax.ppermute(half, ('zh',), [(i, i ^ 1) for i in range(4)])  9.54 us
    ppermute x1, starting transfers between devices, body(): beside = lax.ppermute(mine, ('zh',), [(i, i ^ 3) for i in range(4)])  8.06 us
    ppermute x2, starting transfers between devices, body(): mate = [lax.ppermute(part, SPACE, inside) for part in (first, rest)]  6.8 us
    ppermute x3, starting transfers between devices, body(): lax.ppermute(both, ('zl',), [(i, i + d) for i in range(4 - d)])  5.72 us
    ppermute x1, starting transfers between devices, body(): other = lax.ppermute(sent, SPACE, across)  4.59 us
    ppermute x1, starting transfers between devices, body(): mate = lax.ppermute(total, ('c',), [(0, 1), (1, 0)])  4.58 us
  transfers between devices with their start and end apart: 10, of which 4 were waited for; matrix products, arithmetic and copies ran while one was open for 0% of the time, Pallas kernels for 9%

profile of v6, /device:TPU:1, one launch (start us, length us, event | category | flops | bytes accessed | tf_op | source)
XLA Modules:
  0.0 95.9 jit_solution(6701181091815338953)
XLA Ops:
  0.0 0.7 convert_element_type.3.mask
  0.7 1.0 %copy-done = f32[1,3,16,16,128]{4,3,2,1,0:T(8,128)S(1)} copy-done((f32[1,3,16,16,128]{4,3,2,1,0:T(8,128)S(1)}, f32[1,3,16,16,128]{4,3,2,1,0:T(8,128)}, u32[]{:S(2)}) %copy-start) | copy-done | bytes 393240
  2.3 4.6 %collective-permute-start = (f32[752,128]{1,0:T(8,128)S(1)}, f32[752,128]{1,0:T(8,128)S(1)}, u32[]{:S(2)}, u32[]{:S(2)}) collective-permute-start(f32[752,128]{1,0:T(8,128)S(1)} %get-tuple-element.22), channel_id=1, source_target_pairs={{1,2},{3,4},{5,6},{7,8},{9,10},{11,12},{13,14},{15,16},{17,18},{19... | collective-permute-start | bytes 1155080 | tf_op jit(solution)/shard_map/ppermute | solution.py:546
  6.9 4.9 %collective-permute-start.1 = (f32[512,128]{1,0:T(8,128)S(1)}, f32[512,128]{1,0:T(8,128)S(1)}, u32[]{:S(2)}, u32[]{:S(2)}) collective-permute-start(f32[512,128]{1,0:T(8,128)S(1)} %get-tuple-element.20.own_first), channel_id=1, source_target_pairs={{0,1},{1,0},{2,3},{3,2},{4,5},{5,4},{6,7},{7,6},{8,9},{9,8},{10,11... | collective-permute-start | bytes 786440 | tf_op jit(solution)/shard_map/ppermute | solution.py:552
  11.8 1.9 %collective-permute-start.2 = (f32[272,128]{1,0:T(8,128)S(1)}, f32[272,128]{1,0:T(8,128)S(1)}, u32[]{:S(2)}, u32[]{:S(2)}) collective-permute-start(f32[272,128]{1,0:T(8,128)S(1)} %get-tuple-element.21.own_rest), channel_id=1, source_target_pairs={{0,1},{1,0},{2,3},{3,2},{4,5},{5,4},{6,7},{7,6},{8,9},{9,8},{10,11... | collective-permute-start | bytes 417800 | tf_op jit(solution)/shard_map/ppermute | solution.py:552
  13.7 1.3 %collective-permute-start.3 = (f32[48,128]{1,0:T(8,128)S(1)}, f32[48,128]{1,0:T(8,128)S(1)}, u32[]{:S(2)}, u32[]{:S(2)}) collective-permute-start(f32[48,128]{1,0:T(8,128)S(1)} %get-tuple-element.28), channel_id=1, source_target_pairs={{32,0},{64,32},{96,64},{128,96},{160,128},{192,160},{224,192},{256... | collective-permute-start | bytes 73736 | tf_op jit(solution)/shard_map/ppermute | solution.py:547
  15.1 6.2 %shard_map.57 = (f32[16,128]{1,0:T(8,128)S(1)}, f32[16,128]{1,0:T(8,128)S(1)}) custom-call(f32[16,16]{1,0:T(8,128)S(1)} %copy-done.1, f32[1,16]{1,0:T(1,128)S(1)} %bitcast.18), custom_call_target="tpu_custom_call" | custom-call | flops 10485760 | bytes 1048576 | tf_op jit(solution)/shard_map/pallas_call | solution.py:518
  22.0 2.6 %shard_map.56 = (f32[20,2,8,128]{3,2,1,0:T(8,128)S(1)}, f32[20,2,8,128]{3,2,1,0:T(8,128)S(1)}, f32[20,2,8,128]{3,2,1,0:T(8,128)S(1)}, f32[1,128]{1,0:T(1,128)S(1)}) custom-call(f32[512,128]{1,0:T(8,128)S(1)} %get-tuple-element.20.own_first, f32[272,128]{1,0:T(8,128)S(1)} %get-tuple-element.21.own_rest, f32[512,128]{1,0:T(8,128)S(1)} %collective-permute-done.1.mate_first, ...), custom_call_target="tpu_custom_call" | custom-call | flops 4194304 | bytes 1048576 | tf_op jit(solution)/shard_map/pallas_call | solution.py:518
  24.6 2.8 %shard_map.58 = (f32[48,16,128]{2,1,0:T(8,128)S(1)}, f32[128,128]{1,0:T(8,128)S(1)}) custom-call(f32[512,128]{1,0:T(8,128)S(1)} %get-tuple-element.20.own_first, f32[272,128]{1,0:T(8,128)S(1)} %get-tuple-element.21.own_rest, f32[752,128]{1,0:T(8,128)S(1)} %collective-permute-done.other, f32[20,2,8,128]{3,2,1,0:T(8,128)S(1)} %get-tuple-element.23.h_in, ...), custom_call_target="tpu_custom_call" | custom-call | flops 1048576 | bytes 1048576 | tf_op jit(solution)/shard_map/pallas_call | solution.py:518
  27.4 20.1 %all_to_all.22 = f32[32,4,128]{2,1,0:T(4,128)S(1)} all-to-all(f32[32,4,128]{2,1,0:T(4,128)S(1)} %bitcast.12), channel_id=1, replica_groups=mesh['zl'=4,'x'=4,'zh'=4,'y'=4,'c'=2] {'x','y','c'}, dimensions={0} | all-to-all | bytes 131072 | tf_op jit(solution)/shard_map/all_to_all | solution.py:532
  47.5 8.1 %collective-permute-start.4 = (f32[56,128]{1,0:T(8,128)S(1)}, f32[56,128]{1,0:T(8,128)S(1)}, u32[]{:S(2)}, u32[]{:S(2)}) collective-permute-start(f32[56,128]{1,0:T(8,128)S(1)} %shard_map.59), channel_id=1, source_target_pairs={{0,24},{8,16},{16,8},{24,0},{1,25},{9,17},{17,9},{25,1},{2,26},{10... | collective-permute-start | bytes 86024 | tf_op jit(solution)/shard_map/ppermute | solution.py:568
  55.6 1.3 %collective-permute-done.4 = f32[56,128]{1,0:T(8,128)S(1)} collective-permute-done((f32[56,128]{1,0:T(8,128)S(1)}, f32[56,128]{1,0:T(8,128)S(1)}, u32[]{:S(2)}, u32[]{:S(2)}) %collective-permute-start.4) | collective-permute-done | bytes 28704 | tf_op jit(solution)/shard_map/ppermute | solution.py:568
  56.9 9.5 %collective-permute-start.5 = (f32[112,128]{1,0:T(8,128)S(1)}, f32[112,128]{1,0:T(8,128)S(1)}, u32[]{:S(2)}, u32[]{:S(2)}) collective-permute-start(f32[112,128]{1,0:T(8,128)S(1)} %pad_maximum_fusion.half), channel_id=1, source_target_pairs={{0,8},{8,0},{16,24},{24,16},{1,9},{9,1},{17,25},{25,17},{2,10},{10... | collective-permute-start | bytes 172040 | tf_op jit(solution)/shard_map/ppermute | solution.py:570
  66.4 2.2 %collective-permute-done.5.other_half = f32[112,128]{1,0:T(8,128)S(1)} collective-permute-done((f32[112,128]{1,0:T(8,128)S(1)}, f32[112,128]{1,0:T(8,128)S(1)}, u32[]{:S(2)}, u32[]{:S(2)}) %collective-permute-start.5) | collective-permute-done | bytes 57376 | tf_op jit(solution)/shard_map/ppermute | solution.py:570
  69.0 4.6 %collective-permute-start.6 = (f32[96,128]{1,0:T(8,128)S(1)}, f32[96,128]{1,0:T(8,128)S(1)}, u32[]{:S(2)}, u32[]{:S(2)}) collective-permute-start(f32[96,128]{1,0:T(8,128)S(1)} %get-tuple-element.32.total), channel_id=1, source_target_pairs={{0,1},{1,0},{2,3},{3,2},{4,5},{5,4},{6,7},{7,6},{8,9},{9,8},{10,11... | collective-permute-start | bytes 147464 | tf_op jit(solution)/shard_map/ppermute | solution.py:574
  73.6 0.9 collective-permute-done.6.mate
  74.4 0.7 shard_map.61
  75.1 2.2 %collective-permute-start.9 = (f32[96,128]{1,0:T(8,128)S(1)}, f32[96,128]{1,0:T(8,128)S(1)}, u32[]{:S(2)}, u32[]{:S(2)}) collective-permute-start(f32[96,128]{1,0:T(8,128)S(1)} %shard_map.61), channel_id=1, source_target_pairs={{0,384},{1,385},{2,386},{3,387},{4,388},{5,389},{6,390},{7,391},{8... | collective-permute-start | bytes 147464 | tf_op jit(solution)/shard_map/ppermute | solution.py:577
  77.4 1.3 %collective-permute-start.8 = (f32[96,128]{1,0:T(8,128)S(1)}, f32[96,128]{1,0:T(8,128)S(1)}, u32[]{:S(2)}, u32[]{:S(2)}) collective-permute-start(f32[96,128]{1,0:T(8,128)S(1)} %shard_map.61), channel_id=1, source_target_pairs={{0,256},{128,384},{1,257},{129,385},{2,258},{130,386},{3,259},{131... | collective-permute-start | bytes 147464 | tf_op jit(solution)/shard_map/ppermute | solution.py:577
  78.7 2.2 %collective-permute-start.7 = (f32[96,128]{1,0:T(8,128)S(1)}, f32[96,128]{1,0:T(8,128)S(1)}, u32[]{:S(2)}, u32[]{:S(2)}) collective-permute-start(f32[96,128]{1,0:T(8,128)S(1)} %shard_map.61), channel_id=1, source_target_pairs={{0,128},{128,256},{256,384},{1,129},{129,257},{257,385},{2,130},{1... | collective-permute-start | bytes 147464 | tf_op jit(solution)/shard_map/ppermute | solution.py:577
  81.0 1.1 %collective-permute-done.7.one = f32[96,128]{1,0:T(8,128)S(1)} collective-permute-done((f32[96,128]{1,0:T(8,128)S(1)}, f32[96,128]{1,0:T(8,128)S(1)}, u32[]{:S(2)}, u32[]{:S(2)}) %collective-permute-start.7) | collective-permute-done | bytes 49184 | tf_op jit(solution)/shard_map/ppermute | solution.py:577
  82.0 1.4 %shard_map.63 = f32[128,128]{1,0:T(8,128)S(1)} custom-call(f32[96,128]{1,0:T(8,128)S(1)} %collective-permute-done.7.one, f32[96,128]{1,0:T(8,128)S(1)} %collective-permute-done.8.two, f32[96,128]{1,0:T(8,128)S(1)} %shard_map.62.earlier, f32[96,128]{1,0:T(8,128)S(1)} %collective-permute-done.6.mate, f32[192,128]{1,0:T(8,128)S(1)} %get-tuple-element.34.jumps, ...), custom_call_target="tpu_custom_call" | custom-call | flops 1048576 | bytes 1048576 | tf_op jit(solution)/shard_map/pallas_call | solution.py:518
  83.5 11.3 %all_to_all.23 = f32[32,4,128]{2,1,0:T(4,128)S(1)} all-to-all(f32[32,4,128]{2,1,0:T(4,128)S(1)} %bitcast.11), channel_id=1, replica_groups=mesh['zl'=4,'x'=4,'zh'=4,'y'=4,'c'=2] {'x','y','c'}, dimensions={0} | all-to-all | bytes 131072 | tf_op jit(solution)/shard_map/all_to_all | solution.py:532
  94.8 1.0 %shard_map.64 = f32[768,128]{1,0:T(8,128)} custom-call(f32[48,16,128]{2,1,0:T(8,128)S(1)} %get-tuple-element.29.fine, f32[128,128]{1,0:T(8,128)S(1)} %bitcast.9, f32[16,128]{1,0:T(8,128)S(1)} %get-tuple-element.27.vectors, f32[1,16]{1,0:T(1,128)S(1)} %bitcast.21), custom_call_target="tpu_custom_call" | custom-call | flops 1048576 | bytes 1048576 | tf_op jit(solution)/shard_map/pallas_call | solution.py:518
  (18 shorter events, 1.7 us)
Async XLA Ops:
  0.7 1.0 %copy-start = (f32[1,3,16,16,128]{4,3,2,1,0:T(8,128)S(1)}, f32[1,3,16,16,128]{4,3,2,1,0:T(8,128)}, u32[]{:S(2)}) copy-start(f32[1,3,16,16,128]{4,3,2,1,0:T(8,128)} %param.5) | copy-start | bytes 1179652
  2.3 12.7 %copy-start.1 = (f32[16,16]{1,0:T(8,128)S(1)}, f32[16,16]{1,0:T(8,128)}, u32[]{:S(2)}) copy-start(f32[16,16]{1,0:T(8,128)} %coupling.5) | copy-start | bytes 3076
  2.3 22.3 %collective-permute-start = (f32[752,128]{1,0:T(8,128)S(1)}, f32[752,128]{1,0:T(8,128)S(1)}, u32[]{:S(2)}, u32[]{:S(2)}) collective-permute-start(f32[752,128]{1,0:T(8,128)S(1)} %get-tuple-element.22), channel_id=1, source_target_pairs={{1,2},{3,4},{5,6},{7,8},{9,10},{11,12},{13,14},{15,16},{17,18},{19... | collective-permute-start | bytes 1155080 | tf_op jit(solution)/shard_map/ppermute | solution.py:546
  6.9 14.4 %collective-permute-start.1 = (f32[512,128]{1,0:T(8,128)S(1)}, f32[512,128]{1,0:T(8,128)S(1)}, u32[]{:S(2)}, u32[]{:S(2)}) collective-permute-start(f32[512,128]{1,0:T(8,128)S(1)} %get-tuple-element.20.own_first), channel_id=1, source_target_pairs={{0,1},{1,0},{2,3},{3,2},{4,5},{5,4},{6,7},{7,6},{8,9},{9,8},{10,11... | collective-permute-start | bytes 786440 | tf_op jit(solution)/shard_map/ppermute | solution.py:552
  11.8 9.5 %collective-permute-start.2 = (f32[272,128]{1,0:T(8,128)S(1)}, f32[272,128]{1,0:T(8,128)S(1)}, u32[]{:S(2)}, u32[]{:S(2)}) collective-permute-start(f32[272,128]{1,0:T(8,128)S(1)} %get-tuple-element.21.own_rest), channel_id=1, source_target_pairs={{0,1},{1,0},{2,3},{3,2},{4,5},{5,4},{6,7},{7,6},{8,9},{9,8},{10,11... | collective-permute-start | bytes 417800 | tf_op jit(solution)/shard_map/ppermute | solution.py:552
  13.7 1.3 %copy-start.3 = (f32[16]{0:T(128)S(1)}, f32[16]{0:T(128)}, u32[]{:S(2)}) copy-start(f32[16]{0:T(128)} %param.9) | copy-start | bytes 196
  13.7 10.8 %collective-permute-start.3 = (f32[48,128]{1,0:T(8,128)S(1)}, f32[48,128]{1,0:T(8,128)S(1)}, u32[]{:S(2)}, u32[]{:S(2)}) collective-permute-start(f32[48,128]{1,0:T(8,128)S(1)} %get-tuple-element.28), channel_id=1, source_target_pairs={{32,0},{64,32},{96,64},{128,96},{160,128},{192,160},{224,192},{256... | collective-permute-start | bytes 73736 | tf_op jit(solution)/shard_map/ppermute | solution.py:547
  21.3 0.7 copy-start.2
  47.5 9.3 %collective-permute-start.4 = (f32[56,128]{1,0:T(8,128)S(1)}, f32[56,128]{1,0:T(8,128)S(1)}, u32[]{:S(2)}, u32[]{:S(2)}) collective-permute-start(f32[56,128]{1,0:T(8,128)S(1)} %shard_map.59), channel_id=1, source_target_pairs={{0,24},{8,16},{16,8},{24,0},{1,25},{9,17},{17,9},{25,1},{2,26},{10... | collective-permute-start | bytes 86024 | tf_op jit(solution)/shard_map/ppermute | solution.py:568
  56.9 11.7 %collective-permute-start.5 = (f32[112,128]{1,0:T(8,128)S(1)}, f32[112,128]{1,0:T(8,128)S(1)}, u32[]{:S(2)}, u32[]{:S(2)}) collective-permute-start(f32[112,128]{1,0:T(8,128)S(1)} %pad_maximum_fusion.half), channel_id=1, source_target_pairs={{0,8},{8,0},{16,24},{24,16},{1,9},{9,1},{17,25},{25,17},{2,10},{10... | collective-permute-start | bytes 172040 | tf_op jit(solution)/shard_map/ppermute | solution.py:570
  69.0 5.4 %collective-permute-start.6 = (f32[96,128]{1,0:T(8,128)S(1)}, f32[96,128]{1,0:T(8,128)S(1)}, u32[]{:S(2)}, u32[]{:S(2)}) collective-permute-start(f32[96,128]{1,0:T(8,128)S(1)} %get-tuple-element.32.total), channel_id=1, source_target_pairs={{0,1},{1,0},{2,3},{3,2},{4,5},{5,4},{6,7},{7,6},{8,9},{9,8},{10,11... | collective-permute-start | bytes 147464 | tf_op jit(solution)/shard_map/ppermute | solution.py:574
  75.1 5.7 %collective-permute-start.9 = (f32[96,128]{1,0:T(8,128)S(1)}, f32[96,128]{1,0:T(8,128)S(1)}, u32[]{:S(2)}, u32[]{:S(2)}) collective-permute-start(f32[96,128]{1,0:T(8,128)S(1)} %shard_map.61), channel_id=1, source_target_pairs={{0,384},{1,385},{2,386},{3,387},{4,388},{5,389},{6,390},{7,391},{8... | collective-permute-start | bytes 147464 | tf_op jit(solution)/shard_map/ppermute | solution.py:577
  77.4 3.6 %collective-permute-start.8 = (f32[96,128]{1,0:T(8,128)S(1)}, f32[96,128]{1,0:T(8,128)S(1)}, u32[]{:S(2)}, u32[]{:S(2)}) collective-permute-start(f32[96,128]{1,0:T(8,128)S(1)} %shard_map.61), channel_id=1, source_target_pairs={{0,256},{128,384},{1,257},{129,385},{2,258},{130,386},{3,259},{131... | collective-permute-start | bytes 147464 | tf_op jit(solution)/shard_map/ppermute | solution.py:577
  78.7 3.4 %collective-permute-start.7 = (f32[96,128]{1,0:T(8,128)S(1)}, f32[96,128]{1,0:T(8,128)S(1)}, u32[]{:S(2)}, u32[]{:S(2)}) collective-permute-start(f32[96,128]{1,0:T(8,128)S(1)} %shard_map.61), channel_id=1, source_target_pairs={{0,128},{128,256},{256,384},{1,129},{129,257},{257,385},{2,130},{1... | collective-permute-start | bytes 147464 | tf_op jit(solution)/shard_map/ppermute | solution.py:577

commit v7 on v6

--- a/solution.py
+++ b/solution.py
@@ -399,13 +399,10 @@
 
 
 def collect_kernel(spread, out):
-    for core in range(2):
-
-        @pl.when(core_index() == core)
-        def _():
-            for part in range(PARTS):
-                at = core * 64 + part + (28 if part > 3 else 0)
-                out[part * 8 : part * 8 + 8, :] = spread[pl.ds(at, 8, stride=4), :]
+    for part in range(PARTS):
+        at = part + (28 if part > 3 else 0)
+        both = [spread[pl.ds(core * 64 + at, 8, stride=4), :] for core in range(2)]
+        out[part * 8 : part * 8 + 8, :] = jnp.where(core_index() == 0, both[0], both[1])
 
 
 def pair_kernel(half, other_half, values, fold, jumps, mask_out, total):
@@ -472,12 +469,8 @@
             for cr in range(1, 4):
                 packed[f] = jnp.where(seg == cr, pieces[cr], packed[f])
         for which in range(2):
-
-            @pl.when(core == which)
-            def _():
-                for f in range(3):
-                    chunk[pl.ds((2 * which + x) * 32 + f, 8, stride=4), :] = packed[f]
-
+            for f in range(3):
+                chunk[pl.ds((2 * which + x) * 32 + f, 8, stride=4), :] = jnp.where(core == which, packed[f], 0.0)
         if x == 0:
             state = add_state(state, load_state(jumps))
 

time: 96.7 us -> 96.6 us (level)
  waiting for transfers between devices: 5.38 us -> 8.43 us
  starting transfers between devices: 40.6 us -> 38.3 us
  blocking collectives: 31.5 us -> 29.9 us
  Pallas kernels: 15.9 us -> 17.3 us
    ppermute x1, waiting for transfers between devices: 2.17 us -> 5.23 us  [body(): other_half = lax.ppermute(half, ('zh',), [(i, i ^ 1) for i in range(4)])]
    ppermute x1, starting transfers between devices: 4.58 us -> 2.61 us  [body(): mate = lax.ppermute(total, ('c',), [(0, 1), (1, 0)])]
    all_to_all x2, blocking collectives: 31.5 us -> 29.9 us  [swap(): return lax.all_to_all(block, axes, 0, 0, tiled=True)]
    ppermute x3, starting transfers between devices: 5.72 us -> 4.26 us  [body(): lax.ppermute(both, ('zl',), [(i, i + d) for i in range(4 - d)])]
    pallas_call x10, Pallas kernels: 15.9 us -> 17.3 us  [run(): pl.pallas_call(kernel, out_shape=[jax.ShapeDtypeStruct(s, F32) for s in o...]
  transfers between devices with their start and end apart: 10 -> 10, of which waited for: 4 -> 4; matrix products, arithmetic and copies ran while one was open for 0% -> 0% of each run, Pallas kernels for 9% -> 11%
where the time goes in v7:
time: 96.6 us; the launch traced here: 96.5 us
  starting transfers between devices  38.3 us (40%)
  blocking collectives  29.9 us (31%)
  Pallas kernels  17.3 us (18%)
  waiting for transfers between devices  8.43 us (9%)
  local copies, waits for them, and re-layouts  1.65 us (2%)
    all_to_all x2, blocking collectives, swap(): return lax.all_to_all(block, axes, 0, 0, tiled=True)  29.9 us
    pallas_call x10, Pallas kernels, run(): pl.pallas_call(kernel, out_shape=[jax.ShapeDtypeStruct(s, F32) for s in o...  17.3 us
    ppermute x1, starting transfers between devices, body(): other_half = lax.ppermute(half, ('zh',), [(i, i ^ 1) for i in range(4)])  10.4 us
    ppermute x1, starting transfers between devices, body(): beside = lax.ppermute(mine, ('zh',), [(i, i ^ 3) for i in range(4)])  8.4 us
    ppermute x2, starting transfers between devices, body(): mate = [lax.ppermute(part, SPACE, inside) for part in (first, rest)]  6.8 us
    ppermute x1, waiting for transfers between devices, body(): other_half = lax.ppermute(half, ('zh',), [(i, i ^ 1) for i in range(4)])  5.23 us
    ppermute x1, starting transfers between devices, body(): other = lax.ppermute(sent, SPACE, across)  4.59 us
    ppermute x3, starting transfers between devices, body(): lax.ppermute(both, ('zl',), [(i, i + d) for i in range(4 - d)])  4.26 us
  transfers between devices with their start and end apart: 10, of which 4 were waited for; matrix products, arithmetic and copies ran while one was open for 0% of the time, Pallas kernels for 11%

profile of v7, /device:TPU:1, one launch (start us, length us, event | category | flops | bytes accessed | tf_op | source)
XLA Modules:
  0.0 96.5 jit_solution(7808400292958474663)
XLA Ops:
  0.0 0.7 convert_element_type.3.mask
  0.7 1.0 %copy-done = f32[1,3,16,16,128]{4,3,2,1,0:T(8,128)S(1)} copy-done((f32[1,3,16,16,128]{4,3,2,1,0:T(8,128)S(1)}, f32[1,3,16,16,128]{4,3,2,1,0:T(8,128)}, u32[]{:S(2)}) %copy-start) | copy-done | bytes 393240
  2.3 4.6 %collective-permute-start = (f32[752,128]{1,0:T(8,128)S(1)}, f32[752,128]{1,0:T(8,128)S(1)}, u32[]{:S(2)}, u32[]{:S(2)}) collective-permute-start(f32[752,128]{1,0:T(8,128)S(1)} %get-tuple-element.22), channel_id=1, source_target_pairs={{1,2},{3,4},{5,6},{7,8},{9,10},{11,12},{13,14},{15,16},{17,18},{19... | collective-permute-start | bytes 1155080 | tf_op jit(solution)/shard_map/ppermute | solution.py:539
  6.9 4.9 %collective-permute-start.1 = (f32[512,128]{1,0:T(8,128)S(1)}, f32[512,128]{1,0:T(8,128)S(1)}, u32[]{:S(2)}, u32[]{:S(2)}) collective-permute-start(f32[512,128]{1,0:T(8,128)S(1)} %get-tuple-element.20.own_first), channel_id=1, source_target_pairs={{0,1},{1,0},{2,3},{3,2},{4,5},{5,4},{6,7},{7,6},{8,9},{9,8},{10,11... | collective-permute-start | bytes 786440 | tf_op jit(solution)/shard_map/ppermute | solution.py:545
  11.8 1.9 %collective-permute-start.2 = (f32[272,128]{1,0:T(8,128)S(1)}, f32[272,128]{1,0:T(8,128)S(1)}, u32[]{:S(2)}, u32[]{:S(2)}) collective-permute-start(f32[272,128]{1,0:T(8,128)S(1)} %get-tuple-element.21.own_rest), channel_id=1, source_target_pairs={{0,1},{1,0},{2,3},{3,2},{4,5},{5,4},{6,7},{7,6},{8,9},{9,8},{10,11... | collective-permute-start | bytes 417800 | tf_op jit(solution)/shard_map/ppermute | solution.py:545
  13.7 1.3 %collective-permute-start.3 = (f32[48,128]{1,0:T(8,128)S(1)}, f32[48,128]{1,0:T(8,128)S(1)}, u32[]{:S(2)}, u32[]{:S(2)}) collective-permute-start(f32[48,128]{1,0:T(8,128)S(1)} %get-tuple-element.28), channel_id=1, source_target_pairs={{32,0},{64,32},{96,64},{128,96},{160,128},{192,160},{224,192},{256... | collective-permute-start | bytes 73736 | tf_op jit(solution)/shard_map/ppermute | solution.py:540
  15.1 7.7 %shard_map.57 = (f32[16,128]{1,0:T(8,128)S(1)}, f32[16,128]{1,0:T(8,128)S(1)}) custom-call(f32[16,16]{1,0:T(8,128)S(1)} %copy-done.1, f32[1,16]{1,0:T(1,128)S(1)} %bitcast.18), custom_call_target="tpu_custom_call" | custom-call | flops 10485760 | bytes 1048576 | tf_op jit(solution)/shard_map/pallas_call | solution.py:511
  23.5 2.6 %shard_map.56 = (f32[20,2,8,128]{3,2,1,0:T(8,128)S(1)}, f32[20,2,8,128]{3,2,1,0:T(8,128)S(1)}, f32[20,2,8,128]{3,2,1,0:T(8,128)S(1)}, f32[1,128]{1,0:T(1,128)S(1)}) custom-call(f32[512,128]{1,0:T(8,128)S(1)} %get-tuple-element.20.own_first, f32[272,128]{1,0:T(8,128)S(1)} %get-tuple-element.21.own_rest, f32[512,128]{1,0:T(8,128)S(1)} %collective-permute-done.1.mate_first, ...), custom_call_target="tpu_custom_call" | custom-call | flops 4194304 | bytes 1048576 | tf_op jit(solution)/shard_map/pallas_call | solution.py:511
  26.1 2.8 %shard_map.58 = (f32[48,16,128]{2,1,0:T(8,128)S(1)}, f32[128,128]{1,0:T(8,128)S(1)}) custom-call(f32[512,128]{1,0:T(8,128)S(1)} %get-tuple-element.20.own_first, f32[272,128]{1,0:T(8,128)S(1)} %get-tuple-element.21.own_rest, f32[752,128]{1,0:T(8,128)S(1)} %collective-permute-done.other, f32[20,2,8,128]{3,2,1,0:T(8,128)S(1)} %get-tuple-element.23.h_in, ...), custom_call_target="tpu_custom_call" | custom-call | flops 1048576 | bytes 1048576 | tf_op jit(solution)/shard_map/pallas_call | solution.py:511
  28.9 18.6 %all_to_all.22 = f32[32,4,128]{2,1,0:T(4,128)S(1)} all-to-all(f32[32,4,128]{2,1,0:T(4,128)S(1)} %bitcast.12), channel_id=1, replica_groups=mesh['zl'=4,'x'=4,'zh'=4,'y'=4,'c'=2] {'x','y','c'}, dimensions={0} | all-to-all | bytes 131072 | tf_op jit(solution)/shard_map/all_to_all | solution.py:525
  47.5 8.4 %collective-permute-start.4 = (f32[56,128]{1,0:T(8,128)S(1)}, f32[56,128]{1,0:T(8,128)S(1)}, u32[]{:S(2)}, u32[]{:S(2)}) collective-permute-start(f32[56,128]{1,0:T(8,128)S(1)} %shard_map.59), channel_id=1, source_target_pairs={{0,24},{8,16},{16,8},{24,0},{1,25},{9,17},{17,9},{25,1},{2,26},{10... | collective-permute-start | bytes 86024 | tf_op jit(solution)/shard_map/ppermute | solution.py:561
  56.0 1.3 %collective-permute-done.4 = f32[56,128]{1,0:T(8,128)S(1)} collective-permute-done((f32[56,128]{1,0:T(8,128)S(1)}, f32[56,128]{1,0:T(8,128)S(1)}, u32[]{:S(2)}, u32[]{:S(2)}) %collective-permute-start.4) | collective-permute-done | bytes 28704 | tf_op jit(solution)/shard_map/ppermute | solution.py:561
  57.2 10.4 %collective-permute-start.5 = (f32[112,128]{1,0:T(8,128)S(1)}, f32[112,128]{1,0:T(8,128)S(1)}, u32[]{:S(2)}, u32[]{:S(2)}) collective-permute-start(f32[112,128]{1,0:T(8,128)S(1)} %pad_maximum_fusion.half), channel_id=1, source_target_pairs={{0,8},{8,0},{16,24},{24,16},{1,9},{9,1},{17,25},{25,17},{2,10},{10... | collective-permute-start | bytes 172040 | tf_op jit(solution)/shard_map/ppermute | solution.py:563
  67.6 5.2 %collective-permute-done.5.other_half = f32[112,128]{1,0:T(8,128)S(1)} collective-permute-done((f32[112,128]{1,0:T(8,128)S(1)}, f32[112,128]{1,0:T(8,128)S(1)}, u32[]{:S(2)}, u32[]{:S(2)}) %collective-permute-start.5) | collective-permute-done | bytes 57376 | tf_op jit(solution)/shard_map/ppermute | solution.py:563
  73.2 2.6 %collective-permute-start.6 = (f32[96,128]{1,0:T(8,128)S(1)}, f32[96,128]{1,0:T(8,128)S(1)}, u32[]{:S(2)}, u32[]{:S(2)}) collective-permute-start(f32[96,128]{1,0:T(8,128)S(1)} %get-tuple-element.32.total), channel_id=1, source_target_pairs={{0,1},{1,0},{2,3},{3,2},{4,5},{5,4},{6,7},{7,6},{8,9},{9,8},{10,11... | collective-permute-start | bytes 147464 | tf_op jit(solution)/shard_map/ppermute | solution.py:567
  75.8 0.9 collective-permute-done.6.mate
  76.7 0.7 shard_map.61
  77.4 1.3 %collective-permute-start.9 = (f32[96,128]{1,0:T(8,128)S(1)}, f32[96,128]{1,0:T(8,128)S(1)}, u32[]{:S(2)}, u32[]{:S(2)}) collective-permute-start(f32[96,128]{1,0:T(8,128)S(1)} %shard_map.61), channel_id=1, source_target_pairs={{0,384},{1,385},{2,386},{3,387},{4,388},{5,389},{6,390},{7,391},{8... | collective-permute-start | bytes 147464 | tf_op jit(solution)/shard_map/ppermute | solution.py:570
  78.7 1.3 %collective-permute-start.8 = (f32[96,128]{1,0:T(8,128)S(1)}, f32[96,128]{1,0:T(8,128)S(1)}, u32[]{:S(2)}, u32[]{:S(2)}) collective-permute-start(f32[96,128]{1,0:T(8,128)S(1)} %shard_map.61), channel_id=1, source_target_pairs={{0,256},{128,384},{1,257},{129,385},{2,258},{130,386},{3,259},{131... | collective-permute-start | bytes 147464 | tf_op jit(solution)/shard_map/ppermute | solution.py:570
  80.0 1.7 %collective-permute-start.7 = (f32[96,128]{1,0:T(8,128)S(1)}, f32[96,128]{1,0:T(8,128)S(1)}, u32[]{:S(2)}, u32[]{:S(2)}) collective-permute-start(f32[96,128]{1,0:T(8,128)S(1)} %shard_map.61), channel_id=1, source_target_pairs={{0,128},{128,256},{256,384},{1,129},{129,257},{257,385},{2,130},{1... | collective-permute-start | bytes 147464 | tf_op jit(solution)/shard_map/ppermute | solution.py:570
  81.7 1.1 %collective-permute-done.7.one = f32[96,128]{1,0:T(8,128)S(1)} collective-permute-done((f32[96,128]{1,0:T(8,128)S(1)}, f32[96,128]{1,0:T(8,128)S(1)}, u32[]{:S(2)}, u32[]{:S(2)}) %collective-permute-start.7) | collective-permute-done | bytes 49184 | tf_op jit(solution)/shard_map/ppermute | solution.py:570
  82.8 1.4 %shard_map.63 = f32[128,128]{1,0:T(8,128)S(1)} custom-call(f32[96,128]{1,0:T(8,128)S(1)} %collective-permute-done.7.one, f32[96,128]{1,0:T(8,128)S(1)} %collective-permute-done.8.two, f32[96,128]{1,0:T(8,128)S(1)} %shard_map.62.earlier, f32[96,128]{1,0:T(8,128)S(1)} %collective-permute-done.6.mate, f32[192,128]{1,0:T(8,128)S(1)} %get-tuple-element.34.jumps, ...), custom_call_target="tpu_custom_call" | custom-call | flops 1048576 | bytes 1048576 | tf_op jit(solution)/shard_map/pallas_call | solution.py:511
  84.2 11.2 %all_to_all.23 = f32[32,4,128]{2,1,0:T(4,128)S(1)} all-to-all(f32[32,4,128]{2,1,0:T(4,128)S(1)} %bitcast.11), channel_id=1, replica_groups=mesh['zl'=4,'x'=4,'zh'=4,'y'=4,'c'=2] {'x','y','c'}, dimensions={0} | all-to-all | bytes 131072 | tf_op jit(solution)/shard_map/all_to_all | solution.py:525
  95.4 1.0 %shard_map.64 = f32[768,128]{1,0:T(8,128)} custom-call(f32[48,16,128]{2,1,0:T(8,128)S(1)} %get-tuple-element.29.fine, f32[128,128]{1,0:T(8,128)S(1)} %bitcast.9, f32[16,128]{1,0:T(8,128)S(1)} %get-tuple-element.27.vectors, f32[1,16]{1,0:T(1,128)S(1)} %bitcast.21), custom_call_target="tpu_custom_call" | custom-call | flops 1048576 | bytes 1048576 | tf_op jit(solution)/shard_map/pallas_call | solution.py:511
  (18 shorter events, 1.7 us)
Async XLA Ops:
  0.7 1.0 %copy-start = (f32[1,3,16,16,128]{4,3,2,1,0:T(8,128)S(1)}, f32[1,3,16,16,128]{4,3,2,1,0:T(8,128)}, u32[]{:S(2)}) copy-start(f32[1,3,16,16,128]{4,3,2,1,0:T(8,128)} %param.5) | copy-start | bytes 1179652
  2.3 12.7 %copy-start.1 = (f32[16,16]{1,0:T(8,128)S(1)}, f32[16,16]{1,0:T(8,128)}, u32[]{:S(2)}) copy-start(f32[16,16]{1,0:T(8,128)} %coupling.5) | copy-start | bytes 3076
  2.3 23.8 %collective-permute-start = (f32[752,128]{1,0:T(8,128)S(1)}, f32[752,128]{1,0:T(8,128)S(1)}, u32[]{:S(2)}, u32[]{:S(2)}) collective-permute-start(f32[752,128]{1,0:T(8,128)S(1)} %get-tuple-element.22), channel_id=1, source_target_pairs={{1,2},{3,4},{5,6},{7,8},{9,10},{11,12},{13,14},{15,16},{17,18},{19... | collective-permute-start | bytes 1155080 | tf_op jit(solution)/shard_map/ppermute | solution.py:539
  6.9 15.9 %collective-permute-start.1 = (f32[512,128]{1,0:T(8,128)S(1)}, f32[512,128]{1,0:T(8,128)S(1)}, u32[]{:S(2)}, u32[]{:S(2)}) collective-permute-start(f32[512,128]{1,0:T(8,128)S(1)} %get-tuple-element.20.own_first), channel_id=1, source_target_pairs={{0,1},{1,0},{2,3},{3,2},{4,5},{5,4},{6,7},{7,6},{8,9},{9,8},{10,11... | collective-permute-start | bytes 786440 | tf_op jit(solution)/shard_map/ppermute | solution.py:545
  11.8 11.0 %collective-permute-start.2 = (f32[272,128]{1,0:T(8,128)S(1)}, f32[272,128]{1,0:T(8,128)S(1)}, u32[]{:S(2)}, u32[]{:S(2)}) collective-permute-start(f32[272,128]{1,0:T(8,128)S(1)} %get-tuple-element.21.own_rest), channel_id=1, source_target_pairs={{0,1},{1,0},{2,3},{3,2},{4,5},{5,4},{6,7},{7,6},{8,9},{9,8},{10,11... | collective-permute-start | bytes 417800 | tf_op jit(solution)/shard_map/ppermute | solution.py:545
  13.7 1.3 %copy-start.3 = (f32[16]{0:T(128)S(1)}, f32[16]{0:T(128)}, u32[]{:S(2)}) copy-start(f32[16]{0:T(128)} %param.9) | copy-start | bytes 196
  13.7 12.3 %collective-permute-start.3 = (f32[48,128]{1,0:T(8,128)S(1)}, f32[48,128]{1,0:T(8,128)S(1)}, u32[]{:S(2)}, u32[]{:S(2)}) collective-permute-start(f32[48,128]{1,0:T(8,128)S(1)} %get-tuple-element.28), channel_id=1, source_target_pairs={{32,0},{64,32},{96,64},{128,96},{160,128},{192,160},{224,192},{256... | collective-permute-start | bytes 73736 | tf_op jit(solution)/shard_map/ppermute | solution.py:540
  22.8 0.7 copy-start.2
  47.5 9.7 %collective-permute-start.4 = (f32[56,128]{1,0:T(8,128)S(1)}, f32[56,128]{1,0:T(8,128)S(1)}, u32[]{:S(2)}, u32[]{:S(2)}) collective-permute-start(f32[56,128]{1,0:T(8,128)S(1)} %shard_map.59), channel_id=1, source_target_pairs={{0,24},{8,16},{16,8},{24,0},{1,25},{9,17},{17,9},{25,1},{2,26},{10... | collective-permute-start | bytes 86024 | tf_op jit(solution)/shard_map/ppermute | solution.py:561
  57.2 15.6 %collective-permute-start.5 = (f32[112,128]{1,0:T(8,128)S(1)}, f32[112,128]{1,0:T(8,128)S(1)}, u32[]{:S(2)}, u32[]{:S(2)}) collective-permute-start(f32[112,128]{1,0:T(8,128)S(1)} %pad_maximum_fusion.half), channel_id=1, source_target_pairs={{0,8},{8,0},{16,24},{24,16},{1,9},{9,1},{17,25},{25,17},{2,10},{10... | collective-permute-start | bytes 172040 | tf_op jit(solution)/shard_map/ppermute | solution.py:563
  73.2 3.5 %collective-permute-start.6 = (f32[96,128]{1,0:T(8,128)S(1)}, f32[96,128]{1,0:T(8,128)S(1)}, u32[]{:S(2)}, u32[]{:S(2)}) collective-permute-start(f32[96,128]{1,0:T(8,128)S(1)} %get-tuple-element.32.total), channel_id=1, source_target_pairs={{0,1},{1,0},{2,3},{3,2},{4,5},{5,4},{6,7},{7,6},{8,9},{9,8},{10,11... | collective-permute-start | bytes 147464 | tf_op jit(solution)/shard_map/ppermute | solution.py:567
  77.4 4.3 %collective-permute-start.9 = (f32[96,128]{1,0:T(8,128)S(1)}, f32[96,128]{1,0:T(8,128)S(1)}, u32[]{:S(2)}, u32[]{:S(2)}) collective-permute-start(f32[96,128]{1,0:T(8,128)S(1)} %shard_map.61), channel_id=1, source_target_pairs={{0,384},{1,385},{2,386},{3,387},{4,388},{5,389},{6,390},{7,391},{8... | collective-permute-start | bytes 147464 | tf_op jit(solution)/shard_map/ppermute | solution.py:570
  78.7 3.1 %collective-permute-start.8 = (f32[96,128]{1,0:T(8,128)S(1)}, f32[96,128]{1,0:T(8,128)S(1)}, u32[]{:S(2)}, u32[]{:S(2)}) collective-permute-start(f32[96,128]{1,0:T(8,128)S(1)} %shard_map.61), channel_id=1, source_target_pairs={{0,256},{128,384},{1,257},{129,385},{2,258},{130,386},{3,259},{131... | collective-permute-start | bytes 147464 | tf_op jit(solution)/shard_map/ppermute | solution.py:570
  80.0 2.8 %collective-permute-start.7 = (f32[96,128]{1,0:T(8,128)S(1)}, f32[96,128]{1,0:T(8,128)S(1)}, u32[]{:S(2)}, u32[]{:S(2)}) collective-permute-start(f32[96,128]{1,0:T(8,128)S(1)} %shard_map.61), channel_id=1, source_target_pairs={{0,128},{128,256},{256,384},{1,129},{129,257},{257,385},{2,130},{1... | collective-permute-start | bytes 147464 | tf_op jit(solution)/shard_map/ppermute | solution.py:570
